TPU v7x, 32 devices: a whole 2x2x4 slice. The times are simulated.
32 devices in a mesh: cfg: 2 (over core), seq: 4 (over y, x), tp: 4 (over z).
Axes of the slice: x: 2, y: 2, z: 4, core: 2. Of those that a mesh axis runs over, the one named last changes fastest.
Arguments:
- stream: bfloat16 [2, 160, 3072], P('cfg', 'seq', 'tp'), may hold values from -6 to 6
- queries: bfloat16 [2, 160, 1536], P('cfg', 'seq', 'tp'), may hold values from -6 to 6
- keys: bfloat16 [2, 160, 1536], P('cfg', 'seq', 'tp'), may hold values from -6 to 6
- values: bfloat16 [2, 160, 1536], P('cfg', 'seq', 'tp'), may hold values from -6 to 6
- text_keys: bfloat16 [2, 226, 1536], P('cfg', None, 'tp'), may hold values from -6 to 6
- text_values: bfloat16 [2, 226, 1536], P('cfg', None, 'tp'), may hold values from -6 to 6
- out_weight: bfloat16 [1536, 3072], P('tp'), may hold values from -0.15625 to 0.15625
- gate: float32 [3072], P('tp'), may hold values from -4 to 4
- shift: float32 [3072], P('tp'), may hold values from -3 to 3
- scale: float32 [3072], P('tp'), may hold values from -3 to 3
- proj_weight: float32 [3072, 64], P('tp'), may hold values from -0.109375 to 0.109375
- q_gain: float32 [64], replicated, may hold values from 1.4 to 6
- k_gain: float32 [64], replicated, may hold values from 1.4 to 6
- lengths: int32 [4], replicated, may hold values from 1 to 40, 144 in all
- latents: float32 [160, 64], P('seq', ('cfg', 'tp')), may hold values from -6 to 6
- alphas: float32 [1000], replicated, may hold values from 0.05 to 0.95
- step_index: int32 [1], replicated, may hold values from 20 to 999
Outputs:
- hidden_out: bfloat16 [2, 160, 3072], P('cfg', 'seq', 'tp')
- latents_out: float32 [160, 64], P('seq', ('cfg', 'tp'))
Inputs may be any that keep to these rules, and one draw needn't show every extreme that they name: `lengths`: video tokens held by each index of seq, in token order; they sum to 144 and the largest is exactly 40. The previous step's entry is step_index - 20.
All inputs are finite; a program needn't handle non-finite values.
Results may differ from a plain program's by a relative error of at most 0.012.
The roundings to bfloat16 on the way count: a program that leaves them out, or rounds other values in their place, can miss the bound.
Values may be sent and summed in bfloat16 or wider, within the bound.
No kernel may reach another device: no remote copies, remote signals or barrier semaphores. Data moves between devices by JAX's collectives and lax.ppermute only.
A program may use at most 64 MiB of HBM per device.

v0:
```python
import jax
import jax.numpy as jnp
from jax import lax
from jax.sharding import PartitionSpec as P

D = 3072
HEAD = 64
HP = 30
WP = 45
STRIDE = 20


guide_scale = 6.0
head_eps = 1e-06
final_eps = 1e-05


def partner_2(shard, axis, distance):
    return lax.ppermute(shard, axis, [(i, i ^ 1 << distance) for i in range(lax.axis_size(axis))])


def rope_tables(position):
    frame = position // (HP * WP)
    height = position // WP % HP
    across = position % WP

    def angles(coord, extent):
        freq = 1.0 / 10000.0 ** (jnp.arange(0, extent, 2, dtype=jnp.float32) / extent)
        return coord.astype(jnp.float32)[:, None] * freq[None, :]

    angle = jnp.concatenate([angles(frame, 16), angles(height, 24), angles(across, 24)], axis=1)
    return (jnp.cos(angle), jnp.sin(angle))


def head_norm(field, gain):
    centre = field - jnp.mean(field, axis=-1, keepdims=True)
    spread = jnp.mean(centre * centre, axis=-1, keepdims=True)
    return centre * lax.rsqrt(spread + head_eps) * gain


def rotate_pairs(field, cos_table, sin_table):
    pairs = field.reshape(field.shape[:-1] + (HEAD // 2, 2))
    first = pairs[..., 0]
    second = pairs[..., 1]
    cos_part = cos_table[:, None, :]
    sin_part = sin_table[:, None, :]
    turned = jnp.stack(
        [first * cos_part - second * sin_part, second * cos_part + first * sin_part], axis=-1
    )
    return turned.reshape(field.shape)


def prepare(field, gain, tables):
    count = field.shape[0]
    normed = head_norm(field.astype(jnp.float32).reshape(count, -1, HEAD), gain)
    if tables is not None:
        normed = rotate_pairs(normed, tables[0], tables[1])
    return normed.reshape(count, -1).astype(jnp.bfloat16)


def last_dims(left, right):
    return lax.dot_general(
        left, right, (((1,), (1,)), ((), ())), preferred_element_type=jnp.float32
    )


def shards(
    stream,
    queries,
    keys,
    values,
    text_keys,
    text_values,
    out_weight,
    gate,
    shift,
    scale,
    proj_weight,
    q_gain,
    k_gain,
    lengths,
    latents,
    alphas,
    step_index,
):
    blocks = lax.axis_size("seq")
    group = lax.axis_size("tp")
    rows = queries.shape[1]
    width = queries.shape[2]
    heads_here = width // HEAD
    seq_rank = lax.axis_index("seq")
    order = jnp.arange(blocks, dtype=jnp.int32)
    own_start = jnp.sum(jnp.where(order < seq_rank, lengths, 0))
    own_count = jnp.sum(jnp.where(order == seq_rank, lengths, 0))
    within = jnp.arange(rows, dtype=jnp.int32)
    own_live = within < own_count
    own_tables = rope_tables(own_start + within)
    query_hat = prepare(queries[0], q_gain, own_tables)
    outgoing = keys[0]
    arrived_keys, arrived_values = (
        lax.all_gather(outgoing, "seq", axis=0, tiled=True),
        lax.all_gather(values[0], "seq", axis=0, tiled=True),
    )
    offsets = jnp.cumsum(lengths) - lengths
    all_positions = (offsets[:, None] + within[None, :]).reshape(-1)
    video_keys = prepare(arrived_keys, k_gain, rope_tables(all_positions))
    video_live = (within[None, :] < lengths[:, None]).reshape(-1)
    text_hat = prepare(text_keys[0], k_gain, None)
    text_vals = text_values[0]

    def one_head(head):
        start = head * HEAD
        query_part = lax.dynamic_slice_in_dim(query_hat, start, HEAD, 1)
        video_key_part = lax.dynamic_slice_in_dim(video_keys, start, HEAD, 1)
        video_value_part = lax.dynamic_slice_in_dim(arrived_values, start, HEAD, 1)
        text_key_part = lax.dynamic_slice_in_dim(text_hat, start, HEAD, 1)
        text_value_part = lax.dynamic_slice_in_dim(text_vals, start, HEAD, 1)
        video_scores = last_dims(query_part, video_key_part) * 0.125
        video_scores = jnp.where(video_live[None, :], video_scores, -jnp.inf)
        text_scores = last_dims(query_part, text_key_part) * 0.125
        row_max = jnp.maximum(
            jnp.max(video_scores, axis=1, keepdims=True),
            jnp.max(text_scores, axis=1, keepdims=True),
        )
        video_weights = jnp.exp(video_scores - row_max)
        text_weights = jnp.exp(text_scores - row_max)
        totals = jnp.sum(video_weights, axis=1, keepdims=True) + jnp.sum(
            text_weights, axis=1, keepdims=True
        )
        mixed = jnp.dot(
            video_weights.astype(jnp.bfloat16), video_value_part, preferred_element_type=jnp.float32
        )
        mixed = mixed + jnp.dot(
            text_weights.astype(jnp.bfloat16), text_value_part, preferred_element_type=jnp.float32
        )
        return (mixed / totals).astype(jnp.bfloat16)

    attended = lax.map(one_head, jnp.arange(heads_here, dtype=jnp.int32))
    attended = jnp.transpose(attended, (1, 0, 2)).reshape(rows, width)
    projected = jnp.dot(attended, out_weight, preferred_element_type=jnp.float32)
    summed = lax.psum_scatter(
        projected.astype(jnp.bfloat16), "tp", scatter_dimension=1, tiled=True
    ).astype(jnp.float32)
    hidden = stream[0].astype(jnp.float32) + gate * summed
    hidden = jnp.where(own_live[:, None], hidden, 0.0).astype(jnp.bfloat16)
    widened = lax.optimization_barrier(hidden).astype(jnp.float32)
    row_total, row_square = lax.psum(
        (jnp.sum(widened, axis=1), jnp.sum(widened * widened, axis=1)), "tp"
    )
    mean = row_total[:, None] / D
    square = row_square[:, None] / D
    normed = (widened - mean) * lax.rsqrt(square - mean * mean + final_eps) * (1.0 + scale) + shift
    partial_pred = jnp.dot(
        normed, proj_weight, precision=lax.Precision.HIGHEST, preferred_element_type=jnp.float32
    )
    cfg_rank = lax.axis_index("cfg")
    tp_rank = lax.axis_index("tp")
    piece = proj_weight.shape[1] // (2 * group)
    prediction = lax.psum(partial_pred, "tp")
    partner = partner_2(prediction, "cfg", 0)
    column = (cfg_rank * group + tp_rank) * piece
    mine = lax.dynamic_slice_in_dim(prediction, column, piece, 1)
    theirs = lax.dynamic_slice_in_dim(partner, column, piece, 1)
    is_conditioned = cfg_rank == 0
    conditioned = jnp.where(is_conditioned, mine, theirs)
    unconditioned = jnp.where(is_conditioned, theirs, mine)
    guided = unconditioned + guide_scale * (conditioned - unconditioned)
    current = alphas[step_index[0]]
    earlier = alphas[step_index[0] - STRIDE]
    root_now = jnp.sqrt(current)
    rest_now = jnp.sqrt(1.0 - current)
    clean = root_now * latents - rest_now * guided
    noise = root_now * guided + rest_now * latents
    stepped = jnp.sqrt(earlier) * clean + jnp.sqrt(1.0 - earlier) * noise
    latents_out = jnp.where(own_live[:, None], stepped, 0.0)
    return (hidden[None], latents_out)


def solution(mesh):
    return jax.shard_map(
        shards,
        mesh=mesh,
        in_specs=(
            P("cfg", "seq", "tp"),
            P("cfg", "seq", "tp"),
            P("cfg", "seq", "tp"),
            P("cfg", "seq", "tp"),
            P("cfg", None, "tp"),
            P("cfg", None, "tp"),
            P("tp", None),
            P("tp"),
            P("tp"),
            P("tp"),
            P("tp", None),
            P(),
            P(),
            P(),
            P("seq", ("cfg", "tp")),
            P(),
            P(),
        ),
        out_specs=(P("cfg", "seq", "tp"), P("seq", ("cfg", "tp"))),
        check_vma=False,
    )
```

profile of v0, /device:TPU:0, one launch (start us, length us, event | category | flops | bytes accessed | tf_op | source)
XLA Modules:
  0.0 139.7 jit_solution(6189248102323585336)
XLA Ops:
  7.2 1.0 reduce-window.9
  8.2 1.4 fusion.51
  9.7 0.6 remainder_compare_fusion
  10.3 0.6 negate_power_fusion
  10.9 0.6 negate_power_fusion.1
  11.5 10.1 %all-gather = bf16[1,160,384]{2,1,0:T(8,128)(2,1)S(1)} all-gather(bf16[1,40,384]{2,1,0:T(8,128)(2,1)} %param.21), channel_id=2, replica_groups=mesh['cfg'=2,'seq'=4,'tp'=4] {'seq'}, dimensions={1}, use_global_device_ids=true | all-gather | bytes 153600 | tf_op jit(solution)/shard_map/all_gather | solution.py:101
  22.0 1.2 fusion.53
  23.2 1.2 fusion.57
  24.3 0.8 reshape.432
  25.2 0.9 copy.47
  26.3 1.3 ne.142
  27.6 1.2 ne.145
  29.0 0.8 mul.360
  29.7 0.7 fusion.50
  30.5 0.7 broadcast_multiply_fusion.3
  31.2 0.8 broadcast_multiply_fusion.1
  32.3 0.5 subtract_convert_fusion
  32.9 0.5 pad_maximum_fusion
  33.6 0.7 broadcast_multiply_fusion.7
  34.9 0.8 mul.340
  35.7 0.8 broadcast_multiply_fusion.6
  37.3 1.1 copy.52
  38.6 8.2 %all-gather.1 = bf16[1,160,384]{2,1,0:T(8,128)(2,1)S(1)} all-gather(bf16[1,40,384]{2,1,0:T(8,128)(2,1)S(1)} %copy-done.4), channel_id=3, replica_groups=mesh['cfg'=2,'seq'=4,'tp'=4] {'seq'}, dimensions={1}, use_global_device_ids=true | all-gather | bytes 153600 | tf_op jit(solution)/shard_map/all_gather | solution.py:102
  47.0 30.5 %while.11 = (s32[]{:T(128)}, bf16[6,40,64]{2,1,0:T(8,128)(2,1)}, s32[6]{0:T(128)S(1)}, bf16[40,384]{1,0:T(8,128)(2,1)S(1)}, bf16[160,384]{0,1:T(8,128)(2,1)S(1)}...) while((s32[]{:T(128)}, bf16[6,40,64]{2,1,0:T(8,128)(2,1)}, ...), condition=%wide.region_14.15_spmd.clone, body=%wide.region_9.14_spmd.clone.sunk | while | flops 4059446 | bytes 424239 | solution.py:138
  47.0 0.7 dynamic_slice.78
  48.4 0.7 iota_compare_fusion.3
  49.2 0.3 fusion.78
  49.5 0.3 fusion.79
  50.4 1.7 %fusion.83 = bf16[6,40,64]{2,1,0:T(8,128)(2,1)} fusion(bf16[6,40,64]{2,1,0:T(8,128)(2,1)} %get-tuple-element.236, s32[]{:T(128)} %get-tuple-element.235, f32[40,64]{1,0:T(8,128)S(1)} %fusion.80, bf16[226,384]{1,0:T(8,128)(2,1)} %get-tuple-element.255, s32[]{:T(128)S(6)} %select_n.180, f32[40,226]{1,0:T(8,128)S(1)} %get-tuple-element.221, ...), kind=kOutput, calls=%fused_computation.8.clone.1 | convolution fusion | flops 1182880 | bytes 116868 | tf_op jit(solution)/shard_map/while/body/eval_jaxpr/dot_general | solution.py:133
  52.1 0.7 dynamic_slice.78
  53.5 0.7 iota_compare_fusion.3
  54.3 0.3 fusion.78
  54.6 0.3 fusion.79
  55.5 1.7 %fusion.83 = bf16[6,40,64]{2,1,0:T(8,128)(2,1)} fusion(bf16[6,40,64]{2,1,0:T(8,128)(2,1)} %get-tuple-element.236, s32[]{:T(128)} %get-tuple-element.235, f32[40,64]{1,0:T(8,128)S(1)} %fusion.80, bf16[226,384]{1,0:T(8,128)(2,1)} %get-tuple-element.255, s32[]{:T(128)S(6)} %select_n.180, f32[40,226]{1,0:T(8,128)S(1)} %get-tuple-element.221, ...), kind=kOutput, calls=%fused_computation.8.clone.1 | convolution fusion | flops 1182880 | bytes 116868 | tf_op jit(solution)/shard_map/while/body/eval_jaxpr/dot_general | solution.py:133
  57.2 0.7 dynamic_slice.78
  58.5 0.7 iota_compare_fusion.3
  59.4 0.3 fusion.78
  59.7 0.3 fusion.79
  60.6 1.7 %fusion.83 = bf16[6,40,64]{2,1,0:T(8,128)(2,1)} fusion(bf16[6,40,64]{2,1,0:T(8,128)(2,1)} %get-tuple-element.236, s32[]{:T(128)} %get-tuple-element.235, f32[40,64]{1,0:T(8,128)S(1)} %fusion.80, bf16[226,384]{1,0:T(8,128)(2,1)} %get-tuple-element.255, s32[]{:T(128)S(6)} %select_n.180, f32[40,226]{1,0:T(8,128)S(1)} %get-tuple-element.221, ...), kind=kOutput, calls=%fused_computation.8.clone.1 | convolution fusion | flops 1182880 | bytes 116868 | tf_op jit(solution)/shard_map/while/body/eval_jaxpr/dot_general | solution.py:133
  62.3 0.7 dynamic_slice.78
  63.6 0.7 iota_compare_fusion.3
  64.4 0.3 fusion.78
  64.7 0.3 fusion.79
  65.7 1.7 %fusion.83 = bf16[6,40,64]{2,1,0:T(8,128)(2,1)} fusion(bf16[6,40,64]{2,1,0:T(8,128)(2,1)} %get-tuple-element.236, s32[]{:T(128)} %get-tuple-element.235, f32[40,64]{1,0:T(8,128)S(1)} %fusion.80, bf16[226,384]{1,0:T(8,128)(2,1)} %get-tuple-element.255, s32[]{:T(128)S(6)} %select_n.180, f32[40,226]{1,0:T(8,128)S(1)} %get-tuple-element.221, ...), kind=kOutput, calls=%fused_computation.8.clone.1 | convolution fusion | flops 1182880 | bytes 116868 | tf_op jit(solution)/shard_map/while/body/eval_jaxpr/dot_general | solution.py:133
  67.3 0.7 dynamic_slice.78
  68.7 0.7 iota_compare_fusion.3
  69.5 0.3 fusion.78
  69.8 0.3 fusion.79
  70.8 1.7 %fusion.83 = bf16[6,40,64]{2,1,0:T(8,128)(2,1)} fusion(bf16[6,40,64]{2,1,0:T(8,128)(2,1)} %get-tuple-element.236, s32[]{:T(128)} %get-tuple-element.235, f32[40,64]{1,0:T(8,128)S(1)} %fusion.80, bf16[226,384]{1,0:T(8,128)(2,1)} %get-tuple-element.255, s32[]{:T(128)S(6)} %select_n.180, f32[40,226]{1,0:T(8,128)S(1)} %get-tuple-element.221, ...), kind=kOutput, calls=%fused_computation.8.clone.1 | convolution fusion | flops 1182880 | bytes 116868 | tf_op jit(solution)/shard_map/while/body/eval_jaxpr/dot_general | solution.py:133
  72.4 0.7 dynamic_slice.78
  73.8 0.7 iota_compare_fusion.3
  74.6 0.3 fusion.78
  74.9 0.3 fusion.79
  75.8 1.7 %fusion.83 = bf16[6,40,64]{2,1,0:T(8,128)(2,1)} fusion(bf16[6,40,64]{2,1,0:T(8,128)(2,1)} %get-tuple-element.236, s32[]{:T(128)} %get-tuple-element.235, f32[40,64]{1,0:T(8,128)S(1)} %fusion.80, bf16[226,384]{1,0:T(8,128)(2,1)} %get-tuple-element.255, s32[]{:T(128)S(6)} %select_n.180, f32[40,226]{1,0:T(8,128)S(1)} %get-tuple-element.221, ...), kind=kOutput, calls=%fused_computation.8.clone.1 | convolution fusion | flops 1182880 | bytes 116868 | tf_op jit(solution)/shard_map/while/body/eval_jaxpr/dot_general | solution.py:133
  77.5 0.9 copy.56
  78.5 1.2 convolution_convert_fusion
  79.7 0.7 iota_compare_fusion.1
  80.5 19.4 %reduce-scatter.2.cloned.1.call-done = bf16[40,768]{1,0:T(8,128)(2,1)} async-done(((bf16[40,3072]{1,0:T(8,128)(2,1)}), bf16[40,768]{1,0:T(8,128)(2,1)}) %reduce-scatter.2.cloned.1.call-update) | async-done | bytes 61456 | tf_op jit(solution)/shard_map/reduce_scatter | solution.py:141
  99.8 0.9 fusion.35
  100.9 8.7 %all-reduce = (f32[40]{0:T(128)S(1)}, f32[40]{0:T(128)S(1)}) all-reduce(f32[40]{0:T(128)S(1)} %get-tuple-element.105, f32[40]{0:T(128)S(1)} %get-tuple-element.104), channel_id=1, replica_groups=mesh['cfg'=2,'seq'=4,'tp'=4] {'tp'}, use_global_device_ids=true, to_apply=%region_19.20 | all-reduce | flops 80 | bytes 640 | tf_op jit(solution)/shard_map/psum | solution.py:147
  109.6 0.4 fusion.31
  110.0 17.5 %psum.23 = f32[40,64]{0,1:T(8,128)S(1)} all-reduce(f32[40,64]{0,1:T(8,128)S(1)} %fusion.31), channel_id=1, replica_groups=mesh['cfg'=2,'seq'=4,'tp'=4] {'tp'}, use_global_device_ids=true, to_apply=%region_20.21 | all-reduce | flops 2560 | bytes 20480 | tf_op jit(solution)/shard_map/psum | solution.py:159
  128.2 1.4 fusion.60
  132.2 0.6 add_select_fusion
  (105 shorter events, 7.7 us)
Async XLA Ops:
  7.2 71.3 %copy-start = (bf16[384,3072]{1,0:T(8,128)(2,1)S(1)}, bf16[384,3072]{1,0:T(8,128)(2,1)}, u32[]{:S(2)}) copy-start(bf16[384,3072]{1,0:T(8,128)(2,1)} %param.25) | copy-start | bytes 7077892
  7.2 92.6 %reduce-scatter.2.cloned.1.call-start = ((), (), s32[]{:S(2)}) async-start(), calls=%async_computation.1 | async-start | bytes 307200 | tf_op jit(solution)/shard_map/reduce_scatter | solution.py:141
  30.4 3.1 %copy-start.12 = (f32[40]{0:T(128)S(1)}, f32[40]{0:T(128)}, u32[]{:S(2)}) copy-start(f32[40]{0:T(128)} %fusion.57) | copy-start | bytes 484
  30.5 5.2 %copy-start.10 = (f32[40]{0:T(128)S(1)}, f32[40]{0:T(128)}, u32[]{:S(2)}) copy-start(f32[40]{0:T(128)} %get-tuple-element.157) | copy-start | bytes 484
  30.5 5.2 %copy-start.11 = (f32[40]{0:T(128)S(1)}, f32[40]{0:T(128)}, u32[]{:S(2)}) copy-start(f32[40]{0:T(128)} %get-tuple-element.158) | copy-start | bytes 484
  32.3 6.2 %copy-start.9 = (f32[64]{0:T(128)S(1)}, f32[64]{0:T(128)}, u32[]{:S(2)}) copy-start(f32[64]{0:T(128)} %param.31) | copy-start | bytes 772
  32.3 6.3 %copy-start.4 = (bf16[1,40,384]{2,1,0:T(8,128)(2,1)S(1)}, bf16[1,40,384]{2,1,0:T(8,128)(2,1)}, u32[]{:S(2)}) copy-start(bf16[1,40,384]{2,1,0:T(8,128)(2,1)} %param.22) | copy-start | bytes 92164
  47.0 33.5 %copy-start.8 = (f32[768]{0:T(1024)S(1)}, f32[768]{0:T(1024)}, u32[]{:S(2)}) copy-start(f32[768]{0:T(1024)} %param.28) | copy-start | bytes 9220
  47.0 52.8 %copy-start.3 = (bf16[1,40,768]{2,1,0:T(8,128)(2,1)S(1)}, bf16[1,40,768]{2,1,0:T(8,128)(2,1)}, u32[]{:S(2)}) copy-start(bf16[1,40,768]{2,1,0:T(8,128)(2,1)} %param.19) | copy-start | bytes 184324
  47.0 52.8 %copy-start.6 = (f32[768]{0:T(1024)S(1)}, f32[768]{0:T(1024)}, u32[]{:S(2)}) copy-start(f32[768]{0:T(1024)} %param.26) | copy-start | bytes 9220
  77.5 32.1 %copy-start.2 = (f32[768,64]{0,1:T(8,128)S(1)}, f32[768,64]{0,1:T(8,128)}, u32[]{:S(2)}) copy-start(f32[768,64]{0,1:T(8,128)} %param.29) | copy-start | bytes 589828
  77.5 32.1 %copy-start.5 = (f32[768]{0:T(1024)S(1)}, f32[768]{0:T(1024)}, u32[]{:S(2)}) copy-start(f32[768]{0:T(1024)} %param.27) | copy-start | bytes 9220
  77.5 54.7 %copy-start.7 = (f32[40,8]{0,1:T(8,128)S(1)}, f32[40,8]{0,1:T(8,128)}, u32[]{:S(2)}) copy-start(f32[40,8]{0,1:T(8,128)} %param.33) | copy-start | bytes 3844
  100.7 32.1 %copy-start.1 = (bf16[40,768]{1,0:T(8,128)(2,1)}, bf16[40,768]{1,0:T(8,128)(2,1)S(1)}, u32[]{:S(2)}) copy-start(bf16[40,768]{1,0:T(8,128)(2,1)S(1)} %fusion.35) | copy-start | bytes 184324
  127.5 4.7 %collective-permute-start = (f32[40,64]{0,1:T(8,128)S(1)}, f32[40,64]{0,1:T(8,128)S(1)}, u32[]{:S(2)}, u32[]{:S(2)}) collective-permute-start(f32[40,64]{0,1:T(8,128)S(1)} %psum.23), channel_id=1, source_target_pairs={{0,16},{16,0},{1,17},{17,1},{2,18},{18,2},{3,19},{19,3},{4,20},{20... | collective-permute-start | bytes 30728 | tf_op jit(solution)/shard_map/ppermute | solution.py:19
Sparse Core Ops, SparseCore 0:
  79.9 19.9 reduce-scatter.1
where the time goes:
time: 141 us; the launch traced here: 140 us
  blocking collectives  44.5 us (32%)
  other arithmetic  22.2 us (16%)
  waiting for transfers between devices  19.4 us (14%)
  between operations  17.7 us (13%)
  matrix products  16.5 us (12%)
  local copies, waits for them, and re-layouts  14.9 us (11%)
  loops' own time  4.33 us (3%)
    reduce_scatter x1, waiting for transfers between devices, shards(): lax.psum_scatter(projected.astype(jnp.bfloat16), 'tp', scatter_dimension=...  19.4 us
    psum x1, blocking collectives, shards(): prediction = lax.psum(partial_pred, 'tp')  17.5 us
    all_gather x1, blocking collectives, shards(): lax.all_gather(outgoing, 'seq', axis=0, tiled=True)  10.1 us
    dot_general x6, matrix products, one_head(): jnp.dot(text_weights.astype(jnp.bfloat16), text_value_part, preferred_ele...  9.94 us
    psum x1, blocking collectives, shards(): lax.psum((jnp.sum(widened, axis=1), jnp.sum(widened * widened, axis=1)),...  8.72 us
    all_gather x1, blocking collectives, shards(): lax.all_gather(values[0], 'seq', axis=0, tiled=True)  8.24 us
    lt x6, other arithmetic, shards(): video_live = (within[None, :] < lengths[:, None]).reshape(-1)  4.38 us
    another operation x1, loops' own time, shards(): attended = lax.map(one_head, jnp.arange(heads_here, dtype=jnp.int32))  4.33 us
  transfers between devices with their start and end apart: 2, of which 1 were waited for; matrix products, arithmetic and copies ran while one was open for 1% of the time, Pallas kernels for 0%

commit v1 on v0

v1 whole, which is shorter than its diff:
```python
import functools
import math

import jax
import jax.numpy as jnp
from jax import lax
from jax.experimental import pallas as pl
from jax.experimental.pallas import tpu as pltpu
from jax.sharding import PartitionSpec as P

HEAD = 64
PAIR = 2 * HEAD
HP = 30
WP = 45
STRIDE = 20
LANES = 128

guide_scale = 6.0
head_eps = 1e-06
final_eps = 1e-05

F32 = jnp.float32
BF16 = jnp.bfloat16
VMEM_LIMIT = 24 * 1024 * 1024


def call(kernel, outs, n_in, smem=(), hbm=(), scratch=(), cost=0):
    spaces = [
        pltpu.SMEM if i in smem else pl.ANY if i in hbm else pltpu.VMEM for i in range(n_in)
    ]
    many = isinstance(outs, (list, tuple))
    vmem = pl.BlockSpec(memory_space=pltpu.VMEM)
    return pl.pallas_call(
        kernel,
        out_shape=outs,
        in_specs=[pl.BlockSpec(memory_space=s) for s in spaces],
        out_specs=[vmem] * len(outs) if many else vmem,
        scratch_shapes=list(scratch),
        compiler_params=pltpu.CompilerParams(vmem_limit_bytes=VMEM_LIMIT),
        cost_estimate=pl.CostEstimate(flops=cost, bytes_accessed=cost // 64, transcendentals=0),
    )


def shape(dims, dtype=F32):
    return jax.ShapeDtypeStruct(dims, dtype)


def rows_of(parts, dtype):
    return jnp.concatenate([p.astype(F32) for p in parts], axis=0).astype(dtype)


def nt(left, right):
    return lax.dot_general(left, right, (((1,), (1,)), ((), ())), preferred_element_type=F32)


def nn(left, right):
    return jnp.dot(left, right, preferred_element_type=F32)


def prior(lengths, rank, blocks):
    total = jnp.int32(0)
    for i in range(blocks):
        total = total + jnp.where(i < rank, lengths[i], 0)
    return total


def averager():
    row = lax.broadcasted_iota(jnp.int32, (PAIR, PAIR), 0)
    col = lax.broadcasted_iota(jnp.int32, (PAIR, PAIR), 1)
    return jnp.where((row < HEAD) == (col < HEAD), 1.0 / HEAD, 0.0).astype(BF16)


def head_norm(field, average, gain):
    centre = field.astype(F32) - nn(field, average)
    square = centre * centre
    high = square.astype(BF16)
    low = (square - high.astype(F32)).astype(BF16)
    spread = nn(high, average) + nn(low, average)
    return centre * lax.rsqrt(spread + head_eps) * gain


def rope_tables(start, rows):
    lane = lax.broadcasted_iota(jnp.int32, (rows, PAIR), 1)
    pos = (lax.broadcasted_iota(jnp.int32, (rows, PAIR), 0) + start).astype(F32)
    frame = jnp.floor((pos + 0.5) * (1.0 / (HP * WP)))
    line = jnp.floor((pos + 0.5) * (1.0 / WP))
    across = pos - line * WP
    height = line - frame * HP
    pair = (lane % HEAD) // 2
    in_frame = pair < 8
    in_height = pair < 20
    coord = jnp.where(in_frame, frame, jnp.where(in_height, height, across))
    step = jnp.where(in_frame, pair, jnp.where(in_height, pair - 8, pair - 20)).astype(F32)
    rate = jnp.where(in_frame, 2.0 / 16, 2.0 / 24)
    angle = coord * jnp.exp(step * rate * (-math.log(10000.0)))
    sine = jnp.sin(angle)
    return jnp.cos(angle), jnp.where(lane % 2 == 0, -sine, sine)


def rotate(field, cos_table, sin_table):
    even = lax.broadcasted_iota(jnp.int32, field.shape, 1) % 2 == 0
    other = jnp.where(even, pltpu.roll(field, PAIR - 1, 1), pltpu.roll(field, 1, 1))
    return field * cos_table + other * sin_table


def twice(gain_ref):
    gain = gain_ref[...]
    return jnp.concatenate([gain, gain], axis=1)


def pack_keys_kernel(blocks, lengths, keys, values, gain, packed):
    rows, width = keys.shape[1:]
    start = prior(lengths, lax.axis_index("seq"), blocks)
    tables = rope_tables(start, rows)
    average, gain = averager(), twice(gain)
    for at in range(0, width, PAIR):
        normed = head_norm(keys[0, :, at : at + PAIR], average, gain)
        packed[:, at : at + PAIR] = rotate(normed, *tables).astype(BF16)
    packed[:, width:] = values[0]


def queries_kernel(blocks, order, lengths, queries, text_keys, q_gain, k_gain, stacked, text_scores, bias):
    rows, width = queries.shape[1:]
    rank = lax.axis_index("seq")
    tables = rope_tables(prior(lengths, rank, blocks), rows)
    average, q_gain, k_gain = averager(), twice(q_gain), twice(k_gain)
    left = lax.broadcasted_iota(jnp.int32, (rows, PAIR), 1) < HEAD
    for p, at in enumerate(range(0, width, PAIR)):
        query = rotate(head_norm(queries[0, :, at : at + PAIR], average, q_gain), *tables)
        query = query.astype(BF16).astype(F32) * 0.125
        both = jnp.concatenate([jnp.where(left, query, 0.0), jnp.where(left, 0.0, query)], axis=0)
        both = both.astype(BF16)
        stacked[p] = both
        key = head_norm(text_keys[0, :, at : at + PAIR], average, k_gain).astype(BF16)
        text_scores[p] = nt(both, key)
    lane = lax.broadcasted_iota(jnp.int32, bias.shape, 1)
    live = lane < 0
    for i, block in enumerate(order(rank)):
        live = live | ((lane >= i * rows) & (lane < i * rows + lengths[block]))
    bias[...] = jnp.where(live, 0.0, -jnp.inf)


def attend_kernel(n_blocks, sends, stacked, text_scores, bias, text_values, weight, *rest):
    gathered = rest[:n_blocks]
    attended, outs = rest[n_blocks], rest[n_blocks + 1 : -2]
    held, sem = rest[-2:]
    fetch = pltpu.make_async_copy(weight, held, sem)
    fetch.start()
    pairs, double = stacked.shape[:2]
    rows, width = double // 2, pairs * PAIR
    if n_blocks > 1:
        video = rows_of([g[...] for g in gathered], BF16)
    else:
        video = gathered[0][...]
    left = lax.broadcasted_iota(jnp.int32, (rows, PAIR), 1) < HEAD
    parts = []
    for p in range(pairs):
        at = p * PAIR
        scores_t = text_scores[p]
        scores_v = nt(stacked[p], video[:, at : at + PAIR]) + bias[...]
        row_max = jnp.maximum(
            jnp.max(scores_t, axis=1, keepdims=True), jnp.max(scores_v, axis=1, keepdims=True)
        )
        weights_t = jnp.exp(scores_t - row_max)
        weights_v = jnp.exp(scores_v - row_max)
        totals = jnp.sum(weights_t, axis=1, keepdims=True) + jnp.sum(weights_v, axis=1, keepdims=True)
        mixed = nn(weights_t.astype(BF16), text_values[0, :, at : at + PAIR])
        mixed = mixed + nn(weights_v.astype(BF16), video[:, width + at : width + at + PAIR])
        mixed = mixed / totals
        parts.append(jnp.where(left, mixed[:rows], mixed[rows:]).astype(BF16))
    joined = jnp.concatenate(parts, axis=1)
    attended[...] = joined
    fetch.wait()
    rank = lax.axis_index("tp")
    for out, block in zip(outs, sends(rank)):
        columns = out.shape[1]
        out[...] = nn(joined, held[:, pl.ds(pl.multiple_of(block * columns, columns), columns)]).astype(BF16)


def residual_kernel(
    tp, lengths, alphas, step, attended, weight, stream, gate, shift, scale, proj, latents,
    base, factor, mask, split, consts, coefs, held, sem,
):
    rank = lax.axis_index("tp")
    rows, columns = base.shape
    fetch = pltpu.make_async_copy(
        weight.at[:, pl.ds(pl.multiple_of(rank * columns, columns), columns)], held, sem
    )
    fetch.start()
    count = lengths[lax.axis_index("seq")]
    row = lax.broadcasted_iota(jnp.int32, mask.shape, 0)
    mask[...] = jnp.where(row < count, 1.0, 0.0)
    factor[...] = jnp.where(row[:, :1] < count, gate[...], 0.0)
    channels = proj.shape[0]
    plain = proj[...]
    scaled = plain * (1.0 + scale[...])
    high = scaled.astype(BF16)
    rest = scaled - high.astype(F32)
    middle = rest.astype(BF16)
    split[0:channels] = high
    split[channels : 2 * channels] = middle
    split[2 * channels : 3 * channels] = (rest - middle.astype(F32)).astype(BF16)
    split[3 * channels :] = jnp.ones((16, columns), BF16)
    lane = lax.broadcasted_iota(jnp.int32, consts.shape, 1)
    consts[...] = jnp.where(
        lane == rows,
        jnp.sum(scaled, axis=1, keepdims=True),
        jnp.where(lane == rows + 1, jnp.sum(plain * shift[...], axis=1, keepdims=True), 0.0),
    )
    at = step[0]
    now = jnp.full((8, LANES), alphas[at], F32)
    earlier = jnp.full((8, LANES), alphas[at - STRIDE], F32)
    coefs[0:8] = jnp.sqrt(now)
    coefs[8:16] = jnp.sqrt(1.0 - now)
    coefs[16:24] = jnp.sqrt(earlier)
    coefs[24:32] = jnp.sqrt(1.0 - earlier)
    lane8 = lax.broadcasted_iota(jnp.int32, (8, LANES), 1)
    coefs[32:40] = jnp.where(lane8 < count, 1.0, 0.0)
    coefs[40:48] = jnp.concatenate([latents[...], jnp.zeros((8, LANES - rows), F32)], axis=1)
    fetch.wait()
    base[...] = jnp.where(
        row[:, :1] < count, stream[0].astype(F32) + gate[...] * nn(attended[...], held[...]), 0.0
    )


def hidden_kernel(tp, base, factor, mask, split, consts, *rest):
    arrived, (hidden, *outs), scratch = rest[: tp - 1], rest[tp - 1 : -1], rest[-1]
    summed = arrived[0][...].astype(F32)
    for block in arrived[1:]:
        summed = summed + block[...].astype(F32)
    value = (base[...] + factor[...] * summed).astype(BF16)
    hidden[0] = value
    rows = value.shape[0]
    channels = consts.shape[0]
    wide = value.astype(F32)
    square = wide * wide
    high = square.astype(BF16)
    low = (square - high.astype(F32)).astype(BF16)
    ones = split[3 * channels :]
    first = nt(split[...], value)
    partial = first[:channels] + first[channels : 2 * channels] + first[2 * channels : 3 * channels]
    total = first[3 * channels : 3 * channels + 8]
    squares = (nt(ones, high) + nt(ones, low))[:8]
    blank = jnp.zeros((channels, LANES - rows), F32)
    scratch[...] = jnp.concatenate([partial, blank], axis=1) + consts[...]
    row = lax.broadcasted_iota(jnp.int32, (8, rows), 0)
    stats = jnp.concatenate([jnp.where(row == 0, total, squares), blank[:8]], axis=1)
    rank = lax.axis_index("tp")
    for i, out in enumerate(outs):
        block = rank ^ i
        for half in range(2):
            out[8 * half : 8 * half + 8] = scratch[pl.ds(pl.multiple_of((half * tp + block) * 8, 8), 8)]
        out[16:24] = stats


def total_kernel(own, *rest):
    arrived, (mine, other) = rest[:-2], rest[-2:]
    total = own[...]
    for block in arrived:
        total = total + block[...]
    half = lax.axis_index("cfg")
    first, second, stats = total[0:8], total[8:16], total[16:24]
    mine[0:8] = jnp.where(half == 0, first, second)
    mine[8:16] = stats
    other[0:8] = jnp.where(half == 0, second, first)
    other[8:16] = stats


def step_kernel(features, mine, theirs, coefs, out):
    rows = out.shape[1]

    def predict(block, consts):
        sums = block[0:8, :rows]
        mean = block[8:9, :rows] / features
        square = block[9:10, :rows] / features
        spread = lax.rsqrt(square - mean * mean + final_eps)
        return spread * (sums - mean * consts[0:8, rows : rows + 1]) + consts[0:8, rows + 1 : rows + 2]

    own, partner = predict(mine, mine), predict(theirs, mine)
    is_conditioned = lax.axis_index("cfg") == 0
    conditioned = jnp.where(is_conditioned, own, partner)
    unconditioned = jnp.where(is_conditioned, partner, own)
    guided = unconditioned + guide_scale * (conditioned - unconditioned)
    root_now, rest_now, root_next, rest_next, live, latents = (
        coefs[8 * i : 8 * i + 8, :rows] for i in range(6)
    )
    clean = root_now * latents - rest_now * guided
    noise = root_now * guided + rest_now * latents
    out[...] = jnp.where(live > 0.0, root_next * clean + rest_next * noise, 0.0)


def exchange(value, axis, distance):
    return lax.ppermute(value, axis, [(i, i ^ distance) for i in range(lax.axis_size(axis))])


def shards(
    stream, queries, keys, values, text_keys, text_values, out_weight, gate, shift, scale, proj_weight,
    q_gain, k_gain, lengths, latents, alphas, step_index,
):
    blocks = lax.axis_size("seq")
    tp = lax.axis_size("tp")
    rows, width = queries.shape[1:]
    columns = stream.shape[2]
    text = text_keys.shape[1]
    channels = proj_weight.shape[1]
    pairs = width // PAIR
    direct = blocks <= 4 and blocks & (blocks - 1) == 0

    q_gain, k_gain = q_gain.reshape(1, HEAD), k_gain.reshape(1, HEAD)
    packed = call(
        functools.partial(pack_keys_kernel, blocks), shape((rows, 2 * width), BF16), 4, smem=(0,), cost=2000000
    )(lengths, keys, values, k_gain)
    if direct:
        gathered = [packed] + [exchange(packed, "seq", d) for d in range(1, blocks)]
        order = lambda rank: [rank ^ d for d in range(blocks)]
    else:
        gathered = [lax.all_gather(packed, "seq", axis=0, tiled=True)]
        order = lambda rank: range(blocks)
    stacked, text_scores, bias = call(
        functools.partial(queries_kernel, blocks, order),
        [
            shape((pairs, 2 * rows, PAIR), BF16),
            shape((pairs, 2 * rows, text)),
            shape((1, blocks * rows)),
        ],
        5,
        smem=(0,),
        cost=20000000,
    )(lengths, queries, text_keys, q_gain, k_gain)
    sends = lambda rank: [rank ^ d for d in range(1, tp)]
    attended, *outgoing = call(
        functools.partial(attend_kernel, len(gathered), sends),
        [shape((rows, width), BF16)] + [shape((rows, columns), BF16)] * (tp - 1),
        5 + len(gathered),
        hbm=(4,),
        scratch=[pltpu.VMEM(out_weight.shape, BF16), pltpu.SemaphoreType.DMA],
        cost=100000000,
    )(stacked, text_scores, bias, text_values, out_weight, *gathered)
    arrived = [exchange(block, "tp", d) for d, block in enumerate(outgoing, 1)]
    base, factor, mask, split, consts, coefs = call(
        functools.partial(residual_kernel, tp),
        [
            shape((rows, columns)),
            shape((rows, columns)),
            shape((rows, LANES)),
            shape((3 * channels + 16, columns), BF16),
            shape((channels, LANES)),
            shape((48, LANES)),
        ],
        11,
        smem=(0, 1, 2),
        hbm=(4,),
        scratch=[pltpu.VMEM((width, columns), BF16), pltpu.SemaphoreType.DMA],
        cost=100000000,
    )(
        lengths, alphas, step_index, attended, out_weight, stream, gate.reshape(1, columns),
        shift.reshape(1, columns), scale.reshape(1, columns), proj_weight.T, latents.T,
    )
    hidden, *partials = call(
        functools.partial(hidden_kernel, tp),
        [shape((1, rows, columns), BF16)] + [shape((24, LANES))] * tp,
        5 + tp - 1,
        scratch=[pltpu.VMEM((channels, LANES), F32)],
        cost=20000000,
    )(base, factor, mask, split, consts, *arrived)
    shares = [exchange(block, "tp", d) for d, block in enumerate(partials) if d]
    mine, other = call(total_kernel, [shape((16, LANES))] * 2, tp)(partials[0], *shares)
    theirs = exchange(other, "cfg", 1)
    latents_out = call(
        functools.partial(step_kernel, columns * tp), shape((latents.shape[1], rows)), 3
    )(mine, theirs, coefs)
    return hidden, latents_out.T


def solution(mesh):
    return jax.shard_map(
        shards,
        mesh=mesh,
        in_specs=(
            P("cfg", "seq", "tp"),
            P("cfg", "seq", "tp"),
            P("cfg", "seq", "tp"),
            P("cfg", "seq", "tp"),
            P("cfg", None, "tp"),
            P("cfg", None, "tp"),
            P("tp", None),
            P("tp"),
            P("tp"),
            P("tp"),
            P("tp", None),
            P(),
            P(),
            P(),
            P("seq", ("cfg", "tp")),
            P(),
            P(),
        ),
        out_specs=(P("cfg", "seq", "tp"), P("seq", ("cfg", "tp"))),
        check_vma=False,
    )
```

time: 141 us -> 38.7 us (0.27)
  blocking collectives: 44.5 us -> 0 us
  other arithmetic: 22.2 us -> 0 us
  matrix products: 16.5 us -> 0 us
  between operations: 17.7 us -> 1.49 us
  starting transfers between devices: 0.11 us -> 13.6 us
  waiting for transfers between devices: 19.4 us -> 7.79 us
  Pallas kernels: 0 us -> 6.92 us
  local copies, waits for them, and re-layouts: 14.9 us -> 8.46 us
  loops' own time: 4.33 us -> 0 us
    psum x2 -> x0, blocking collectives: 26.2 us -> none  [the longest x1 17.5 us: shards(): prediction = lax.psum(partial_pred, 'tp')]
    reduce_scatter x1 -> x0, waiting for transfers between devices: 19.4 us -> none  [shards(): lax.psum_scatter(projected.astype(jnp.bfloat16), 'tp', scatter_dimension=...]
    all_gather x2 -> x0, blocking collectives: 18.3 us -> none  [the longest x1 10.1 us: shards(): lax.all_gather(outgoing, 'seq', axis=0, tiled=True)]
    dot_general x26 -> x0, matrix products: 16.5 us -> none  [the longest x6 9.94 us: one_head(): jnp.dot(text_weights.astype(jnp.bfloat16), text_value_part, preferred_ele...]
    ppermute x1 -> x10, starting transfers between devices: 0.07 us -> 13.6 us  [exchange(): lax.ppermute(value, axis, [(i, i ^ distance) for i in range(lax.axis_size...]
    ppermute x1 -> x10, waiting for transfers between devices: 0.01 us -> 7.79 us  [exchange(): lax.ppermute(value, axis, [(i, i ^ distance) for i in range(lax.axis_size...]
    unnamed x28 -> x36, local copies, waits for them, and re-layouts: 1.21 us -> 8.44 us
    pallas_call x0 -> x7, Pallas kernels: none -> 6.92 us  [the longest x1 2.06 us: shards(): call(functools.partial(queries_kernel, blocks, order), [shape((pairs, 2 *...]
  transfers between devices with their start and end apart: 2 -> 10, of which waited for: 1 -> 5; matrix products, arithmetic and copies ran while one was open for 1% -> 0% of each run, Pallas kernels for 0% -> 8%
where the time goes in v1:
time: 38.7 us; the launch traced here: 38.3 us
  starting transfers between devices  13.6 us (35%)
  local copies, waits for them, and re-layouts  8.46 us (22%)
  waiting for transfers between devices  7.79 us (20%)
  Pallas kernels  6.92 us (18%)
  between operations  1.49 us (4%)
    ppermute x10, starting transfers between devices, exchange(): lax.ppermute(value, axis, [(i, i ^ distance) for i in range(lax.axis_size...  13.6 us
    unnamed x36, local copies, waits for them, and re-layouts  8.44 us
    ppermute x10, waiting for transfers between devices, exchange(): lax.ppermute(value, axis, [(i, i ^ distance) for i in range(lax.axis_size...  7.79 us
    pallas_call x1, Pallas kernels, shards(): call(functools.partial(queries_kernel, blocks, order), [shape((pairs, 2 *...  2.06 us
    pallas_call x1, Pallas kernels, shards(): call(functools.partial(pack_keys_kernel, blocks), shape((rows, 2 * width)...  1.19 us
    pallas_call x1, Pallas kernels, shards(): call(functools.partial(attend_kernel, len(gathered), sends), [shape((rows...  1.16 us
    pallas_call x1, Pallas kernels, shards(): call(functools.partial(residual_kernel, tp), [shape((rows, columns)), sha...  1.05 us
  transfers between devices with their start and end apart: 10, of which 5 were waited for; matrix products, arithmetic and copies ran while one was open for 0% of the time, Pallas kernels for 8%

profile of v1, /device:TPU:0, one launch (start us, length us, event | category | flops | bytes accessed | tf_op | source)
XLA Modules:
  0.0 38.3 jit_solution(4502468023127723227)
XLA Ops:
  0.6 0.0 copy-start.2
  0.6 0.0 copy-start.7
  0.7 0.8 %copy-done.7 = bf16[1,40,384]{2,1,0:T(8,128)(2,1)S(1)} copy-done((bf16[1,40,384]{2,1,0:T(8,128)(2,1)S(1)}, bf16[1,40,384]{2,1,0:T(8,128)(2,1)}, u32[]{:S(2)}) %copy-start.7) | copy-done | bytes 30744
  1.4 0.0 copy-start.8
  1.4 0.8 %copy-done.8 = bf16[1,40,384]{2,1,0:T(8,128)(2,1)S(1)} copy-done((bf16[1,40,384]{2,1,0:T(8,128)(2,1)S(1)}, bf16[1,40,384]{2,1,0:T(8,128)(2,1)}, u32[]{:S(2)}) %copy-start.8) | copy-done | bytes 30744
  2.2 0.0 copy-start.9
  2.2 0.7 %copy-done.9 = s32[4]{0:T(128)S(1)} copy-done((s32[4]{0:T(128)S(1)}, s32[4]{0:T(128)}, u32[]{:S(2)}) %copy-start.9) | copy-done | bytes 40
  2.8 0.0 copy-start.12
  2.8 0.7 %copy-done.12 = f32[64]{0:T(128)S(1)} copy-done((f32[64]{0:T(128)S(1)}, f32[64]{0:T(128)}, u32[]{:S(2)}) %copy-start.12) | copy-done | bytes 280
  3.5 1.2 %shard_map.177.rest_0_ = bf16[40,768]{1,0:T(8,128)(2,1)S(1)} custom-call(s32[4]{0:T(128)S(1)} %copy-done.9, bf16[1,40,384]{2,1,0:T(8,128)(2,1)S(1)} %copy-done.7, bf16[1,40,384]{2,1,0:T(8,128)(2,1)S(1)} %copy-done.8, f32[1,64]{1,0:T(1,128)S(1)} %bitcast.7), custom_call_target="tpu_custom_call" | custom-call | flops 2000000 | bytes 31250 | tf_op jit(solution)/shard_map/pallas_call | solution.py:310
  4.7 4.0 %collective-permute-start.2 = (bf16[40,768]{1,0:T(8,128)(2,1)S(1)}, bf16[40,768]{1,0:T(8,128)(2,1)S(1)}, u32[]{:S(2)}, u32[]{:S(2)}) collective-permute-start(bf16[40,768]{1,0:T(8,128)(2,1)S(1)} %shard_map.177.rest_0_), channel_id=1, source_target_pairs={{0,12},{4,8},{8,4},{12,0},{1,13},{5,9},{9,5},{13,1},{2,14},{6,10},... | collective-permute-start | bytes 184328 | tf_op jit(solution)/shard_map/ppermute | solution.py:293
  8.6 0.5 %collective-permute-start.1 = (bf16[40,768]{1,0:T(8,128)(2,1)S(1)}, bf16[40,768]{1,0:T(8,128)(2,1)S(1)}, u32[]{:S(2)}, u32[]{:S(2)}) collective-permute-start(bf16[40,768]{1,0:T(8,128)(2,1)S(1)} %shard_map.177.rest_0_), channel_id=1, source_target_pairs={{0,8},{4,12},{8,0},{12,4},{1,9},{5,13},{9,1},{13,5},{2,10},{6,14},... | collective-permute-start | bytes 184328 | tf_op jit(solution)/shard_map/ppermute | solution.py:293
  9.2 0.1 collective-permute-start
  9.3 0.0 copy-start.4
  9.3 0.9 %copy-done.4 = bf16[1,226,384]{2,1,0:T(8,128)(2,1)S(1)} copy-done((bf16[1,226,384]{2,1,0:T(8,128)(2,1)S(1)}, bf16[1,226,384]{2,1,0:T(8,128)(2,1)}, u32[]{:S(2)}) %copy-start.4) | copy-done | bytes 173592
  10.2 0.0 copy-start.6
  10.2 0.8 %copy-done.6 = bf16[1,40,384]{2,1,0:T(8,128)(2,1)S(1)} copy-done((bf16[1,40,384]{2,1,0:T(8,128)(2,1)S(1)}, bf16[1,40,384]{2,1,0:T(8,128)(2,1)}, u32[]{:S(2)}) %copy-start.6) | copy-done | bytes 30744
  11.0 0.0 copy-start.13
  11.0 0.7 %copy-done.13 = f32[64]{0:T(128)S(1)} copy-done((f32[64]{0:T(128)S(1)}, f32[64]{0:T(128)}, u32[]{:S(2)}) %copy-start.13) | copy-done | bytes 280
  11.6 0.0 copy-start.14
  11.6 0.7 %copy-done.14 = f32[64]{0:T(128)S(1)} copy-done((f32[64]{0:T(128)S(1)}, f32[64]{0:T(128)}, u32[]{:S(2)}) %copy-start.14) | copy-done | bytes 280
  12.3 0.0 copy-start.15
  12.3 0.0 copy-start.16
  12.3 0.0 copy-start.17
  12.3 0.0 copy-start.5
  12.3 0.0 copy-start.10
  12.3 0.0 copy-start.11
  12.3 2.1 %shard_map.176 = (bf16[3,80,128]{2,1,0:T(8,128)(2,1)S(1)}, f32[3,80,226]{2,1,0:T(8,128)S(1)}, f32[1,160]{1,0:T(1,128)S(1)}) custom-call(s32[4]{0:T(128)S(1)} %copy-done.9, bf16[1,40,384]{2,1,0:T(8,128)(2,1)S(1)} %copy-done.6, bf16[1,226,384]{2,1,0:T(8,128)(2,1)S(1)} %copy-done.4, f32[1,64]{1,0:T(1,128)S(1)} %bitcast.9, f32[1,64]{1,0:T(1,128)S(1)} %bitcast.8), custom_call_target="tpu_custom_call" | custom-call | flops 20000000 | bytes 312500 | tf_op jit(solution)/shard_map/pallas_call | solution.py:319
  14.4 0.0 collective-permute-done.2.rest_3_
  14.4 0.0 collective-permute-done.1.rest_2_
  14.4 0.0 collective-permute-done.rest_1_
  14.4 0.0 copy-start
  14.4 1.7 %copy-done = bf16[384,3072]{1,0:T(8,128)(2,1)S(1)} copy-done((bf16[384,3072]{1,0:T(8,128)(2,1)S(1)}, bf16[384,3072]{1,0:T(8,128)(2,1)}, u32[]{:S(2)}) %copy-start) | copy-done | bytes 2359320
  16.1 0.0 copy-start.3
  16.1 0.9 %copy-done.3 = bf16[1,226,384]{2,1,0:T(8,128)(2,1)S(1)} copy-done((bf16[1,226,384]{2,1,0:T(8,128)(2,1)S(1)}, bf16[1,226,384]{2,1,0:T(8,128)(2,1)}, u32[]{:S(2)}) %copy-start.3) | copy-done | bytes 173592
  17.0 0.0 copy-start.1
  17.0 1.2 %shard_map.178 = (bf16[40,384]{1,0:T(8,128)(2,1)S(1)}, bf16[40,768]{1,0:T(8,128)(2,1)S(1)}, bf16[40,768]{1,0:T(8,128)(2,1)S(1)}, bf16[40,768]{1,0:T(8,128)(2,1)S(1)}) custom-call(bf16[3,80,128]{2,1,0:T(8,128)(2,1)S(1)} %get-tuple-element.22.stacked, f32[3,80,226]{2,1,0:T(8,128)S(1)} %get-tuple-element.23.text_scores, f32[1,160]{1,0:T(1,128)S(1)} %get-tuple-element.24.bias, ...), custom_call_target="tpu_custom_call" | custom-call | flops 100000000 | bytes 1562500 | tf_op jit(solution)/shard_map/pallas_call | solution.py:331
  18.2 2.0 %collective-permute-start.3 = (bf16[40,768]{1,0:T(8,128)(2,1)S(1)}, bf16[40,768]{1,0:T(8,128)(2,1)S(1)}, u32[]{:S(2)}, u32[]{:S(2)}) collective-permute-start(bf16[40,768]{1,0:T(8,128)(2,1)S(1)} %get-tuple-element.31), channel_id=1, source_target_pairs={{0,1},{1,0},{2,3},{3,2},{4,5},{5,4},{6,7},{7,6},{8,9},{9,8},{10,11... | collective-permute-start | bytes 184328 | tf_op jit(solution)/shard_map/ppermute | solution.py:293
  20.2 2.6 %collective-permute-start.4 = (bf16[40,768]{1,0:T(8,128)(2,1)S(1)}, bf16[40,768]{1,0:T(8,128)(2,1)S(1)}, u32[]{:S(2)}, u32[]{:S(2)}) collective-permute-start(bf16[40,768]{1,0:T(8,128)(2,1)S(1)} %get-tuple-element.32), channel_id=1, source_target_pairs={{0,2},{1,3},{2,0},{3,1},{4,6},{5,7},{6,4},{7,5},{8,10},{9,11},{10,... | collective-permute-start | bytes 184328 | tf_op jit(solution)/shard_map/ppermute | solution.py:293
  22.8 0.0 collective-permute-start.5
  23.5 0.0 copy-done.15
  23.5 0.0 copy-done.16
  23.5 0.0 copy-done.17
  23.5 0.0 copy-done.2
  23.5 0.0 copy-done.5
  23.5 0.0 copy-done.10
  23.5 0.0 copy-done.11
  23.6 0.0 copy-done.1
  23.6 1.1 %shard_map.179 = (f32[40,768]{1,0:T(8,128)S(1)}, f32[40,768]{1,0:T(8,128)S(1)}, f32[40,128]{1,0:T(8,128)S(1)}, bf16[208,768]{1,0:T(8,128)(2,1)S(1)}, f32[64,128]{1,0:T(8,128)S(1)}, /*index=5*/f32[48,128]{1,0:T(8,128)S(1)}) custom-call(s32[4]{0:T(128)S(1)} %copy-done.9, f32[1000]{0:T(1024)S(1)} %copy-done.10, s32[1]{0:T(128)S(6)} %copy.19.step, ...), custom_call_target="tpu_custom_call" | custom-call | flops 100000000 | bytes 1562500 | tf_op jit(solution)/shard_map/pallas_call | solution.py:340
  24.6 0.0 collective-permute-done.3.rest_0_
  24.6 2.0 %collective-permute-done.4.rest_1_ = bf16[40,768]{1,0:T(8,128)(2,1)S(1)} collective-permute-done((bf16[40,768]{1,0:T(8,128)(2,1)S(1)}, bf16[40,768]{1,0:T(8,128)(2,1)S(1)}, u32[]{:S(2)}, u32[]{:S(2)}) %collective-permute-start.4) | collective-permute-done | bytes 61472 | tf_op jit(solution)/shard_map/ppermute | solution.py:293
  26.6 2.2 %collective-permute-done.5.rest_2_ = bf16[40,768]{1,0:T(8,128)(2,1)S(1)} collective-permute-done((bf16[40,768]{1,0:T(8,128)(2,1)S(1)}, bf16[40,768]{1,0:T(8,128)(2,1)S(1)}, u32[]{:S(2)}, u32[]{:S(2)}) %collective-permute-start.5) | collective-permute-done | bytes 61472 | tf_op jit(solution)/shard_map/ppermute | solution.py:293
  28.8 0.8 %shard_map.180 = (bf16[1,40,768]{2,1,0:T(8,128)(2,1)}, f32[24,128]{1,0:T(8,128)S(1)}, f32[24,128]{1,0:T(8,128)S(1)}, f32[24,128]{1,0:T(8,128)S(1)}, f32[24,128]{1,0:T(8,128)S(1)}) custom-call(f32[40,768]{1,0:T(8,128)S(1)} %get-tuple-element.26.base, f32[40,768]{1,0:T(8,128)S(1)} %get-tuple-element.27.factor, f32[40,128]{1,0:T(8,128)S(1)} %get-tuple-element.28.mask, ...), custom_call_target="tpu_custom_call" | custom-call | flops 20000000 | bytes 312500 | tf_op jit(solution)/shard_map/pallas_call | solution.py:359
  29.6 0.0 collective-permute-start.6
  29.6 1.3 %collective-permute-start.7 = (f32[24,128]{1,0:T(8,128)S(1)}, f32[24,128]{1,0:T(8,128)S(1)}, u32[]{:S(2)}, u32[]{:S(2)}) collective-permute-start(f32[24,128]{1,0:T(8,128)S(1)} %get-tuple-element.37), channel_id=1, source_target_pairs={{0,2},{1,3},{2,0},{3,1},{4,6},{5,7},{6,4},{7,5},{8,10},{9,11},{10,... | collective-permute-start | bytes 36872 | tf_op jit(solution)/shard_map/ppermute | solution.py:293
  30.9 3.1 %collective-permute-start.8 = (f32[24,128]{1,0:T(8,128)S(1)}, f32[24,128]{1,0:T(8,128)S(1)}, u32[]{:S(2)}, u32[]{:S(2)}) collective-permute-start(f32[24,128]{1,0:T(8,128)S(1)} %get-tuple-element.38), channel_id=1, source_target_pairs={{0,3},{1,2},{2,1},{3,0},{4,7},{5,6},{6,5},{7,4},{8,11},{9,10},{10,... | collective-permute-start | bytes 36872 | tf_op jit(solution)/shard_map/ppermute | solution.py:293
  34.0 0.0 collective-permute-done.6.rest_0_
  34.0 0.2 collective-permute-done.7.rest_1_
  34.2 2.2 %collective-permute-done.8.rest_2_ = f32[24,128]{1,0:T(8,128)S(1)} collective-permute-done((f32[24,128]{1,0:T(8,128)S(1)}, f32[24,128]{1,0:T(8,128)S(1)}, u32[]{:S(2)}, u32[]{:S(2)}) %collective-permute-start.8) | collective-permute-done | bytes 12320 | tf_op jit(solution)/shard_map/ppermute | solution.py:293
  36.4 0.0 collective-permute-start.9
  36.4 1.2 %collective-permute-done.9.theirs = f32[16,128]{1,0:T(8,128)S(1)} collective-permute-done((f32[16,128]{1,0:T(8,128)S(1)}, f32[16,128]{1,0:T(8,128)S(1)}, u32[]{:S(2)}, u32[]{:S(2)}) %collective-permute-start.9) | collective-permute-done | bytes 8224 | tf_op jit(solution)/shard_map/ppermute | solution.py:293
  37.6 0.7 %shard_map.182 = f32[8,40]{1,0:T(8,128)} custom-call(f32[16,128]{1,0:T(8,128)S(1)} %get-tuple-element.39.mine, f32[16,128]{1,0:T(8,128)S(1)} %collective-permute-done.9.theirs, f32[48,128]{1,0:T(8,128)S(1)} %get-tuple-element.41.coefs), custom_call_target="tpu_custom_call" | custom-call | tf_op jit(solution)/shard_map/pallas_call | solution.py:369
  (4 shorter events, 0.0 us)
Async XLA Ops:
  0.6 22.9 %copy-start.2 = (f32[768,64]{0,1:T(8,128)S(1)}, f32[768,64]{0,1:T(8,128)}, u32[]{:S(2)}) copy-start(f32[768,64]{0,1:T(8,128)} %param.27) | copy-start | bytes 589828
  0.6 0.8 %copy-start.7 = (bf16[1,40,384]{2,1,0:T(8,128)(2,1)S(1)}, bf16[1,40,384]{2,1,0:T(8,128)(2,1)}, u32[]{:S(2)}) copy-start(bf16[1,40,384]{2,1,0:T(8,128)(2,1)} %keys.1) | copy-start | bytes 92164
  1.4 0.8 %copy-start.8 = (bf16[1,40,384]{2,1,0:T(8,128)(2,1)S(1)}, bf16[1,40,384]{2,1,0:T(8,128)(2,1)}, u32[]{:S(2)}) copy-start(bf16[1,40,384]{2,1,0:T(8,128)(2,1)} %values.1) | copy-start | bytes 92164
  2.2 0.7 %copy-start.9 = (s32[4]{0:T(128)S(1)}, s32[4]{0:T(128)}, u32[]{:S(2)}) copy-start(s32[4]{0:T(128)} %lengths.5) | copy-start | bytes 52
  2.8 0.7 %copy-start.12 = (f32[64]{0:T(128)S(1)}, f32[64]{0:T(128)}, u32[]{:S(2)}) copy-start(f32[64]{0:T(128)} %param.29) | copy-start | bytes 772
  4.7 9.7 %collective-permute-start.2 = (bf16[40,768]{1,0:T(8,128)(2,1)S(1)}, bf16[40,768]{1,0:T(8,128)(2,1)S(1)}, u32[]{:S(2)}, u32[]{:S(2)}) collective-permute-start(bf16[40,768]{1,0:T(8,128)(2,1)S(1)} %shard_map.177.rest_0_), channel_id=1, source_target_pairs={{0,12},{4,8},{8,4},{12,0},{1,13},{5,9},{9,5},{13,1},{2,14},{6,10},... | collective-permute-start | bytes 184328 | tf_op jit(solution)/shard_map/ppermute | solution.py:293
  8.6 5.7 %collective-permute-start.1 = (bf16[40,768]{1,0:T(8,128)(2,1)S(1)}, bf16[40,768]{1,0:T(8,128)(2,1)S(1)}, u32[]{:S(2)}, u32[]{:S(2)}) collective-permute-start(bf16[40,768]{1,0:T(8,128)(2,1)S(1)} %shard_map.177.rest_0_), channel_id=1, source_target_pairs={{0,8},{4,12},{8,0},{12,4},{1,9},{5,13},{9,1},{13,5},{2,10},{6,14},... | collective-permute-start | bytes 184328 | tf_op jit(solution)/shard_map/ppermute | solution.py:293
  9.2 5.2 %collective-permute-start = (bf16[40,768]{1,0:T(8,128)(2,1)S(1)}, bf16[40,768]{1,0:T(8,128)(2,1)S(1)}, u32[]{:S(2)}, u32[]{:S(2)}) collective-permute-start(bf16[40,768]{1,0:T(8,128)(2,1)S(1)} %shard_map.177.rest_0_), channel_id=1, source_target_pairs={{0,4},{4,0},{8,12},{12,8},{1,5},{5,1},{9,13},{13,9},{2,6},{6,2},{1... | collective-permute-start | bytes 184328 | tf_op jit(solution)/shard_map/ppermute | solution.py:293
  9.3 0.9 %copy-start.4 = (bf16[1,226,384]{2,1,0:T(8,128)(2,1)S(1)}, bf16[1,226,384]{2,1,0:T(8,128)(2,1)}, u32[]{:S(2)}) copy-start(bf16[1,226,384]{2,1,0:T(8,128)(2,1)} %text_keys.1) | copy-start | bytes 520708
  10.2 0.8 %copy-start.6 = (bf16[1,40,384]{2,1,0:T(8,128)(2,1)S(1)}, bf16[1,40,384]{2,1,0:T(8,128)(2,1)}, u32[]{:S(2)}) copy-start(bf16[1,40,384]{2,1,0:T(8,128)(2,1)} %queries.1) | copy-start | bytes 92164
  11.0 0.7 %copy-start.13 = (f32[64]{0:T(128)S(1)}, f32[64]{0:T(128)}, u32[]{:S(2)}) copy-start(f32[64]{0:T(128)} %param.29) | copy-start | bytes 772
  11.6 0.7 %copy-start.14 = (f32[64]{0:T(128)S(1)}, f32[64]{0:T(128)}, u32[]{:S(2)}) copy-start(f32[64]{0:T(128)} %param.28) | copy-start | bytes 772
  12.3 11.2 %copy-start.15 = (f32[768]{0:T(1024)S(1)}, f32[768]{0:T(1024)}, u32[]{:S(2)}) copy-start(f32[768]{0:T(1024)} %param.24) | copy-start | bytes 9220
  12.3 11.2 %copy-start.16 = (f32[768]{0:T(1024)S(1)}, f32[768]{0:T(1024)}, u32[]{:S(2)}) copy-start(f32[768]{0:T(1024)} %param.25) | copy-start | bytes 9220
  12.3 11.2 %copy-start.17 = (f32[768]{0:T(1024)S(1)}, f32[768]{0:T(1024)}, u32[]{:S(2)}) copy-start(f32[768]{0:T(1024)} %param.26) | copy-start | bytes 9220
  12.3 11.2 %copy-start.5 = (bf16[1,40,768]{2,1,0:T(8,128)(2,1)S(1)}, bf16[1,40,768]{2,1,0:T(8,128)(2,1)}, u32[]{:S(2)}) copy-start(bf16[1,40,768]{2,1,0:T(8,128)(2,1)} %stream.1) | copy-start | bytes 184324
  12.3 11.3 %copy-start.10 = (f32[1000]{0:T(1024)S(1)}, f32[1000]{0:T(1024)}, u32[]{:S(2)}) copy-start(f32[1000]{0:T(1024)} %alphas.1) | copy-start | bytes 12004
  12.3 11.3 %copy-start.11 = (f32[40,8]{0,1:T(8,128)S(1)}, f32[40,8]{0,1:T(8,128)}, u32[]{:S(2)}) copy-start(f32[40,8]{0,1:T(8,128)} %param.31) | copy-start | bytes 3844
  14.4 1.7 %copy-start = (bf16[384,3072]{1,0:T(8,128)(2,1)S(1)}, bf16[384,3072]{1,0:T(8,128)(2,1)}, u32[]{:S(2)}) copy-start(bf16[384,3072]{1,0:T(8,128)(2,1)} %weight.3) | copy-start | bytes 7077892
  16.1 0.9 %copy-start.3 = (bf16[1,226,384]{2,1,0:T(8,128)(2,1)S(1)}, bf16[1,226,384]{2,1,0:T(8,128)(2,1)}, u32[]{:S(2)}) copy-start(bf16[1,226,384]{2,1,0:T(8,128)(2,1)} %text_values.1) | copy-start | bytes 520708
  17.0 6.6 %copy-start.1 = (bf16[384,3072]{1,0:T(8,128)(2,1)S(1)}, bf16[384,3072]{1,0:T(8,128)(2,1)}, u32[]{:S(2)}) copy-start(bf16[384,3072]{1,0:T(8,128)(2,1)} %weight.3) | copy-start | bytes 7077892
  18.2 6.5 %collective-permute-start.3 = (bf16[40,768]{1,0:T(8,128)(2,1)S(1)}, bf16[40,768]{1,0:T(8,128)(2,1)S(1)}, u32[]{:S(2)}, u32[]{:S(2)}) collective-permute-start(bf16[40,768]{1,0:T(8,128)(2,1)S(1)} %get-tuple-element.31), channel_id=1, source_target_pairs={{0,1},{1,0},{2,3},{3,2},{4,5},{5,4},{6,7},{7,6},{8,9},{9,8},{10,11... | collective-permute-start | bytes 184328 | tf_op jit(solution)/shard_map/ppermute | solution.py:293
  20.2 6.4 %collective-permute-start.4 = (bf16[40,768]{1,0:T(8,128)(2,1)S(1)}, bf16[40,768]{1,0:T(8,128)(2,1)S(1)}, u32[]{:S(2)}, u32[]{:S(2)}) collective-permute-start(bf16[40,768]{1,0:T(8,128)(2,1)S(1)} %get-tuple-element.32), channel_id=1, source_target_pairs={{0,2},{1,3},{2,0},{3,1},{4,6},{5,7},{6,4},{7,5},{8,10},{9,11},{10,... | collective-permute-start | bytes 184328 | tf_op jit(solution)/shard_map/ppermute | solution.py:293
  22.8 6.0 %collective-permute-start.5 = (bf16[40,768]{1,0:T(8,128)(2,1)S(1)}, bf16[40,768]{1,0:T(8,128)(2,1)S(1)}, u32[]{:S(2)}, u32[]{:S(2)}) collective-permute-start(bf16[40,768]{1,0:T(8,128)(2,1)S(1)} %get-tuple-element.33), channel_id=1, source_target_pairs={{0,3},{1,2},{2,1},{3,0},{4,7},{5,6},{6,5},{7,4},{8,11},{9,10},{10,... | collective-permute-start | bytes 184328 | tf_op jit(solution)/shard_map/ppermute | solution.py:293
  29.6 4.4 %collective-permute-start.6 = (f32[24,128]{1,0:T(8,128)S(1)}, f32[24,128]{1,0:T(8,128)S(1)}, u32[]{:S(2)}, u32[]{:S(2)}) collective-permute-start(f32[24,128]{1,0:T(8,128)S(1)} %get-tuple-element.36), channel_id=1, source_target_pairs={{0,1},{1,0},{2,3},{3,2},{4,5},{5,4},{6,7},{7,6},{8,9},{9,8},{10,11... | collective-permute-start | bytes 36872 | tf_op jit(solution)/shard_map/ppermute | solution.py:293
  29.6 4.6 %collective-permute-start.7 = (f32[24,128]{1,0:T(8,128)S(1)}, f32[24,128]{1,0:T(8,128)S(1)}, u32[]{:S(2)}, u32[]{:S(2)}) collective-permute-start(f32[24,128]{1,0:T(8,128)S(1)} %get-tuple-element.37), channel_id=1, source_target_pairs={{0,2},{1,3},{2,0},{3,1},{4,6},{5,7},{6,4},{7,5},{8,10},{9,11},{10,... | collective-permute-start | bytes 36872 | tf_op jit(solution)/shard_map/ppermute | solution.py:293
  30.9 5.5 %collective-permute-start.8 = (f32[24,128]{1,0:T(8,128)S(1)}, f32[24,128]{1,0:T(8,128)S(1)}, u32[]{:S(2)}, u32[]{:S(2)}) collective-permute-start(f32[24,128]{1,0:T(8,128)S(1)} %get-tuple-element.38), channel_id=1, source_target_pairs={{0,3},{1,2},{2,1},{3,0},{4,7},{5,6},{6,5},{7,4},{8,11},{9,10},{10,... | collective-permute-start | bytes 36872 | tf_op jit(solution)/shard_map/ppermute | solution.py:293
  36.4 1.2 %collective-permute-start.9 = (f32[16,128]{1,0:T(8,128)S(1)}, f32[16,128]{1,0:T(8,128)S(1)}, u32[]{:S(2)}, u32[]{:S(2)}) collective-permute-start(f32[16,128]{1,0:T(8,128)S(1)} %get-tuple-element.40), channel_id=1, source_target_pairs={{0,16},{16,0},{1,17},{17,1},{2,18},{18,2},{3,19},{19,3},{4,20},{20... | collective-permute-start | bytes 24584 | tf_op jit(solution)/shard_map/ppermute | solution.py:293

commit v2 on v1

--- a/solution.py
+++ b/solution.py
@@ -24,25 +24,38 @@
 VMEM_LIMIT = 24 * 1024 * 1024
 
 
-def call(kernel, outs, n_in, smem=(), hbm=(), scratch=(), cost=0):
-    spaces = [
-        pltpu.SMEM if i in smem else pl.ANY if i in hbm else pltpu.VMEM for i in range(n_in)
-    ]
-    many = isinstance(outs, (list, tuple))
-    vmem = pl.BlockSpec(memory_space=pltpu.VMEM)
-    return pl.pallas_call(
+def call(kernel, outs, ins, scratch=(), cost=0):
+    spaces = {"v": pltpu.VMEM, "s": pltpu.SMEM, "h": pltpu.HBM}
+    run = pl.pallas_call(
         kernel,
-        out_shape=outs,
-        in_specs=[pl.BlockSpec(memory_space=s) for s in spaces],
-        out_specs=[vmem] * len(outs) if many else vmem,
+        out_shape=[o[0] for o in outs],
+        in_specs=[pl.BlockSpec(memory_space=spaces[i]) for i in ins],
+        out_specs=[pl.BlockSpec(memory_space=spaces[o[1]]) for o in outs],
         scratch_shapes=list(scratch),
         compiler_params=pltpu.CompilerParams(vmem_limit_bytes=VMEM_LIMIT),
         cost_estimate=pl.CostEstimate(flops=cost, bytes_accessed=cost // 64, transcendentals=0),
     )
 
-
-def shape(dims, dtype=F32):
-    return jax.ShapeDtypeStruct(dims, dtype)
+    def placed(*operands):
+        return run(
+            *(
+                pltpu.with_memory_space_constraint(x, pltpu.HBM) if i == "h" else x
+                for i, x in zip(ins, operands, strict=True)
+            )
+        )
+
+    return placed
+
+
+def vmem(dims, dtype=F32):
+    return jax.ShapeDtypeStruct(dims, dtype), "v"
+
+
+def copies(sems, *pairs):
+    started = [pltpu.make_async_copy(src, dst, sems.at[i]) for i, (src, dst) in enumerate(pairs)]
+    for one in started:
+        one.start()
+    return started
 
 
 def rows_of(parts, dtype):
@@ -108,44 +121,58 @@
     return jnp.concatenate([gain, gain], axis=1)
 
 
-def pack_keys_kernel(blocks, lengths, keys, values, gain, packed):
+def pack_keys_kernel(blocks, lengths_at, keys_at, values_at, gain_at, packed, lengths, keys, values, gain, sems):
+    arriving = copies(sems, (lengths_at, lengths), (keys_at, keys), (gain_at, gain), (values_at, values))
     rows, width = keys.shape[1:]
-    start = prior(lengths, lax.axis_index("seq"), blocks)
-    tables = rope_tables(start, rows)
-    average, gain = averager(), twice(gain)
+    average = averager()
+    arriving[0].wait()
+    tables = rope_tables(prior(lengths, lax.axis_index("seq"), blocks), rows)
+    arriving[1].wait()
+    arriving[2].wait()
+    wide = twice(gain)
     for at in range(0, width, PAIR):
-        normed = head_norm(keys[0, :, at : at + PAIR], average, gain)
+        normed = head_norm(keys[0, :, at : at + PAIR], average, wide)
         packed[:, at : at + PAIR] = rotate(normed, *tables).astype(BF16)
+    arriving[3].wait()
     packed[:, width:] = values[0]
 
 
-def queries_kernel(blocks, order, lengths, queries, text_keys, q_gain, k_gain, stacked, text_scores, bias):
+def queries_kernel(
+    blocks, order, lengths_at, queries_at, text_keys_at, q_gain_at, k_gain_at, text_values_at, weight_at,
+    stacked, text_scores, bias, text_values, weight, lengths, queries, text_keys, q_gain, k_gain, sems,
+):
+    arriving = copies(
+        sems, (lengths_at, lengths), (queries_at, queries), (q_gain_at, q_gain), (k_gain_at, k_gain),
+        (text_keys_at, text_keys), (text_values_at, text_values), (weight_at, weight),
+    )
     rows, width = queries.shape[1:]
     rank = lax.axis_index("seq")
+    average = averager()
+    left = lax.broadcasted_iota(jnp.int32, (rows, PAIR), 1) < HEAD
+    lane = lax.broadcasted_iota(jnp.int32, bias.shape, 1)
+    live = lane < 0
+    arriving[0].wait()
+    for i, block in enumerate(order(rank)):
+        live = live | ((lane >= i * rows) & (lane < i * rows + lengths[block]))
+    bias[...] = jnp.where(live, 0.0, -jnp.inf)
     tables = rope_tables(prior(lengths, rank, blocks), rows)
-    average, q_gain, k_gain = averager(), twice(q_gain), twice(k_gain)
-    left = lax.broadcasted_iota(jnp.int32, (rows, PAIR), 1) < HEAD
+    for one in arriving[1:5]:
+        one.wait()
+    q_wide, k_wide = twice(q_gain), twice(k_gain)
     for p, at in enumerate(range(0, width, PAIR)):
-        query = rotate(head_norm(queries[0, :, at : at + PAIR], average, q_gain), *tables)
+        query = rotate(head_norm(queries[0, :, at : at + PAIR], average, q_wide), *tables)
         query = query.astype(BF16).astype(F32) * 0.125
         both = jnp.concatenate([jnp.where(left, query, 0.0), jnp.where(left, 0.0, query)], axis=0)
         both = both.astype(BF16)
         stacked[p] = both
-        key = head_norm(text_keys[0, :, at : at + PAIR], average, k_gain).astype(BF16)
+        key = head_norm(text_keys[0, :, at : at + PAIR], average, k_wide).astype(BF16)
         text_scores[p] = nt(both, key)
-    lane = lax.broadcasted_iota(jnp.int32, bias.shape, 1)
-    live = lane < 0
-    for i, block in enumerate(order(rank)):
-        live = live | ((lane >= i * rows) & (lane < i * rows + lengths[block]))
-    bias[...] = jnp.where(live, 0.0, -jnp.inf)
+    arriving[5].wait()
+    arriving[6].wait()
 
 
 def attend_kernel(n_blocks, sends, stacked, text_scores, bias, text_values, weight, *rest):
-    gathered = rest[:n_blocks]
-    attended, outs = rest[n_blocks], rest[n_blocks + 1 : -2]
-    held, sem = rest[-2:]
-    fetch = pltpu.make_async_copy(weight, held, sem)
-    fetch.start()
+    gathered, attended, outs = rest[:n_blocks], rest[n_blocks], rest[n_blocks + 1 :]
     pairs, double = stacked.shape[:2]
     rows, width = double // 2, pairs * PAIR
     if n_blocks > 1:
@@ -170,27 +197,34 @@
         parts.append(jnp.where(left, mixed[:rows], mixed[rows:]).astype(BF16))
     joined = jnp.concatenate(parts, axis=1)
     attended[...] = joined
-    fetch.wait()
-    rank = lax.axis_index("tp")
-    for out, block in zip(outs, sends(rank)):
+    project(sends, joined, weight, outs)
+
+
+def project(sends, joined, weight, outs):
+    for out, block in zip(outs, sends(lax.axis_index("tp"))):
         columns = out.shape[1]
-        out[...] = nn(joined, held[:, pl.ds(pl.multiple_of(block * columns, columns), columns)]).astype(BF16)
+        at = pl.multiple_of(block * columns, columns)
+        out[...] = nn(joined, weight[:, pl.ds(at, columns)]).astype(out.dtype)
+
+
+def project_kernel(sends, attended, weight, *outs):
+    project(sends, attended[...], weight, outs)
+
+
+def keep_kernel(value, out, sem):
+    (one,) = copies(sem, (value, out.at[0]))
+    one.wait()
 
 
 def residual_kernel(
     tp, lengths, alphas, step, attended, weight, stream, gate, shift, scale, proj, latents,
-    base, factor, mask, split, consts, coefs, held, sem,
+    base, factor, split, consts, coefs,
 ):
     rank = lax.axis_index("tp")
     rows, columns = base.shape
-    fetch = pltpu.make_async_copy(
-        weight.at[:, pl.ds(pl.multiple_of(rank * columns, columns), columns)], held, sem
-    )
-    fetch.start()
     count = lengths[lax.axis_index("seq")]
-    row = lax.broadcasted_iota(jnp.int32, mask.shape, 0)
-    mask[...] = jnp.where(row < count, 1.0, 0.0)
-    factor[...] = jnp.where(row[:, :1] < count, gate[...], 0.0)
+    alive = lax.broadcasted_iota(jnp.int32, (rows, 1), 0) < count
+    factor[...] = jnp.where(alive, gate[...], 0.0)
     channels = proj.shape[0]
     plain = proj[...]
     scaled = plain * (1.0 + scale[...])
@@ -217,19 +251,17 @@
     lane8 = lax.broadcasted_iota(jnp.int32, (8, LANES), 1)
     coefs[32:40] = jnp.where(lane8 < count, 1.0, 0.0)
     coefs[40:48] = jnp.concatenate([latents[...], jnp.zeros((8, LANES - rows), F32)], axis=1)
-    fetch.wait()
-    base[...] = jnp.where(
-        row[:, :1] < count, stream[0].astype(F32) + gate[...] * nn(attended[...], held[...]), 0.0
-    )
-
-
-def hidden_kernel(tp, base, factor, mask, split, consts, *rest):
+    own = nn(attended[...], weight[:, pl.ds(pl.multiple_of(rank * columns, columns), columns)])
+    base[...] = jnp.where(alive, stream[0].astype(F32) + gate[...] * own, 0.0)
+
+
+def hidden_kernel(tp, base, factor, split, consts, *rest):
     arrived, (hidden, *outs), scratch = rest[: tp - 1], rest[tp - 1 : -1], rest[-1]
     summed = arrived[0][...].astype(F32)
     for block in arrived[1:]:
         summed = summed + block[...].astype(F32)
     value = (base[...] + factor[...] * summed).astype(BF16)
-    hidden[0] = value
+    hidden[...] = value
     rows = value.shape[0]
     channels = consts.shape[0]
     wide = value.astype(F32)
@@ -305,10 +337,16 @@
     channels = proj_weight.shape[1]
     pairs = width // PAIR
     direct = blocks <= 4 and blocks & (blocks - 1) == 0
-
     q_gain, k_gain = q_gain.reshape(1, HEAD), k_gain.reshape(1, HEAD)
-    packed = call(
-        functools.partial(pack_keys_kernel, blocks), shape((rows, 2 * width), BF16), 4, smem=(0,), cost=2000000
+    one_gain = pltpu.VMEM(q_gain.shape, F32)
+    counts = pltpu.SMEM(lengths.shape, jnp.int32)
+
+    (packed,) = call(
+        functools.partial(pack_keys_kernel, blocks),
+        [vmem((rows, 2 * width), BF16)],
+        "hhhh",
+        [counts, pltpu.VMEM(keys.shape, BF16), pltpu.VMEM(values.shape, BF16), one_gain, pltpu.SemaphoreType.DMA((4,))],
+        cost=2000000,
     )(lengths, keys, values, k_gain)
     if direct:
         gathered = [packed] + [exchange(packed, "seq", d) for d in range(1, blocks)]
@@ -316,60 +354,62 @@
     else:
         gathered = [lax.all_gather(packed, "seq", axis=0, tiled=True)]
         order = lambda rank: range(blocks)
-    stacked, text_scores, bias = call(
+    stacked, text_scores, bias, held_values, held_weight = call(
         functools.partial(queries_kernel, blocks, order),
         [
-            shape((pairs, 2 * rows, PAIR), BF16),
-            shape((pairs, 2 * rows, text)),
-            shape((1, blocks * rows)),
+            vmem((pairs, 2 * rows, PAIR), BF16),
+            vmem((pairs, 2 * rows, text)),
+            vmem((1, blocks * rows)),
+            vmem(text_values.shape, BF16),
+            vmem(out_weight.shape, BF16),
         ],
-        5,
-        smem=(0,),
+        "hhhhhhh",
+        [
+            counts, pltpu.VMEM(queries.shape, BF16), pltpu.VMEM(text_keys.shape, BF16), one_gain, one_gain,
+            pltpu.SemaphoreType.DMA((7,)),
+        ],
         cost=20000000,
-    )(lengths, queries, text_keys, q_gain, k_gain)
-    sends = lambda rank: [rank ^ d for d in range(1, tp)]
+    )(lengths, queries, text_keys, q_gain, k_gain, text_values, out_weight)
+    partners = list(range(tp - 1, 0, -1))
     attended, *outgoing = call(
-        functools.partial(attend_kernel, len(gathered), sends),
-        [shape((rows, width), BF16)] + [shape((rows, columns), BF16)] * (tp - 1),
-        5 + len(gathered),
-        hbm=(4,),
-        scratch=[pltpu.VMEM(out_weight.shape, BF16), pltpu.SemaphoreType.DMA],
+        functools.partial(attend_kernel, len(gathered), lambda rank: [rank ^ d for d in partners]),
+        [vmem((rows, width), BF16)] + [vmem((rows, columns), BF16)] * (tp - 1),
+        "v" * (5 + len(gathered)),
         cost=100000000,
-    )(stacked, text_scores, bias, text_values, out_weight, *gathered)
-    arrived = [exchange(block, "tp", d) for d, block in enumerate(outgoing, 1)]
-    base, factor, mask, split, consts, coefs = call(
+    )(stacked, text_scores, bias, held_values, held_weight, *gathered)
+    arrived = [exchange(block, "tp", d) for d, block in zip(partners, outgoing)]
+    base, factor, split, consts, coefs = call(
         functools.partial(residual_kernel, tp),
         [
-            shape((rows, columns)),
-            shape((rows, columns)),
-            shape((rows, LANES)),
-            shape((3 * channels + 16, columns), BF16),
-            shape((channels, LANES)),
-            shape((48, LANES)),
+            vmem((rows, columns)),
+            vmem((rows, columns)),
+            vmem((3 * channels + 16, columns), BF16),
+            vmem((channels, LANES)),
+            vmem((48, LANES)),
         ],
-        11,
-        smem=(0, 1, 2),
-        hbm=(4,),
-        scratch=[pltpu.VMEM((width, columns), BF16), pltpu.SemaphoreType.DMA],
+        "sss" + "v" * 8,
         cost=100000000,
     )(
-        lengths, alphas, step_index, attended, out_weight, stream, gate.reshape(1, columns),
+        lengths, alphas, step_index, attended, held_weight, stream, gate.reshape(1, columns),
         shift.reshape(1, columns), scale.reshape(1, columns), proj_weight.T, latents.T,
     )
     hidden, *partials = call(
         functools.partial(hidden_kernel, tp),
-        [shape((1, rows, columns), BF16)] + [shape((24, LANES))] * tp,
-        5 + tp - 1,
-        scratch=[pltpu.VMEM((channels, LANES), F32)],
+        [vmem((rows, columns), BF16)] + [vmem((24, LANES))] * tp,
+        "v" * (4 + tp - 1),
+        [pltpu.VMEM((channels, LANES), F32)],
         cost=20000000,
-    )(base, factor, mask, split, consts, *arrived)
-    shares = [exchange(block, "tp", d) for d, block in enumerate(partials) if d]
-    mine, other = call(total_kernel, [shape((16, LANES))] * 2, tp)(partials[0], *shares)
+    )(base, factor, split, consts, *arrived)
+    shares = [exchange(partials[d], "tp", d) for d in partners]
+    (hidden_out,) = call(
+        keep_kernel, [(jax.ShapeDtypeStruct(stream.shape, BF16), "h")], "v", [pltpu.SemaphoreType.DMA((1,))], cost=2000000
+    )(hidden)
+    mine, other = call(total_kernel, [vmem((16, LANES))] * 2, "v" * tp)(partials[0], *shares)
     theirs = exchange(other, "cfg", 1)
-    latents_out = call(
-        functools.partial(step_kernel, columns * tp), shape((latents.shape[1], rows)), 3
+    (latents_out,) = call(
+        functools.partial(step_kernel, columns * tp), [vmem((latents.shape[1], rows))], "vvv"
     )(mine, theirs, coefs)
-    return hidden, latents_out.T
+    return hidden_out, latents_out.T
 
 
 def solution(mesh):

time: 38.7 us -> 30.2 us (0.78)
  local copies, waits for them, and re-layouts: 8.46 us -> 0.05 us
  Pallas kernels: 6.92 us -> 7.55 us
  waiting for transfers between devices: 7.79 us -> 7.35 us
    unnamed x36 -> x16, local copies, waits for them, and re-layouts: 8.44 us -> 0.04 us
    pallas_call x7 -> x8, Pallas kernels: 6.92 us -> 7.55 us  [placed(): run(*(pltpu.with_memory_space_constraint(x, pltpu.HBM) if i == 'h' else x...]
    ppermute x10, waiting for transfers between devices: 7.79 us -> 7.35 us  [exchange(): lax.ppermute(value, axis, [(i, i ^ distance) for i in range(lax.axis_size...]
  transfers between devices with their start and end apart: 10 -> 10, of which waited for: 5 -> 6; matrix products, arithmetic and copies ran while one was open for 0% -> 0% of each run, Pallas kernels for 8% -> 14%
where the time goes in v2:
time: 30.2 us; the launch traced here: 29.9 us
  starting transfers between devices  13.5 us (45%)
  Pallas kernels  7.55 us (25%)
  waiting for transfers between devices  7.35 us (24%)
  between operations  1.46 us (5%)
    ppermute x10, starting transfers between devices, exchange(): lax.ppermute(value, axis, [(i, i ^ distance) for i in range(lax.axis_size...  13.5 us
    pallas_call x8, Pallas kernels, placed(): run(*(pltpu.with_memory_space_constraint(x, pltpu.HBM) if i == 'h' else x...  7.55 us
    ppermute x10, waiting for transfers between devices, exchange(): lax.ppermute(value, axis, [(i, i ^ distance) for i in range(lax.axis_size...  7.35 us
  transfers between devices with their start and end apart: 10, of which 6 were waited for; matrix products, arithmetic and copies ran while one was open for 0% of the time, Pallas kernels for 14%

profile of v2, /device:TPU:0, one launch (start us, length us, event | category | flops | bytes accessed | tf_op | source)
XLA Modules:
  0.0 29.9 jit_solution(17104767624085248003)
XLA Ops:
  0.6 1.5 %shard_map.177.rest_0_ = bf16[40,768]{1,0:T(8,128)(2,1)S(1)} custom-call(s32[4]{0:T(128)} %lengths.1, bf16[1,40,384]{2,1,0:T(8,128)(2,1)} %keys_at.1, bf16[1,40,384]{2,1,0:T(8,128)(2,1)} %values_at.1, f32[1,64]{1,0:T(1,128)} %bitcast.8), custom_call_target="tpu_custom_call" | custom-call | flops 2000000 | bytes 31250 | tf_op jit(solution)/shard_map/pallas_call | solution.py:40
  2.1 3.0 %collective-permute-start = (bf16[40,768]{1,0:T(8,128)(2,1)S(1)}, bf16[40,768]{1,0:T(8,128)(2,1)S(1)}, u32[]{:S(2)}, u32[]{:S(2)}) collective-permute-start(bf16[40,768]{1,0:T(8,128)(2,1)S(1)} %shard_map.177.rest_0_), channel_id=1, source_target_pairs={{0,4},{4,0},{8,12},{12,8},{1,5},{5,1},{9,13},{13,9},{2,6},{6,2},{1... | collective-permute-start | bytes 184328 | tf_op jit(solution)/shard_map/ppermute | solution.py:325
  5.1 1.5 %collective-permute-start.1 = (bf16[40,768]{1,0:T(8,128)(2,1)S(1)}, bf16[40,768]{1,0:T(8,128)(2,1)S(1)}, u32[]{:S(2)}, u32[]{:S(2)}) collective-permute-start(bf16[40,768]{1,0:T(8,128)(2,1)S(1)} %shard_map.177.rest_0_), channel_id=1, source_target_pairs={{0,8},{4,12},{8,0},{12,4},{1,9},{5,13},{9,1},{13,5},{2,10},{6,14},... | collective-permute-start | bytes 184328 | tf_op jit(solution)/shard_map/ppermute | solution.py:325
  6.6 0.0 collective-permute-start.2
  6.7 0.0 copy-start.5
  6.7 0.0 copy-start.6
  6.7 0.0 copy-start.7
  6.7 0.0 copy-start
  6.7 0.0 copy-start.1
  6.7 0.0 copy-start.2
  6.7 0.0 copy-start.3
  6.7 0.0 copy-start.4
  6.7 2.7 %shard_map.176 = (bf16[3,80,128]{2,1,0:T(8,128)(2,1)S(1)}, f32[3,80,226]{2,1,0:T(8,128)S(1)}, f32[1,160]{1,0:T(1,128)S(1)}, bf16[1,226,384]{2,1,0:T(8,128)(2,1)S(1)}, bf16[384,3072]{1,0:T(8,128)(2,1)S(1)}) custom-call(s32[4]{0:T(128)} %lengths.1, bf16[1,40,384]{2,1,0:T(8,128)(2,1)} %queries_at.1, bf16[1,226,384]{2,1,0:T(8,128)(2,1)} %text_keys_at.1, ...), custom_call_target="tpu_custom_call" | custom-call | flops 20000000 | bytes 312500 | tf_op jit(solution)/shard_map/pallas_call | solution.py:40
  9.4 0.0 collective-permute-done.rest_1_
  9.5 0.0 collective-permute-done.1.rest_2_
  9.5 2.3 %collective-permute-done.2.rest_3_ = bf16[40,768]{1,0:T(8,128)(2,1)S(1)} collective-permute-done((bf16[40,768]{1,0:T(8,128)(2,1)S(1)}, bf16[40,768]{1,0:T(8,128)(2,1)S(1)}, u32[]{:S(2)}, u32[]{:S(2)}) %collective-permute-start.2) | collective-permute-done | bytes 61472 | tf_op jit(solution)/shard_map/ppermute | solution.py:325
  11.8 0.9 %shard_map.178 = (bf16[40,384]{1,0:T(8,128)(2,1)S(1)}, bf16[40,768]{1,0:T(8,128)(2,1)S(1)}, bf16[40,768]{1,0:T(8,128)(2,1)S(1)}, bf16[40,768]{1,0:T(8,128)(2,1)S(1)}) custom-call(bf16[3,80,128]{2,1,0:T(8,128)(2,1)S(1)} %get-tuple-element.23.stacked, f32[3,80,226]{2,1,0:T(8,128)S(1)} %get-tuple-element.24.text_scores, f32[1,160]{1,0:T(1,128)S(1)} %get-tuple-element.25.bias, ...), custom_call_target="tpu_custom_call" | custom-call | flops 100000000 | bytes 1562500 | tf_op jit(solution)/shard_map/pallas_call | solution.py:40
  12.7 3.7 %collective-permute-start.3 = (bf16[40,768]{1,0:T(8,128)(2,1)S(1)}, bf16[40,768]{1,0:T(8,128)(2,1)S(1)}, u32[]{:S(2)}, u32[]{:S(2)}) collective-permute-start(bf16[40,768]{1,0:T(8,128)(2,1)S(1)} %get-tuple-element.33), channel_id=1, source_target_pairs={{0,3},{1,2},{2,1},{3,0},{4,7},{5,6},{6,5},{7,4},{8,11},{9,10},{10,... | collective-permute-start | bytes 184328 | tf_op jit(solution)/shard_map/ppermute | solution.py:325
  16.3 0.0 collective-permute-start.4
  16.3 0.8 %collective-permute-start.5 = (bf16[40,768]{1,0:T(8,128)(2,1)S(1)}, bf16[40,768]{1,0:T(8,128)(2,1)S(1)}, u32[]{:S(2)}, u32[]{:S(2)}) collective-permute-start(bf16[40,768]{1,0:T(8,128)(2,1)S(1)} %get-tuple-element.35), channel_id=1, source_target_pairs={{0,1},{1,0},{2,3},{3,2},{4,5},{5,4},{6,7},{7,6},{8,9},{9,8},{10,11... | collective-permute-start | bytes 184328 | tf_op jit(solution)/shard_map/ppermute | solution.py:325
  17.1 0.0 copy-done.5
  17.1 0.0 copy-done.6
  17.1 0.0 copy-done.7
  17.8 0.0 copy-done
  17.8 0.0 copy-done.1
  17.8 0.0 copy-done.2
  17.8 0.0 copy-done.3
  17.9 0.0 copy-done.4
  17.9 0.9 %shard_map.179 = (f32[40,768]{1,0:T(8,128)S(1)}, f32[40,768]{1,0:T(8,128)S(1)}, bf16[208,768]{1,0:T(8,128)(2,1)S(1)}, f32[64,128]{1,0:T(8,128)S(1)}, f32[48,128]{1,0:T(8,128)S(1)}) custom-call(s32[4]{0:T(128)S(1)} %copy-done.2, f32[1000]{0:T(1024)S(1)} %copy-done.3, s32[1]{0:T(128)S(6)} %copy.19.step, bf16[40,384]{1,0:T(8,128)(2,1)S(1)} %get-tuple-element.28.attended, ...), custom_call_target="tpu_custom_call" | custom-call | flops 100000000 | bytes 1562500 | tf_op jit(solution)/shard_map/pallas_call | solution.py:40
  18.7 0.1 collective-permute-done.3.rest_0_
  18.9 2.6 %collective-permute-done.4.rest_1_ = bf16[40,768]{1,0:T(8,128)(2,1)S(1)} collective-permute-done((bf16[40,768]{1,0:T(8,128)(2,1)S(1)}, bf16[40,768]{1,0:T(8,128)(2,1)S(1)}, u32[]{:S(2)}, u32[]{:S(2)}) %collective-permute-start.4) | collective-permute-done | bytes 61472 | tf_op jit(solution)/shard_map/ppermute | solution.py:325
  21.5 0.0 collective-permute-done.5.rest_2_
  21.5 0.3 shard_map.180
  21.8 1.6 %collective-permute-start.6 = (f32[24,128]{1,0:T(8,128)S(1)}, f32[24,128]{1,0:T(8,128)S(1)}, u32[]{:S(2)}, u32[]{:S(2)}) collective-permute-start(f32[24,128]{1,0:T(8,128)S(1)} %get-tuple-element.38), channel_id=1, source_target_pairs={{0,3},{1,2},{2,1},{3,0},{4,7},{5,6},{6,5},{7,4},{8,11},{9,10},{10,... | collective-permute-start | bytes 36872 | tf_op jit(solution)/shard_map/ppermute | solution.py:325
  23.4 0.5 %collective-permute-start.7 = (f32[24,128]{1,0:T(8,128)S(1)}, f32[24,128]{1,0:T(8,128)S(1)}, u32[]{:S(2)}, u32[]{:S(2)}) collective-permute-start(f32[24,128]{1,0:T(8,128)S(1)} %get-tuple-element.39), channel_id=1, source_target_pairs={{0,2},{1,3},{2,0},{3,1},{4,6},{5,7},{6,4},{7,5},{8,10},{9,11},{10,... | collective-permute-start | bytes 36872 | tf_op jit(solution)/shard_map/ppermute | solution.py:325
  23.9 2.3 %collective-permute-start.8 = (f32[24,128]{1,0:T(8,128)S(1)}, f32[24,128]{1,0:T(8,128)S(1)}, u32[]{:S(2)}, u32[]{:S(2)}) collective-permute-start(f32[24,128]{1,0:T(8,128)S(1)} %get-tuple-element.40), channel_id=1, source_target_pairs={{0,1},{1,0},{2,3},{3,2},{4,5},{5,4},{6,7},{7,6},{8,9},{9,8},{10,11... | collective-permute-start | bytes 36872 | tf_op jit(solution)/shard_map/ppermute | solution.py:325
  26.2 1.1 %collective-permute-done.6.rest_0_ = f32[24,128]{1,0:T(8,128)S(1)} collective-permute-done((f32[24,128]{1,0:T(8,128)S(1)}, f32[24,128]{1,0:T(8,128)S(1)}, u32[]{:S(2)}, u32[]{:S(2)}) %collective-permute-start.6) | collective-permute-done | bytes 12320 | tf_op jit(solution)/shard_map/ppermute | solution.py:325
  27.3 0.7 %collective-permute-done.7.rest_1_ = f32[24,128]{1,0:T(8,128)S(1)} collective-permute-done((f32[24,128]{1,0:T(8,128)S(1)}, f32[24,128]{1,0:T(8,128)S(1)}, u32[]{:S(2)}, u32[]{:S(2)}) %collective-permute-start.7) | collective-permute-done | bytes 12320 | tf_op jit(solution)/shard_map/ppermute | solution.py:325
  28.0 0.0 collective-permute-done.8.rest_2_
  28.0 0.1 collective-permute-start.9
  28.1 0.6 %shard_map.181 = bf16[1,40,768]{2,1,0:T(8,128)(2,1)} custom-call(bf16[40,768]{1,0:T(8,128)(2,1)S(1)} %get-tuple-element.36.value), custom_call_target="tpu_custom_call" | custom-call | flops 2000000 | bytes 31250 | tf_op jit(solution)/shard_map/pallas_call | solution.py:40
  28.7 0.5 %collective-permute-done.9.theirs = f32[16,128]{1,0:T(8,128)S(1)} collective-permute-done((f32[16,128]{1,0:T(8,128)S(1)}, f32[16,128]{1,0:T(8,128)S(1)}, u32[]{:S(2)}, u32[]{:S(2)}) %collective-permute-start.9) | collective-permute-done | bytes 8224 | tf_op jit(solution)/shard_map/ppermute | solution.py:325
  29.3 0.7 %shard_map.183 = f32[8,40]{1,0:T(8,128)} custom-call(f32[16,128]{1,0:T(8,128)S(1)} %get-tuple-element.41.mine, f32[16,128]{1,0:T(8,128)S(1)} %collective-permute-done.9.theirs, f32[48,128]{1,0:T(8,128)S(1)} %get-tuple-element.43.coefs), custom_call_target="tpu_custom_call" | custom-call | tf_op jit(solution)/shard_map/pallas_call | solution.py:40
  (4 shorter events, 0.0 us)
Async XLA Ops:
  2.1 7.3 %collective-permute-start = (bf16[40,768]{1,0:T(8,128)(2,1)S(1)}, bf16[40,768]{1,0:T(8,128)(2,1)S(1)}, u32[]{:S(2)}, u32[]{:S(2)}) collective-permute-start(bf16[40,768]{1,0:T(8,128)(2,1)S(1)} %shard_map.177.rest_0_), channel_id=1, source_target_pairs={{0,4},{4,0},{8,12},{12,8},{1,5},{5,1},{9,13},{13,9},{2,6},{6,2},{1... | collective-permute-start | bytes 184328 | tf_op jit(solution)/shard_map/ppermute | solution.py:325
  5.1 4.3 %collective-permute-start.1 = (bf16[40,768]{1,0:T(8,128)(2,1)S(1)}, bf16[40,768]{1,0:T(8,128)(2,1)S(1)}, u32[]{:S(2)}, u32[]{:S(2)}) collective-permute-start(bf16[40,768]{1,0:T(8,128)(2,1)S(1)} %shard_map.177.rest_0_), channel_id=1, source_target_pairs={{0,8},{4,12},{8,0},{12,4},{1,9},{5,13},{9,1},{13,5},{2,10},{6,14},... | collective-permute-start | bytes 184328 | tf_op jit(solution)/shard_map/ppermute | solution.py:325
  6.6 5.1 %collective-permute-start.2 = (bf16[40,768]{1,0:T(8,128)(2,1)S(1)}, bf16[40,768]{1,0:T(8,128)(2,1)S(1)}, u32[]{:S(2)}, u32[]{:S(2)}) collective-permute-start(bf16[40,768]{1,0:T(8,128)(2,1)S(1)} %shard_map.177.rest_0_), channel_id=1, source_target_pairs={{0,12},{4,8},{8,4},{12,0},{1,13},{5,9},{9,5},{13,1},{2,14},{6,10},... | collective-permute-start | bytes 184328 | tf_op jit(solution)/shard_map/ppermute | solution.py:325
  6.7 10.5 %copy-start.5 = (f32[768]{0:T(1024)S(1)}, f32[768]{0:T(1024)}, u32[]{:S(2)}) copy-start(f32[768]{0:T(1024)} %param.24) | copy-start | bytes 9220
  6.7 10.5 %copy-start.6 = (f32[768]{0:T(1024)S(1)}, f32[768]{0:T(1024)}, u32[]{:S(2)}) copy-start(f32[768]{0:T(1024)} %param.25) | copy-start | bytes 9220
  6.7 10.5 %copy-start.7 = (f32[768]{0:T(1024)S(1)}, f32[768]{0:T(1024)}, u32[]{:S(2)}) copy-start(f32[768]{0:T(1024)} %param.26) | copy-start | bytes 9220
  6.7 11.2 %copy-start = (f32[768,64]{0,1:T(8,128)S(1)}, f32[768,64]{0,1:T(8,128)}, u32[]{:S(2)}) copy-start(f32[768,64]{0,1:T(8,128)} %param.27) | copy-start | bytes 589828
  6.7 11.2 %copy-start.1 = (bf16[1,40,768]{2,1,0:T(8,128)(2,1)S(1)}, bf16[1,40,768]{2,1,0:T(8,128)(2,1)}, u32[]{:S(2)}) copy-start(bf16[1,40,768]{2,1,0:T(8,128)(2,1)} %stream.1) | copy-start | bytes 184324
  6.7 11.2 %copy-start.2 = (s32[4]{0:T(128)S(1)}, s32[4]{0:T(128)}, u32[]{:S(2)}) copy-start(s32[4]{0:T(128)} %lengths.1) | copy-start | bytes 52
  6.7 11.2 %copy-start.3 = (f32[1000]{0:T(1024)S(1)}, f32[1000]{0:T(1024)}, u32[]{:S(2)}) copy-start(f32[1000]{0:T(1024)} %alphas.1) | copy-start | bytes 12004
  6.7 11.2 %copy-start.4 = (f32[40,8]{0,1:T(8,128)S(1)}, f32[40,8]{0,1:T(8,128)}, u32[]{:S(2)}) copy-start(f32[40,8]{0,1:T(8,128)} %param.31) | copy-start | bytes 3844
  12.7 6.2 %collective-permute-start.3 = (bf16[40,768]{1,0:T(8,128)(2,1)S(1)}, bf16[40,768]{1,0:T(8,128)(2,1)S(1)}, u32[]{:S(2)}, u32[]{:S(2)}) collective-permute-start(bf16[40,768]{1,0:T(8,128)(2,1)S(1)} %get-tuple-element.33), channel_id=1, source_target_pairs={{0,3},{1,2},{2,1},{3,0},{4,7},{5,6},{6,5},{7,4},{8,11},{9,10},{10,... | collective-permute-start | bytes 184328 | tf_op jit(solution)/shard_map/ppermute | solution.py:325
  16.3 5.1 %collective-permute-start.4 = (bf16[40,768]{1,0:T(8,128)(2,1)S(1)}, bf16[40,768]{1,0:T(8,128)(2,1)S(1)}, u32[]{:S(2)}, u32[]{:S(2)}) collective-permute-start(bf16[40,768]{1,0:T(8,128)(2,1)S(1)} %get-tuple-element.34), channel_id=1, source_target_pairs={{0,2},{1,3},{2,0},{3,1},{4,6},{5,7},{6,4},{7,5},{8,10},{9,11},{10,... | collective-permute-start | bytes 184328 | tf_op jit(solution)/shard_map/ppermute | solution.py:325
  16.3 5.1 %collective-permute-start.5 = (bf16[40,768]{1,0:T(8,128)(2,1)S(1)}, bf16[40,768]{1,0:T(8,128)(2,1)S(1)}, u32[]{:S(2)}, u32[]{:S(2)}) collective-permute-start(bf16[40,768]{1,0:T(8,128)(2,1)S(1)} %get-tuple-element.35), channel_id=1, source_target_pairs={{0,1},{1,0},{2,3},{3,2},{4,5},{5,4},{6,7},{7,6},{8,9},{9,8},{10,11... | collective-permute-start | bytes 184328 | tf_op jit(solution)/shard_map/ppermute | solution.py:325
  21.8 5.6 %collective-permute-start.6 = (f32[24,128]{1,0:T(8,128)S(1)}, f32[24,128]{1,0:T(8,128)S(1)}, u32[]{:S(2)}, u32[]{:S(2)}) collective-permute-start(f32[24,128]{1,0:T(8,128)S(1)} %get-tuple-element.38), channel_id=1, source_target_pairs={{0,3},{1,2},{2,1},{3,0},{4,7},{5,6},{6,5},{7,4},{8,11},{9,10},{10,... | collective-permute-start | bytes 36872 | tf_op jit(solution)/shard_map/ppermute | solution.py:325
  23.4 4.6 %collective-permute-start.7 = (f32[24,128]{1,0:T(8,128)S(1)}, f32[24,128]{1,0:T(8,128)S(1)}, u32[]{:S(2)}, u32[]{:S(2)}) collective-permute-start(f32[24,128]{1,0:T(8,128)S(1)} %get-tuple-element.39), channel_id=1, source_target_pairs={{0,2},{1,3},{2,0},{3,1},{4,6},{5,7},{6,4},{7,5},{8,10},{9,11},{10,... | collective-permute-start | bytes 36872 | tf_op jit(solution)/shard_map/ppermute | solution.py:325
  23.9 4.1 %collective-permute-start.8 = (f32[24,128]{1,0:T(8,128)S(1)}, f32[24,128]{1,0:T(8,128)S(1)}, u32[]{:S(2)}, u32[]{:S(2)}) collective-permute-start(f32[24,128]{1,0:T(8,128)S(1)} %get-tuple-element.40), channel_id=1, source_target_pairs={{0,1},{1,0},{2,3},{3,2},{4,5},{5,4},{6,7},{7,6},{8,9},{9,8},{10,11... | collective-permute-start | bytes 36872 | tf_op jit(solution)/shard_map/ppermute | solution.py:325
  28.0 1.2 %collective-permute-start.9 = (f32[16,128]{1,0:T(8,128)S(1)}, f32[16,128]{1,0:T(8,128)S(1)}, u32[]{:S(2)}, u32[]{:S(2)}) collective-permute-start(f32[16,128]{1,0:T(8,128)S(1)} %get-tuple-element.42), channel_id=1, source_target_pairs={{0,16},{16,0},{1,17},{17,1},{2,18},{18,2},{3,19},{19,3},{4,20},{20... | collective-permute-start | bytes 24584 | tf_op jit(solution)/shard_map/ppermute | solution.py:325

commit v3 on v2

--- a/solution.py
+++ b/solution.py
@@ -255,7 +255,7 @@
     base[...] = jnp.where(alive, stream[0].astype(F32) + gate[...] * own, 0.0)
 
 
-def hidden_kernel(tp, base, factor, split, consts, *rest):
+def hidden_kernel(tp, routes, base, factor, split, consts, *rest):
     arrived, (hidden, *outs), scratch = rest[: tp - 1], rest[tp - 1 : -1], rest[-1]
     summed = arrived[0][...].astype(F32)
     for block in arrived[1:]:
@@ -279,7 +279,7 @@
     stats = jnp.concatenate([jnp.where(row == 0, total, squares), blank[:8]], axis=1)
     rank = lax.axis_index("tp")
     for i, out in enumerate(outs):
-        block = rank ^ i
+        block = entry(routes[i], rank)
         for half in range(2):
             out[8 * half : 8 * half + 8] = scratch[pl.ds(pl.multiple_of((half * tp + block) * 8, 8), 8)]
         out[16:24] = stats
@@ -323,6 +323,17 @@
 
 def exchange(value, axis, distance):
     return lax.ppermute(value, axis, [(i, i ^ distance) for i in range(lax.axis_size(axis))])
+
+
+def send(value, axis, route):
+    return lax.ppermute(value, axis, list(enumerate(route)))
+
+
+def entry(route, rank):
+    place = jnp.int32(route[0])
+    for i, to in enumerate(route[1:], 1):
+        place = jnp.where(rank == i, to, place)
+    return place
 
 
 def shards(
@@ -349,8 +360,8 @@
         cost=2000000,
     )(lengths, keys, values, k_gain)
     if direct:
-        gathered = [packed] + [exchange(packed, "seq", d) for d in range(1, blocks)]
-        order = lambda rank: [rank ^ d for d in range(blocks)]
+        gathered = [packed] + [exchange(packed, "seq", d) for d in (3, 2, 1)]
+        order = lambda rank: [rank] + [rank ^ d for d in (3, 2, 1)]
     else:
         gathered = [lax.all_gather(packed, "seq", axis=0, tiled=True)]
         order = lambda rank: range(blocks)
@@ -370,14 +381,15 @@
         ],
         cost=20000000,
     )(lengths, queries, text_keys, q_gain, k_gain, text_values, out_weight)
-    partners = list(range(tp - 1, 0, -1))
+    routes = [[i ^ d for i in range(tp)] for d in range(tp - 1, 0, -1)]
+    late_routes = routes
     attended, *outgoing = call(
-        functools.partial(attend_kernel, len(gathered), lambda rank: [rank ^ d for d in partners]),
+        functools.partial(attend_kernel, len(gathered), lambda rank: [entry(r, rank) for r in routes]),
         [vmem((rows, width), BF16)] + [vmem((rows, columns), BF16)] * (tp - 1),
         "v" * (5 + len(gathered)),
         cost=100000000,
     )(stacked, text_scores, bias, held_values, held_weight, *gathered)
-    arrived = [exchange(block, "tp", d) for d, block in zip(partners, outgoing)]
+    arrived = [send(block, "tp", r) for r, block in zip(routes, outgoing)]
     base, factor, split, consts, coefs = call(
         functools.partial(residual_kernel, tp),
         [
@@ -394,13 +406,13 @@
         shift.reshape(1, columns), scale.reshape(1, columns), proj_weight.T, latents.T,
     )
     hidden, *partials = call(
-        functools.partial(hidden_kernel, tp),
+        functools.partial(hidden_kernel, tp, [list(range(tp))] + late_routes),
         [vmem((rows, columns), BF16)] + [vmem((24, LANES))] * tp,
         "v" * (4 + tp - 1),
         [pltpu.VMEM((channels, LANES), F32)],
         cost=20000000,
     )(base, factor, split, consts, *arrived)
-    shares = [exchange(partials[d], "tp", d) for d in partners]
+    shares = [send(block, "tp", r) for r, block in zip(late_routes, partials[1:])]
     (hidden_out,) = call(
         keep_kernel, [(jax.ShapeDtypeStruct(stream.shape, BF16), "h")], "v", [pltpu.SemaphoreType.DMA((1,))], cost=2000000
     )(hidden)

time: 30.2 us -> 29.3 us (0.970)
  waiting for transfers between devices: 7.35 us -> 6.45 us
    ppermute x0 -> x6, starting transfers between devices: none -> 8.91 us  [send(): return lax.ppermute(value, axis, list(enumerate(route)))]
    ppermute x10 -> x4, starting transfers between devices: 13.5 us -> 4.67 us  [exchange(): lax.ppermute(value, axis, [(i, i ^ distance) for i in range(lax.axis_size...]
    ppermute x10 -> x4, waiting for transfers between devices: 7.35 us -> 1.81 us  [exchange(): lax.ppermute(value, axis, [(i, i ^ distance) for i in range(lax.axis_size...]
    ppermute x0 -> x6, waiting for transfers between devices: none -> 4.64 us  [send(): return lax.ppermute(value, axis, list(enumerate(route)))]
where the time goes in v3:
time: 29.3 us; the launch traced here: 29.1 us
  starting transfers between devices  13.6 us (46%)
  Pallas kernels  7.55 us (26%)
  waiting for transfers between devices  6.45 us (22%)
  between operations  1.45 us (5%)
    ppermute x6, starting transfers between devices, send(): return lax.ppermute(value, axis, list(enumerate(route)))  8.91 us
    pallas_call x8, Pallas kernels, placed(): run(*(pltpu.with_memory_space_constraint(x, pltpu.HBM) if i == 'h' else x...  7.55 us
    ppermute x4, starting transfers between devices, exchange(): lax.ppermute(value, axis, [(i, i ^ distance) for i in range(lax.axis_size...  4.67 us
    ppermute x6, waiting for transfers between devices, send(): return lax.ppermute(value, axis, list(enumerate(route)))  4.64 us
    ppermute x4, waiting for transfers between devices, exchange(): lax.ppermute(value, axis, [(i, i ^ distance) for i in range(lax.axis_size...  1.81 us
  transfers between devices with their start and end apart: 10, of which 6 were waited for; matrix products, arithmetic and copies ran while one was open for 0% of the time, Pallas kernels for 14%

profile of v3, /device:TPU:0, one launch (start us, length us, event | category | flops | bytes accessed | tf_op | source)
XLA Modules:
  0.0 29.1 jit_solution(3457297153013922212)
XLA Ops:
  0.6 1.5 %shard_map.177.rest_0_ = bf16[40,768]{1,0:T(8,128)(2,1)S(1)} custom-call(s32[4]{0:T(128)} %lengths.1, bf16[1,40,384]{2,1,0:T(8,128)(2,1)} %keys_at.1, bf16[1,40,384]{2,1,0:T(8,128)(2,1)} %values_at.1, f32[1,64]{1,0:T(1,128)} %bitcast.8), custom_call_target="tpu_custom_call" | custom-call | flops 2000000 | bytes 31250 | tf_op jit(solution)/shard_map/pallas_call | solution.py:40
  2.1 4.0 %collective-permute-start = (bf16[40,768]{1,0:T(8,128)(2,1)S(1)}, bf16[40,768]{1,0:T(8,128)(2,1)S(1)}, u32[]{:S(2)}, u32[]{:S(2)}) collective-permute-start(bf16[40,768]{1,0:T(8,128)(2,1)S(1)} %shard_map.177.rest_0_), channel_id=1, source_target_pairs={{0,12},{4,8},{8,4},{12,0},{1,13},{5,9},{9,5},{13,1},{2,14},{6,10},... | collective-permute-start | bytes 184328 | tf_op jit(solution)/shard_map/ppermute | solution.py:325
  6.1 0.5 %collective-permute-start.1 = (bf16[40,768]{1,0:T(8,128)(2,1)S(1)}, bf16[40,768]{1,0:T(8,128)(2,1)S(1)}, u32[]{:S(2)}, u32[]{:S(2)}) collective-permute-start(bf16[40,768]{1,0:T(8,128)(2,1)S(1)} %shard_map.177.rest_0_), channel_id=1, source_target_pairs={{0,8},{4,12},{8,0},{12,4},{1,9},{5,13},{9,1},{13,5},{2,10},{6,14},... | collective-permute-start | bytes 184328 | tf_op jit(solution)/shard_map/ppermute | solution.py:325
  6.6 0.1 collective-permute-start.2
  6.7 0.0 copy-start.5
  6.7 0.0 copy-start.6
  6.7 0.0 copy-start.7
  6.7 0.0 copy-start
  6.7 0.0 copy-start.1
  6.7 0.0 copy-start.2
  6.8 0.0 copy-start.3
  6.8 0.0 copy-start.4
  6.8 2.7 %shard_map.176 = (bf16[3,80,128]{2,1,0:T(8,128)(2,1)S(1)}, f32[3,80,226]{2,1,0:T(8,128)S(1)}, f32[1,160]{1,0:T(1,128)S(1)}, bf16[1,226,384]{2,1,0:T(8,128)(2,1)S(1)}, bf16[384,3072]{1,0:T(8,128)(2,1)S(1)}) custom-call(s32[4]{0:T(128)} %lengths.1, bf16[1,40,384]{2,1,0:T(8,128)(2,1)} %queries_at.1, bf16[1,226,384]{2,1,0:T(8,128)(2,1)} %text_keys_at.1, ...), custom_call_target="tpu_custom_call" | custom-call | flops 20000000 | bytes 312500 | tf_op jit(solution)/shard_map/pallas_call | solution.py:40
  9.5 0.0 collective-permute-done.rest_1_
  9.5 0.8 %collective-permute-done.1.rest_2_ = bf16[40,768]{1,0:T(8,128)(2,1)S(1)} collective-permute-done((bf16[40,768]{1,0:T(8,128)(2,1)S(1)}, bf16[40,768]{1,0:T(8,128)(2,1)S(1)}, u32[]{:S(2)}, u32[]{:S(2)}) %collective-permute-start.1) | collective-permute-done | bytes 61472 | tf_op jit(solution)/shard_map/ppermute | solution.py:325
  10.3 0.5 %collective-permute-done.2.rest_3_ = bf16[40,768]{1,0:T(8,128)(2,1)S(1)} collective-permute-done((bf16[40,768]{1,0:T(8,128)(2,1)S(1)}, bf16[40,768]{1,0:T(8,128)(2,1)S(1)}, u32[]{:S(2)}, u32[]{:S(2)}) %collective-permute-start.2) | collective-permute-done | bytes 61472 | tf_op jit(solution)/shard_map/ppermute | solution.py:325
  10.8 0.9 %shard_map.178 = (bf16[40,384]{1,0:T(8,128)(2,1)S(1)}, bf16[40,768]{1,0:T(8,128)(2,1)S(1)}, bf16[40,768]{1,0:T(8,128)(2,1)S(1)}, bf16[40,768]{1,0:T(8,128)(2,1)S(1)}) custom-call(bf16[3,80,128]{2,1,0:T(8,128)(2,1)S(1)} %get-tuple-element.23.stacked, f32[3,80,226]{2,1,0:T(8,128)S(1)} %get-tuple-element.24.text_scores, f32[1,160]{1,0:T(1,128)S(1)} %get-tuple-element.25.bias, ...), custom_call_target="tpu_custom_call" | custom-call | flops 100000000 | bytes 1562500 | tf_op jit(solution)/shard_map/pallas_call | solution.py:40
  11.7 3.7 %collective-permute-start.3 = (bf16[40,768]{1,0:T(8,128)(2,1)S(1)}, bf16[40,768]{1,0:T(8,128)(2,1)S(1)}, u32[]{:S(2)}, u32[]{:S(2)}) collective-permute-start(bf16[40,768]{1,0:T(8,128)(2,1)S(1)} %get-tuple-element.33), channel_id=1, source_target_pairs={{0,3},{1,2},{2,1},{3,0},{4,7},{5,6},{6,5},{7,4},{8,11},{9,10},{10,... | collective-permute-start | bytes 184328 | tf_op jit(solution)/shard_map/ppermute | solution.py:329
  15.4 0.0 collective-permute-start.4
  15.4 0.8 %collective-permute-start.5 = (bf16[40,768]{1,0:T(8,128)(2,1)S(1)}, bf16[40,768]{1,0:T(8,128)(2,1)S(1)}, u32[]{:S(2)}, u32[]{:S(2)}) collective-permute-start(bf16[40,768]{1,0:T(8,128)(2,1)S(1)} %get-tuple-element.35), channel_id=1, source_target_pairs={{0,1},{1,0},{2,3},{3,2},{4,5},{5,4},{6,7},{7,6},{8,9},{9,8},{10,11... | collective-permute-start | bytes 184328 | tf_op jit(solution)/shard_map/ppermute | solution.py:329
  16.2 0.0 copy-done.5
  16.2 0.0 copy-done.6
  16.2 0.0 copy-done.7
  16.9 0.0 copy-done
  16.9 0.0 copy-done.1
  16.9 0.0 copy-done.2
  16.9 0.0 copy-done.3
  16.9 0.0 copy-done.4
  16.9 0.9 %shard_map.179 = (f32[40,768]{1,0:T(8,128)S(1)}, f32[40,768]{1,0:T(8,128)S(1)}, bf16[208,768]{1,0:T(8,128)(2,1)S(1)}, f32[64,128]{1,0:T(8,128)S(1)}, f32[48,128]{1,0:T(8,128)S(1)}) custom-call(s32[4]{0:T(128)S(1)} %copy-done.2, f32[1000]{0:T(1024)S(1)} %copy-done.3, s32[1]{0:T(128)S(6)} %copy.19.step, bf16[40,384]{1,0:T(8,128)(2,1)S(1)} %get-tuple-element.28.attended, ...), custom_call_target="tpu_custom_call" | custom-call | flops 100000000 | bytes 1562500 | tf_op jit(solution)/shard_map/pallas_call | solution.py:40
  17.8 0.0 collective-permute-done.3.rest_0_
  17.8 2.7 %collective-permute-done.4.rest_1_ = bf16[40,768]{1,0:T(8,128)(2,1)S(1)} collective-permute-done((bf16[40,768]{1,0:T(8,128)(2,1)S(1)}, bf16[40,768]{1,0:T(8,128)(2,1)S(1)}, u32[]{:S(2)}, u32[]{:S(2)}) %collective-permute-start.4) | collective-permute-done | bytes 61472 | tf_op jit(solution)/shard_map/ppermute | solution.py:329
  20.5 0.0 collective-permute-done.5.rest_2_
  20.5 0.3 shard_map.180
  20.8 1.8 %collective-permute-start.6 = (f32[24,128]{1,0:T(8,128)S(1)}, f32[24,128]{1,0:T(8,128)S(1)}, u32[]{:S(2)}, u32[]{:S(2)}) collective-permute-start(f32[24,128]{1,0:T(8,128)S(1)} %get-tuple-element.38), channel_id=1, source_target_pairs={{0,3},{1,2},{2,1},{3,0},{4,7},{5,6},{6,5},{7,4},{8,11},{9,10},{10,... | collective-permute-start | bytes 36872 | tf_op jit(solution)/shard_map/ppermute | solution.py:329
  22.6 0.4 %collective-permute-start.7 = (f32[24,128]{1,0:T(8,128)S(1)}, f32[24,128]{1,0:T(8,128)S(1)}, u32[]{:S(2)}, u32[]{:S(2)}) collective-permute-start(f32[24,128]{1,0:T(8,128)S(1)} %get-tuple-element.39), channel_id=1, source_target_pairs={{0,2},{1,3},{2,0},{3,1},{4,6},{5,7},{6,4},{7,5},{8,10},{9,11},{10,... | collective-permute-start | bytes 36872 | tf_op jit(solution)/shard_map/ppermute | solution.py:329
  23.0 2.3 %collective-permute-start.8 = (f32[24,128]{1,0:T(8,128)S(1)}, f32[24,128]{1,0:T(8,128)S(1)}, u32[]{:S(2)}, u32[]{:S(2)}) collective-permute-start(f32[24,128]{1,0:T(8,128)S(1)} %get-tuple-element.40), channel_id=1, source_target_pairs={{0,1},{1,0},{2,3},{3,2},{4,5},{5,4},{6,7},{7,6},{8,9},{9,8},{10,11... | collective-permute-start | bytes 36872 | tf_op jit(solution)/shard_map/ppermute | solution.py:329
  25.3 1.1 %collective-permute-done.6.rest_0_ = f32[24,128]{1,0:T(8,128)S(1)} collective-permute-done((f32[24,128]{1,0:T(8,128)S(1)}, f32[24,128]{1,0:T(8,128)S(1)}, u32[]{:S(2)}, u32[]{:S(2)}) %collective-permute-start.6) | collective-permute-done | bytes 12320 | tf_op jit(solution)/shard_map/ppermute | solution.py:329
  26.4 0.8 %collective-permute-done.7.rest_1_ = f32[24,128]{1,0:T(8,128)S(1)} collective-permute-done((f32[24,128]{1,0:T(8,128)S(1)}, f32[24,128]{1,0:T(8,128)S(1)}, u32[]{:S(2)}, u32[]{:S(2)}) %collective-permute-start.7) | collective-permute-done | bytes 12320 | tf_op jit(solution)/shard_map/ppermute | solution.py:329
  27.2 0.0 collective-permute-done.8.rest_2_
  27.2 0.1 collective-permute-start.9
  27.3 0.6 %shard_map.181 = bf16[1,40,768]{2,1,0:T(8,128)(2,1)} custom-call(bf16[40,768]{1,0:T(8,128)(2,1)S(1)} %get-tuple-element.36.value), custom_call_target="tpu_custom_call" | custom-call | flops 2000000 | bytes 31250 | tf_op jit(solution)/shard_map/pallas_call | solution.py:40
  27.9 0.5 %collective-permute-done.9.theirs = f32[16,128]{1,0:T(8,128)S(1)} collective-permute-done((f32[16,128]{1,0:T(8,128)S(1)}, f32[16,128]{1,0:T(8,128)S(1)}, u32[]{:S(2)}, u32[]{:S(2)}) %collective-permute-start.9) | collective-permute-done | bytes 8224 | tf_op jit(solution)/shard_map/ppermute | solution.py:325
  28.4 0.7 %shard_map.183 = f32[8,40]{1,0:T(8,128)} custom-call(f32[16,128]{1,0:T(8,128)S(1)} %get-tuple-element.41.mine, f32[16,128]{1,0:T(8,128)S(1)} %collective-permute-done.9.theirs, f32[48,128]{1,0:T(8,128)S(1)} %get-tuple-element.43.coefs), custom_call_target="tpu_custom_call" | custom-call | tf_op jit(solution)/shard_map/pallas_call | solution.py:40
  (4 shorter events, 0.0 us)
Async XLA Ops:
  2.1 7.4 %collective-permute-start = (bf16[40,768]{1,0:T(8,128)(2,1)S(1)}, bf16[40,768]{1,0:T(8,128)(2,1)S(1)}, u32[]{:S(2)}, u32[]{:S(2)}) collective-permute-start(bf16[40,768]{1,0:T(8,128)(2,1)S(1)} %shard_map.177.rest_0_), channel_id=1, source_target_pairs={{0,12},{4,8},{8,4},{12,0},{1,13},{5,9},{9,5},{13,1},{2,14},{6,10},... | collective-permute-start | bytes 184328 | tf_op jit(solution)/shard_map/ppermute | solution.py:325
  6.1 4.2 %collective-permute-start.1 = (bf16[40,768]{1,0:T(8,128)(2,1)S(1)}, bf16[40,768]{1,0:T(8,128)(2,1)S(1)}, u32[]{:S(2)}, u32[]{:S(2)}) collective-permute-start(bf16[40,768]{1,0:T(8,128)(2,1)S(1)} %shard_map.177.rest_0_), channel_id=1, source_target_pairs={{0,8},{4,12},{8,0},{12,4},{1,9},{5,13},{9,1},{13,5},{2,10},{6,14},... | collective-permute-start | bytes 184328 | tf_op jit(solution)/shard_map/ppermute | solution.py:325
  6.6 4.2 %collective-permute-start.2 = (bf16[40,768]{1,0:T(8,128)(2,1)S(1)}, bf16[40,768]{1,0:T(8,128)(2,1)S(1)}, u32[]{:S(2)}, u32[]{:S(2)}) collective-permute-start(bf16[40,768]{1,0:T(8,128)(2,1)S(1)} %shard_map.177.rest_0_), channel_id=1, source_target_pairs={{0,4},{4,0},{8,12},{12,8},{1,5},{5,1},{9,13},{13,9},{2,6},{6,2},{1... | collective-permute-start | bytes 184328 | tf_op jit(solution)/shard_map/ppermute | solution.py:325
  6.7 9.5 %copy-start.5 = (f32[768]{0:T(1024)S(1)}, f32[768]{0:T(1024)}, u32[]{:S(2)}) copy-start(f32[768]{0:T(1024)} %param.24) | copy-start | bytes 9220
  6.7 9.5 %copy-start.6 = (f32[768]{0:T(1024)S(1)}, f32[768]{0:T(1024)}, u32[]{:S(2)}) copy-start(f32[768]{0:T(1024)} %param.25) | copy-start | bytes 9220
  6.7 9.5 %copy-start.7 = (f32[768]{0:T(1024)S(1)}, f32[768]{0:T(1024)}, u32[]{:S(2)}) copy-start(f32[768]{0:T(1024)} %param.26) | copy-start | bytes 9220
  6.7 10.1 %copy-start = (f32[768,64]{0,1:T(8,128)S(1)}, f32[768,64]{0,1:T(8,128)}, u32[]{:S(2)}) copy-start(f32[768,64]{0,1:T(8,128)} %param.27) | copy-start | bytes 589828
  6.7 10.1 %copy-start.1 = (bf16[1,40,768]{2,1,0:T(8,128)(2,1)S(1)}, bf16[1,40,768]{2,1,0:T(8,128)(2,1)}, u32[]{:S(2)}) copy-start(bf16[1,40,768]{2,1,0:T(8,128)(2,1)} %stream.1) | copy-start | bytes 184324
  6.7 10.1 %copy-start.2 = (s32[4]{0:T(128)S(1)}, s32[4]{0:T(128)}, u32[]{:S(2)}) copy-start(s32[4]{0:T(128)} %lengths.1) | copy-start | bytes 52
  6.8 10.1 %copy-start.3 = (f32[1000]{0:T(1024)S(1)}, f32[1000]{0:T(1024)}, u32[]{:S(2)}) copy-start(f32[1000]{0:T(1024)} %alphas.1) | copy-start | bytes 12004
  6.8 10.1 %copy-start.4 = (f32[40,8]{0,1:T(8,128)S(1)}, f32[40,8]{0,1:T(8,128)}, u32[]{:S(2)}) copy-start(f32[40,8]{0,1:T(8,128)} %param.31) | copy-start | bytes 3844
  11.7 6.1 %collective-permute-start.3 = (bf16[40,768]{1,0:T(8,128)(2,1)S(1)}, bf16[40,768]{1,0:T(8,128)(2,1)S(1)}, u32[]{:S(2)}, u32[]{:S(2)}) collective-permute-start(bf16[40,768]{1,0:T(8,128)(2,1)S(1)} %get-tuple-element.33), channel_id=1, source_target_pairs={{0,3},{1,2},{2,1},{3,0},{4,7},{5,6},{6,5},{7,4},{8,11},{9,10},{10,... | collective-permute-start | bytes 184328 | tf_op jit(solution)/shard_map/ppermute | solution.py:329
  15.4 5.1 %collective-permute-start.4 = (bf16[40,768]{1,0:T(8,128)(2,1)S(1)}, bf16[40,768]{1,0:T(8,128)(2,1)S(1)}, u32[]{:S(2)}, u32[]{:S(2)}) collective-permute-start(bf16[40,768]{1,0:T(8,128)(2,1)S(1)} %get-tuple-element.34), channel_id=1, source_target_pairs={{0,2},{1,3},{2,0},{3,1},{4,6},{5,7},{6,4},{7,5},{8,10},{9,11},{10,... | collective-permute-start | bytes 184328 | tf_op jit(solution)/shard_map/ppermute | solution.py:329
  15.4 5.1 %collective-permute-start.5 = (bf16[40,768]{1,0:T(8,128)(2,1)S(1)}, bf16[40,768]{1,0:T(8,128)(2,1)S(1)}, u32[]{:S(2)}, u32[]{:S(2)}) collective-permute-start(bf16[40,768]{1,0:T(8,128)(2,1)S(1)} %get-tuple-element.35), channel_id=1, source_target_pairs={{0,1},{1,0},{2,3},{3,2},{4,5},{5,4},{6,7},{7,6},{8,9},{9,8},{10,11... | collective-permute-start | bytes 184328 | tf_op jit(solution)/shard_map/ppermute | solution.py:329
  20.8 5.6 %collective-permute-start.6 = (f32[24,128]{1,0:T(8,128)S(1)}, f32[24,128]{1,0:T(8,128)S(1)}, u32[]{:S(2)}, u32[]{:S(2)}) collective-permute-start(f32[24,128]{1,0:T(8,128)S(1)} %get-tuple-element.38), channel_id=1, source_target_pairs={{0,3},{1,2},{2,1},{3,0},{4,7},{5,6},{6,5},{7,4},{8,11},{9,10},{10,... | collective-permute-start | bytes 36872 | tf_op jit(solution)/shard_map/ppermute | solution.py:329
  22.6 4.6 %collective-permute-start.7 = (f32[24,128]{1,0:T(8,128)S(1)}, f32[24,128]{1,0:T(8,128)S(1)}, u32[]{:S(2)}, u32[]{:S(2)}) collective-permute-start(f32[24,128]{1,0:T(8,128)S(1)} %get-tuple-element.39), channel_id=1, source_target_pairs={{0,2},{1,3},{2,0},{3,1},{4,6},{5,7},{6,4},{7,5},{8,10},{9,11},{10,... | collective-permute-start | bytes 36872 | tf_op jit(solution)/shard_map/ppermute | solution.py:329
  23.0 4.2 %collective-permute-start.8 = (f32[24,128]{1,0:T(8,128)S(1)}, f32[24,128]{1,0:T(8,128)S(1)}, u32[]{:S(2)}, u32[]{:S(2)}) collective-permute-start(f32[24,128]{1,0:T(8,128)S(1)} %get-tuple-element.40), channel_id=1, source_target_pairs={{0,1},{1,0},{2,3},{3,2},{4,5},{5,4},{6,7},{7,6},{8,9},{9,8},{10,11... | collective-permute-start | bytes 36872 | tf_op jit(solution)/shard_map/ppermute | solution.py:329
  27.2 1.2 %collective-permute-start.9 = (f32[16,128]{1,0:T(8,128)S(1)}, f32[16,128]{1,0:T(8,128)S(1)}, u32[]{:S(2)}, u32[]{:S(2)}) collective-permute-start(f32[16,128]{1,0:T(8,128)S(1)} %get-tuple-element.42), channel_id=1, source_target_pairs={{0,16},{16,0},{1,17},{17,1},{2,18},{18,2},{3,19},{19,3},{4,20},{20... | collective-permute-start | bytes 24584 | tf_op jit(solution)/shard_map/ppermute | solution.py:325

commit v4 on v3

--- a/solution.py
+++ b/solution.py
@@ -84,12 +84,16 @@
 
 
 def head_norm(field, average, gain):
-    centre = field.astype(F32) - nn(field, average)
+    rows, width = field.shape
+    pairs = [field[:, at : at + PAIR].astype(F32) for at in range(0, width, PAIR)]
+    tall = jnp.concatenate(pairs, axis=0)
+    centre = tall - nn(tall.astype(BF16), average)
     square = centre * centre
     high = square.astype(BF16)
     low = (square - high.astype(F32)).astype(BF16)
     spread = nn(high, average) + nn(low, average)
-    return centre * lax.rsqrt(spread + head_eps) * gain
+    normed = centre * lax.rsqrt(spread + head_eps) * gain
+    return [normed[rows * p : rows * p + rows] for p in range(len(pairs))]
 
 
 def rope_tables(start, rows):
@@ -130,9 +134,8 @@
     arriving[1].wait()
     arriving[2].wait()
     wide = twice(gain)
-    for at in range(0, width, PAIR):
-        normed = head_norm(keys[0, :, at : at + PAIR], average, wide)
-        packed[:, at : at + PAIR] = rotate(normed, *tables).astype(BF16)
+    for p, normed in enumerate(head_norm(keys[0], average, wide)):
+        packed[:, PAIR * p : PAIR * p + PAIR] = rotate(normed, *tables).astype(BF16)
     arriving[3].wait()
     packed[:, width:] = values[0]
 
@@ -159,14 +162,16 @@
     for one in arriving[1:5]:
         one.wait()
     q_wide, k_wide = twice(q_gain), twice(k_gain)
-    for p, at in enumerate(range(0, width, PAIR)):
-        query = rotate(head_norm(queries[0, :, at : at + PAIR], average, q_wide), *tables)
+    text_hat = []
+    for at in range(0, width, PAIR):
+        text_hat += head_norm(text_keys[0, :, at : at + PAIR], average, k_wide)
+    for p, normed in enumerate(head_norm(queries[0], average, q_wide)):
+        query = rotate(normed, *tables)
         query = query.astype(BF16).astype(F32) * 0.125
         both = jnp.concatenate([jnp.where(left, query, 0.0), jnp.where(left, 0.0, query)], axis=0)
         both = both.astype(BF16)
         stacked[p] = both
-        key = head_norm(text_keys[0, :, at : at + PAIR], average, k_wide).astype(BF16)
-        text_scores[p] = nt(both, key)
+        text_scores[p] = nt(both, text_hat[p].astype(BF16))
     arriving[5].wait()
     arriving[6].wait()
 
@@ -381,11 +386,11 @@
         ],
         cost=20000000,
     )(lengths, queries, text_keys, q_gain, k_gain, text_values, out_weight)
-    routes = [[i ^ d for i in range(tp)] for d in range(tp - 1, 0, -1)]
-    late_routes = routes
+    routes = [[i ^ d for i in range(tp)] for d in [3, 2, 1]]
+    late_routes = [[i ^ d for i in range(tp)] for d in (3, 2, 1)]
     attended, *outgoing = call(
-        functools.partial(attend_kernel, len(gathered), lambda rank: [entry(r, rank) for r in routes]),
-        [vmem((rows, width), BF16)] + [vmem((rows, columns), BF16)] * (tp - 1),
+        functools.partial(attend_kernel, len(gathered), lambda rank: [entry(r, rank) for r in routes[:3]]),
+        [vmem((rows, width), BF16)] + [vmem((rows, columns), BF16)] * 3,
         "v" * (5 + len(gathered)),
         cost=100000000,
     )(stacked, text_scores, bias, held_values, held_weight, *gathered)

time: 29.3 us -> 29 us (0.990)
  Pallas kernels: 7.55 us -> 6.93 us
  waiting for transfers between devices: 6.45 us -> 6.79 us
    pallas_call x8, Pallas kernels: 7.55 us -> 6.93 us  [placed(): run(*(pltpu.with_memory_space_constraint(x, pltpu.HBM) if i == 'h' else x...]
    ppermute x4, waiting for transfers between devices: 1.81 us -> 2.15 us  [exchange(): lax.ppermute(value, axis, [(i, i ^ distance) for i in range(lax.axis_size...]
  transfers between devices with their start and end apart: 10 -> 10, of which waited for: 6 -> 6; matrix products, arithmetic and copies ran while one was open for 0% -> 0% of each run, Pallas kernels for 14% -> 13%
where the time goes in v4:
time: 29 us; the launch traced here: 28.8 us
  starting transfers between devices  13.6 us (47%)
  Pallas kernels  6.93 us (24%)
  waiting for transfers between devices  6.79 us (23%)
  between operations  1.45 us (5%)
    ppermute x6, starting transfers between devices, send(): return lax.ppermute(value, axis, list(enumerate(route)))  8.91 us
    pallas_call x8, Pallas kernels, placed(): run(*(pltpu.with_memory_space_constraint(x, pltpu.HBM) if i == 'h' else x...  6.93 us
    ppermute x4, starting transfers between devices, exchange(): lax.ppermute(value, axis, [(i, i ^ distance) for i in range(lax.axis_size...  4.67 us
    ppermute x6, waiting for transfers between devices, send(): return lax.ppermute(value, axis, list(enumerate(route)))  4.64 us
    ppermute x4, waiting for transfers between devices, exchange(): lax.ppermute(value, axis, [(i, i ^ distance) for i in range(lax.axis_size...  2.15 us
  transfers between devices with their start and end apart: 10, of which 6 were waited for; matrix products, arithmetic and copies ran while one was open for 0% of the time, Pallas kernels for 13%

profile of v4, /device:TPU:0, one launch (start us, length us, event | category | flops | bytes accessed | tf_op | source)
XLA Modules:
  0.0 28.8 jit_solution(16683581032424693295)
XLA Ops:
  0.6 1.2 %shard_map.177.rest_0_ = bf16[40,768]{1,0:T(8,128)(2,1)S(1)} custom-call(s32[4]{0:T(128)} %lengths.1, bf16[1,40,384]{2,1,0:T(8,128)(2,1)} %keys_at.1, bf16[1,40,384]{2,1,0:T(8,128)(2,1)} %values_at.1, f32[1,64]{1,0:T(1,128)} %bitcast.8), custom_call_target="tpu_custom_call" | custom-call | flops 2000000 | bytes 31250 | tf_op jit(solution)/shard_map/pallas_call | solution.py:40
  1.8 4.0 %collective-permute-start = (bf16[40,768]{1,0:T(8,128)(2,1)S(1)}, bf16[40,768]{1,0:T(8,128)(2,1)S(1)}, u32[]{:S(2)}, u32[]{:S(2)}) collective-permute-start(bf16[40,768]{1,0:T(8,128)(2,1)S(1)} %shard_map.177.rest_0_), channel_id=1, source_target_pairs={{0,12},{4,8},{8,4},{12,0},{1,13},{5,9},{9,5},{13,1},{2,14},{6,10},... | collective-permute-start | bytes 184328 | tf_op jit(solution)/shard_map/ppermute | solution.py:330
  5.8 0.5 %collective-permute-start.1 = (bf16[40,768]{1,0:T(8,128)(2,1)S(1)}, bf16[40,768]{1,0:T(8,128)(2,1)S(1)}, u32[]{:S(2)}, u32[]{:S(2)}) collective-permute-start(bf16[40,768]{1,0:T(8,128)(2,1)S(1)} %shard_map.177.rest_0_), channel_id=1, source_target_pairs={{0,8},{4,12},{8,0},{12,4},{1,9},{5,13},{9,1},{13,5},{2,10},{6,14},... | collective-permute-start | bytes 184328 | tf_op jit(solution)/shard_map/ppermute | solution.py:330
  6.3 0.1 collective-permute-start.2
  6.4 0.0 copy-start.5
  6.4 0.0 copy-start.6
  6.4 0.0 copy-start.7
  6.4 0.0 copy-start
  6.4 0.0 copy-start.1
  6.5 0.0 copy-start.2
  6.5 0.0 copy-start.3
  6.5 0.0 copy-start.4
  6.5 2.4 %shard_map.176 = (bf16[3,80,128]{2,1,0:T(8,128)(2,1)S(1)}, f32[3,80,226]{2,1,0:T(8,128)S(1)}, f32[1,160]{1,0:T(1,128)S(1)}, bf16[1,226,384]{2,1,0:T(8,128)(2,1)S(1)}, bf16[384,3072]{1,0:T(8,128)(2,1)S(1)}) custom-call(s32[4]{0:T(128)} %lengths.1, bf16[1,40,384]{2,1,0:T(8,128)(2,1)} %queries_at.1, bf16[1,226,384]{2,1,0:T(8,128)(2,1)} %text_keys_at.1, ...), custom_call_target="tpu_custom_call" | custom-call | flops 20000000 | bytes 312500 | tf_op jit(solution)/shard_map/pallas_call | solution.py:40
  8.9 0.0 collective-permute-done.rest_1_
  8.9 1.1 %collective-permute-done.1.rest_2_ = bf16[40,768]{1,0:T(8,128)(2,1)S(1)} collective-permute-done((bf16[40,768]{1,0:T(8,128)(2,1)S(1)}, bf16[40,768]{1,0:T(8,128)(2,1)S(1)}, u32[]{:S(2)}, u32[]{:S(2)}) %collective-permute-start.1) | collective-permute-done | bytes 61472 | tf_op jit(solution)/shard_map/ppermute | solution.py:330
  10.0 0.5 %collective-permute-done.2.rest_3_ = bf16[40,768]{1,0:T(8,128)(2,1)S(1)} collective-permute-done((bf16[40,768]{1,0:T(8,128)(2,1)S(1)}, bf16[40,768]{1,0:T(8,128)(2,1)S(1)}, u32[]{:S(2)}, u32[]{:S(2)}) %collective-permute-start.2) | collective-permute-done | bytes 61472 | tf_op jit(solution)/shard_map/ppermute | solution.py:330
  10.5 0.9 %shard_map.178 = (bf16[40,384]{1,0:T(8,128)(2,1)S(1)}, bf16[40,768]{1,0:T(8,128)(2,1)S(1)}, bf16[40,768]{1,0:T(8,128)(2,1)S(1)}, bf16[40,768]{1,0:T(8,128)(2,1)S(1)}) custom-call(bf16[3,80,128]{2,1,0:T(8,128)(2,1)S(1)} %get-tuple-element.23.stacked, f32[3,80,226]{2,1,0:T(8,128)S(1)} %get-tuple-element.24.text_scores, f32[1,160]{1,0:T(1,128)S(1)} %get-tuple-element.25.bias, ...), custom_call_target="tpu_custom_call" | custom-call | flops 100000000 | bytes 1562500 | tf_op jit(solution)/shard_map/pallas_call | solution.py:40
  11.4 3.7 %collective-permute-start.3 = (bf16[40,768]{1,0:T(8,128)(2,1)S(1)}, bf16[40,768]{1,0:T(8,128)(2,1)S(1)}, u32[]{:S(2)}, u32[]{:S(2)}) collective-permute-start(bf16[40,768]{1,0:T(8,128)(2,1)S(1)} %get-tuple-element.33), channel_id=1, source_target_pairs={{0,3},{1,2},{2,1},{3,0},{4,7},{5,6},{6,5},{7,4},{8,11},{9,10},{10,... | collective-permute-start | bytes 184328 | tf_op jit(solution)/shard_map/ppermute | solution.py:334
  15.1 0.0 collective-permute-start.4
  15.1 0.8 %collective-permute-start.5 = (bf16[40,768]{1,0:T(8,128)(2,1)S(1)}, bf16[40,768]{1,0:T(8,128)(2,1)S(1)}, u32[]{:S(2)}, u32[]{:S(2)}) collective-permute-start(bf16[40,768]{1,0:T(8,128)(2,1)S(1)} %get-tuple-element.35), channel_id=1, source_target_pairs={{0,1},{1,0},{2,3},{3,2},{4,5},{5,4},{6,7},{7,6},{8,9},{9,8},{10,11... | collective-permute-start | bytes 184328 | tf_op jit(solution)/shard_map/ppermute | solution.py:334
  15.9 0.0 copy-done.5
  15.9 0.0 copy-done.6
  15.9 0.0 copy-done.7
  16.6 0.0 copy-done
  16.6 0.0 copy-done.1
  16.6 0.0 copy-done.2
  16.6 0.0 copy-done.3
  16.6 0.0 copy-done.4
  16.6 0.9 %shard_map.179 = (f32[40,768]{1,0:T(8,128)S(1)}, f32[40,768]{1,0:T(8,128)S(1)}, bf16[208,768]{1,0:T(8,128)(2,1)S(1)}, f32[64,128]{1,0:T(8,128)S(1)}, f32[48,128]{1,0:T(8,128)S(1)}) custom-call(s32[4]{0:T(128)S(1)} %copy-done.2, f32[1000]{0:T(1024)S(1)} %copy-done.3, s32[1]{0:T(128)S(6)} %copy.19.step, bf16[40,384]{1,0:T(8,128)(2,1)S(1)} %get-tuple-element.28.attended, ...), custom_call_target="tpu_custom_call" | custom-call | flops 100000000 | bytes 1562500 | tf_op jit(solution)/shard_map/pallas_call | solution.py:40
  17.5 0.0 collective-permute-done.3.rest_0_
  17.5 2.7 %collective-permute-done.4.rest_1_ = bf16[40,768]{1,0:T(8,128)(2,1)S(1)} collective-permute-done((bf16[40,768]{1,0:T(8,128)(2,1)S(1)}, bf16[40,768]{1,0:T(8,128)(2,1)S(1)}, u32[]{:S(2)}, u32[]{:S(2)}) %collective-permute-start.4) | collective-permute-done | bytes 61472 | tf_op jit(solution)/shard_map/ppermute | solution.py:334
  20.2 0.0 collective-permute-done.5.rest_2_
  20.2 0.3 shard_map.180
  20.5 1.8 %collective-permute-start.6 = (f32[24,128]{1,0:T(8,128)S(1)}, f32[24,128]{1,0:T(8,128)S(1)}, u32[]{:S(2)}, u32[]{:S(2)}) collective-permute-start(f32[24,128]{1,0:T(8,128)S(1)} %get-tuple-element.38), channel_id=1, source_target_pairs={{0,3},{1,2},{2,1},{3,0},{4,7},{5,6},{6,5},{7,4},{8,11},{9,10},{10,... | collective-permute-start | bytes 36872 | tf_op jit(solution)/shard_map/ppermute | solution.py:334
  22.3 0.4 %collective-permute-start.7 = (f32[24,128]{1,0:T(8,128)S(1)}, f32[24,128]{1,0:T(8,128)S(1)}, u32[]{:S(2)}, u32[]{:S(2)}) collective-permute-start(f32[24,128]{1,0:T(8,128)S(1)} %get-tuple-element.39), channel_id=1, source_target_pairs={{0,2},{1,3},{2,0},{3,1},{4,6},{5,7},{6,4},{7,5},{8,10},{9,11},{10,... | collective-permute-start | bytes 36872 | tf_op jit(solution)/shard_map/ppermute | solution.py:334
  22.7 2.3 %collective-permute-start.8 = (f32[24,128]{1,0:T(8,128)S(1)}, f32[24,128]{1,0:T(8,128)S(1)}, u32[]{:S(2)}, u32[]{:S(2)}) collective-permute-start(f32[24,128]{1,0:T(8,128)S(1)} %get-tuple-element.40), channel_id=1, source_target_pairs={{0,1},{1,0},{2,3},{3,2},{4,5},{5,4},{6,7},{7,6},{8,9},{9,8},{10,11... | collective-permute-start | bytes 36872 | tf_op jit(solution)/shard_map/ppermute | solution.py:334
  25.0 1.1 %collective-permute-done.6.rest_0_ = f32[24,128]{1,0:T(8,128)S(1)} collective-permute-done((f32[24,128]{1,0:T(8,128)S(1)}, f32[24,128]{1,0:T(8,128)S(1)}, u32[]{:S(2)}, u32[]{:S(2)}) %collective-permute-start.6) | collective-permute-done | bytes 12320 | tf_op jit(solution)/shard_map/ppermute | solution.py:334
  26.1 0.8 %collective-permute-done.7.rest_1_ = f32[24,128]{1,0:T(8,128)S(1)} collective-permute-done((f32[24,128]{1,0:T(8,128)S(1)}, f32[24,128]{1,0:T(8,128)S(1)}, u32[]{:S(2)}, u32[]{:S(2)}) %collective-permute-start.7) | collective-permute-done | bytes 12320 | tf_op jit(solution)/shard_map/ppermute | solution.py:334
  26.9 0.0 collective-permute-done.8.rest_2_
  26.9 0.1 collective-permute-start.9
  27.0 0.6 %shard_map.181 = bf16[1,40,768]{2,1,0:T(8,128)(2,1)} custom-call(bf16[40,768]{1,0:T(8,128)(2,1)S(1)} %get-tuple-element.36.value), custom_call_target="tpu_custom_call" | custom-call | flops 2000000 | bytes 31250 | tf_op jit(solution)/shard_map/pallas_call | solution.py:40
  27.6 0.5 %collective-permute-done.9.theirs = f32[16,128]{1,0:T(8,128)S(1)} collective-permute-done((f32[16,128]{1,0:T(8,128)S(1)}, f32[16,128]{1,0:T(8,128)S(1)}, u32[]{:S(2)}, u32[]{:S(2)}) %collective-permute-start.9) | collective-permute-done | bytes 8224 | tf_op jit(solution)/shard_map/ppermute | solution.py:330
  28.1 0.7 %shard_map.183 = f32[8,40]{1,0:T(8,128)} custom-call(f32[16,128]{1,0:T(8,128)S(1)} %get-tuple-element.41.mine, f32[16,128]{1,0:T(8,128)S(1)} %collective-permute-done.9.theirs, f32[48,128]{1,0:T(8,128)S(1)} %get-tuple-element.43.coefs), custom_call_target="tpu_custom_call" | custom-call | tf_op jit(solution)/shard_map/pallas_call | solution.py:40
  (4 shorter events, 0.0 us)
Async XLA Ops:
  1.8 7.1 %collective-permute-start = (bf16[40,768]{1,0:T(8,128)(2,1)S(1)}, bf16[40,768]{1,0:T(8,128)(2,1)S(1)}, u32[]{:S(2)}, u32[]{:S(2)}) collective-permute-start(bf16[40,768]{1,0:T(8,128)(2,1)S(1)} %shard_map.177.rest_0_), channel_id=1, source_target_pairs={{0,12},{4,8},{8,4},{12,0},{1,13},{5,9},{9,5},{13,1},{2,14},{6,10},... | collective-permute-start | bytes 184328 | tf_op jit(solution)/shard_map/ppermute | solution.py:330
  5.8 4.2 %collective-permute-start.1 = (bf16[40,768]{1,0:T(8,128)(2,1)S(1)}, bf16[40,768]{1,0:T(8,128)(2,1)S(1)}, u32[]{:S(2)}, u32[]{:S(2)}) collective-permute-start(bf16[40,768]{1,0:T(8,128)(2,1)S(1)} %shard_map.177.rest_0_), channel_id=1, source_target_pairs={{0,8},{4,12},{8,0},{12,4},{1,9},{5,13},{9,1},{13,5},{2,10},{6,14},... | collective-permute-start | bytes 184328 | tf_op jit(solution)/shard_map/ppermute | solution.py:330
  6.3 4.2 %collective-permute-start.2 = (bf16[40,768]{1,0:T(8,128)(2,1)S(1)}, bf16[40,768]{1,0:T(8,128)(2,1)S(1)}, u32[]{:S(2)}, u32[]{:S(2)}) collective-permute-start(bf16[40,768]{1,0:T(8,128)(2,1)S(1)} %shard_map.177.rest_0_), channel_id=1, source_target_pairs={{0,4},{4,0},{8,12},{12,8},{1,5},{5,1},{9,13},{13,9},{2,6},{6,2},{1... | collective-permute-start | bytes 184328 | tf_op jit(solution)/shard_map/ppermute | solution.py:330
  6.4 9.5 %copy-start.5 = (f32[768]{0:T(1024)S(1)}, f32[768]{0:T(1024)}, u32[]{:S(2)}) copy-start(f32[768]{0:T(1024)} %param.24) | copy-start | bytes 9220
  6.4 9.5 %copy-start.6 = (f32[768]{0:T(1024)S(1)}, f32[768]{0:T(1024)}, u32[]{:S(2)}) copy-start(f32[768]{0:T(1024)} %param.25) | copy-start | bytes 9220
  6.4 9.5 %copy-start.7 = (f32[768]{0:T(1024)S(1)}, f32[768]{0:T(1024)}, u32[]{:S(2)}) copy-start(f32[768]{0:T(1024)} %param.26) | copy-start | bytes 9220
  6.4 10.1 %copy-start = (f32[768,64]{0,1:T(8,128)S(1)}, f32[768,64]{0,1:T(8,128)}, u32[]{:S(2)}) copy-start(f32[768,64]{0,1:T(8,128)} %param.27) | copy-start | bytes 589828
  6.4 10.1 %copy-start.1 = (bf16[1,40,768]{2,1,0:T(8,128)(2,1)S(1)}, bf16[1,40,768]{2,1,0:T(8,128)(2,1)}, u32[]{:S(2)}) copy-start(bf16[1,40,768]{2,1,0:T(8,128)(2,1)} %stream.1) | copy-start | bytes 184324
  6.5 10.1 %copy-start.2 = (s32[4]{0:T(128)S(1)}, s32[4]{0:T(128)}, u32[]{:S(2)}) copy-start(s32[4]{0:T(128)} %lengths.1) | copy-start | bytes 52
  6.5 10.1 %copy-start.3 = (f32[1000]{0:T(1024)S(1)}, f32[1000]{0:T(1024)}, u32[]{:S(2)}) copy-start(f32[1000]{0:T(1024)} %alphas.1) | copy-start | bytes 12004
  6.5 10.1 %copy-start.4 = (f32[40,8]{0,1:T(8,128)S(1)}, f32[40,8]{0,1:T(8,128)}, u32[]{:S(2)}) copy-start(f32[40,8]{0,1:T(8,128)} %param.31) | copy-start | bytes 3844
  11.4 6.1 %collective-permute-start.3 = (bf16[40,768]{1,0:T(8,128)(2,1)S(1)}, bf16[40,768]{1,0:T(8,128)(2,1)S(1)}, u32[]{:S(2)}, u32[]{:S(2)}) collective-permute-start(bf16[40,768]{1,0:T(8,128)(2,1)S(1)} %get-tuple-element.33), channel_id=1, source_target_pairs={{0,3},{1,2},{2,1},{3,0},{4,7},{5,6},{6,5},{7,4},{8,11},{9,10},{10,... | collective-permute-start | bytes 184328 | tf_op jit(solution)/shard_map/ppermute | solution.py:334
  15.1 5.1 %collective-permute-start.4 = (bf16[40,768]{1,0:T(8,128)(2,1)S(1)}, bf16[40,768]{1,0:T(8,128)(2,1)S(1)}, u32[]{:S(2)}, u32[]{:S(2)}) collective-permute-start(bf16[40,768]{1,0:T(8,128)(2,1)S(1)} %get-tuple-element.34), channel_id=1, source_target_pairs={{0,2},{1,3},{2,0},{3,1},{4,6},{5,7},{6,4},{7,5},{8,10},{9,11},{10,... | collective-permute-start | bytes 184328 | tf_op jit(solution)/shard_map/ppermute | solution.py:334
  15.1 5.1 %collective-permute-start.5 = (bf16[40,768]{1,0:T(8,128)(2,1)S(1)}, bf16[40,768]{1,0:T(8,128)(2,1)S(1)}, u32[]{:S(2)}, u32[]{:S(2)}) collective-permute-start(bf16[40,768]{1,0:T(8,128)(2,1)S(1)} %get-tuple-element.35), channel_id=1, source_target_pairs={{0,1},{1,0},{2,3},{3,2},{4,5},{5,4},{6,7},{7,6},{8,9},{9,8},{10,11... | collective-permute-start | bytes 184328 | tf_op jit(solution)/shard_map/ppermute | solution.py:334
  20.5 5.6 %collective-permute-start.6 = (f32[24,128]{1,0:T(8,128)S(1)}, f32[24,128]{1,0:T(8,128)S(1)}, u32[]{:S(2)}, u32[]{:S(2)}) collective-permute-start(f32[24,128]{1,0:T(8,128)S(1)} %get-tuple-element.38), channel_id=1, source_target_pairs={{0,3},{1,2},{2,1},{3,0},{4,7},{5,6},{6,5},{7,4},{8,11},{9,10},{10,... | collective-permute-start | bytes 36872 | tf_op jit(solution)/shard_map/ppermute | solution.py:334
  22.3 4.6 %collective-permute-start.7 = (f32[24,128]{1,0:T(8,128)S(1)}, f32[24,128]{1,0:T(8,128)S(1)}, u32[]{:S(2)}, u32[]{:S(2)}) collective-permute-start(f32[24,128]{1,0:T(8,128)S(1)} %get-tuple-element.39), channel_id=1, source_target_pairs={{0,2},{1,3},{2,0},{3,1},{4,6},{5,7},{6,4},{7,5},{8,10},{9,11},{10,... | collective-permute-start | bytes 36872 | tf_op jit(solution)/shard_map/ppermute | solution.py:334
  22.7 4.2 %collective-permute-start.8 = (f32[24,128]{1,0:T(8,128)S(1)}, f32[24,128]{1,0:T(8,128)S(1)}, u32[]{:S(2)}, u32[]{:S(2)}) collective-permute-start(f32[24,128]{1,0:T(8,128)S(1)} %get-tuple-element.40), channel_id=1, source_target_pairs={{0,1},{1,0},{2,3},{3,2},{4,5},{5,4},{6,7},{7,6},{8,9},{9,8},{10,11... | collective-permute-start | bytes 36872 | tf_op jit(solution)/shard_map/ppermute | solution.py:334
  26.9 1.2 %collective-permute-start.9 = (f32[16,128]{1,0:T(8,128)S(1)}, f32[16,128]{1,0:T(8,128)S(1)}, u32[]{:S(2)}, u32[]{:S(2)}) collective-permute-start(f32[16,128]{1,0:T(8,128)S(1)} %get-tuple-element.42), channel_id=1, source_target_pairs={{0,16},{16,0},{1,17},{17,1},{2,18},{18,2},{3,19},{19,3},{4,20},{20... | collective-permute-start | bytes 24584 | tf_op jit(solution)/shard_map/ppermute | solution.py:330

commit v5 on v4

--- a/solution.py
+++ b/solution.py
@@ -21,6 +21,7 @@
 
 F32 = jnp.float32
 BF16 = jnp.bfloat16
+CROSS = (False, True)
 VMEM_LIMIT = 24 * 1024 * 1024
 
 
@@ -290,30 +291,33 @@
         out[16:24] = stats
 
 
-def total_kernel(own, *rest):
+def total_kernel(crossing, own, *rest):
     arrived, (mine, other) = rest[:-2], rest[-2:]
-    total = own[...]
-    for block in arrived:
-        total = total + block[...]
-    half = lax.axis_index("cfg")
-    first, second, stats = total[0:8], total[8:16], total[16:24]
-    mine[0:8] = jnp.where(half == 0, first, second)
-    mine[8:16] = stats
-    other[0:8] = jnp.where(half == 0, second, first)
-    other[8:16] = stats
+    totals = [own[...], jnp.zeros(own.shape, F32)]
+    for cross, block in zip(crossing, arrived):
+        totals[cross] = totals[cross] + block[...]
+    first = lax.axis_index("cfg") == 0
+    for i, total in enumerate(totals):
+        low, high, stats = total[0:8], total[8:16], total[16:24]
+        at = 16 * i
+        mine[at : at + 8] = jnp.where(first, low, high)
+        other[at : at + 8] = jnp.where(first, high, low)
+        mine[at + 8 : at + 16] = stats
+        other[at + 8 : at + 16] = stats
 
 
 def step_kernel(features, mine, theirs, coefs, out):
     rows = out.shape[1]
-
-    def predict(block, consts):
+    consts = mine[0:8, rows : rows + 2] + mine[16:24, rows : rows + 2]
+
+    def predict(block):
         sums = block[0:8, :rows]
         mean = block[8:9, :rows] / features
         square = block[9:10, :rows] / features
         spread = lax.rsqrt(square - mean * mean + final_eps)
-        return spread * (sums - mean * consts[0:8, rows : rows + 1]) + consts[0:8, rows + 1 : rows + 2]
-
-    own, partner = predict(mine, mine), predict(theirs, mine)
+        return spread * (sums - mean * consts[:, 0:1]) + consts[:, 1:2]
+
+    own, partner = predict(mine[0:16] + theirs[16:32]), predict(mine[16:32] + theirs[0:16])
     is_conditioned = lax.axis_index("cfg") == 0
     conditioned = jnp.where(is_conditioned, own, partner)
     unconditioned = jnp.where(is_conditioned, partner, own)
@@ -330,8 +334,12 @@
     return lax.ppermute(value, axis, [(i, i ^ distance) for i in range(lax.axis_size(axis))])
 
 
-def send(value, axis, route):
-    return lax.ppermute(value, axis, list(enumerate(route)))
+def send(value, route, cross=False):
+    if not cross:
+        return lax.ppermute(value, "tp", list(enumerate(route)))
+    tp = len(route)
+    pairs = [(half * tp + i, (1 - half) * tp + to) for half in range(2) for i, to in enumerate(route)]
+    return lax.ppermute(value, ("cfg", "tp"), pairs)
 
 
 def entry(route, rank):
@@ -365,8 +373,8 @@
         cost=2000000,
     )(lengths, keys, values, k_gain)
     if direct:
-        gathered = [packed] + [exchange(packed, "seq", d) for d in (3, 2, 1)]
-        order = lambda rank: [rank] + [rank ^ d for d in (3, 2, 1)]
+        gathered = [packed] + [exchange(packed, "seq", d) for d in range(blocks - 1, 0, -1)]
+        order = lambda rank: [rank] + [rank ^ d for d in range(blocks - 1, 0, -1)]
     else:
         gathered = [lax.all_gather(packed, "seq", axis=0, tiled=True)]
         order = lambda rank: range(blocks)
@@ -386,15 +394,16 @@
         ],
         cost=20000000,
     )(lengths, queries, text_keys, q_gain, k_gain, text_values, out_weight)
-    routes = [[i ^ d for i in range(tp)] for d in [3, 2, 1]]
-    late_routes = [[i ^ d for i in range(tp)] for d in (3, 2, 1)]
+    distances = range(tp - 1, 0, -1)
+    routes = [[i ^ d for i in range(tp)] for d in distances]
+    crossing = [CROSS[d % 2] for d in distances]
     attended, *outgoing = call(
-        functools.partial(attend_kernel, len(gathered), lambda rank: [entry(r, rank) for r in routes[:3]]),
-        [vmem((rows, width), BF16)] + [vmem((rows, columns), BF16)] * 3,
+        functools.partial(attend_kernel, len(gathered), lambda rank: [entry(r, rank) for r in routes]),
+        [vmem((rows, width), BF16)] + [vmem((rows, columns), BF16)] * (tp - 1),
         "v" * (5 + len(gathered)),
         cost=100000000,
     )(stacked, text_scores, bias, held_values, held_weight, *gathered)
-    arrived = [send(block, "tp", r) for r, block in zip(routes, outgoing)]
+    arrived = [send(block, r) for r, block in zip(routes, outgoing)]
     base, factor, split, consts, coefs = call(
         functools.partial(residual_kernel, tp),
         [
@@ -411,17 +420,17 @@
         shift.reshape(1, columns), scale.reshape(1, columns), proj_weight.T, latents.T,
     )
     hidden, *partials = call(
-        functools.partial(hidden_kernel, tp, [list(range(tp))] + late_routes),
+        functools.partial(hidden_kernel, tp, [list(range(tp))] + routes),
         [vmem((rows, columns), BF16)] + [vmem((24, LANES))] * tp,
         "v" * (4 + tp - 1),
         [pltpu.VMEM((channels, LANES), F32)],
         cost=20000000,
     )(base, factor, split, consts, *arrived)
-    shares = [send(block, "tp", r) for r, block in zip(late_routes, partials[1:])]
+    shares = [send(block, r, cross) for r, cross, block in zip(routes, crossing, partials[1:])]
     (hidden_out,) = call(
         keep_kernel, [(jax.ShapeDtypeStruct(stream.shape, BF16), "h")], "v", [pltpu.SemaphoreType.DMA((1,))], cost=2000000
     )(hidden)
-    mine, other = call(total_kernel, [vmem((16, LANES))] * 2, "v" * tp)(partials[0], *shares)
+    mine, other = call(functools.partial(total_kernel, crossing), [vmem((32, LANES))] * 2, "v" * tp)(partials[0], *shares)
     theirs = exchange(other, "cfg", 1)
     (latents_out,) = call(
         functools.partial(step_kernel, columns * tp), [vmem((latents.shape[1], rows))], "vvv"

time: 29 us -> 27.9 us (0.962)
  starting transfers between devices: 13.6 us -> 13 us
  waiting for transfers between devices: 6.79 us -> 6.25 us
    ppermute x6, starting transfers between devices: 8.91 us -> 8.34 us  [the longest x4 6.54 us: send(): return lax.ppermute(value, 'tp', list(enumerate(route)))]
    ppermute x6, waiting for transfers between devices: 4.64 us -> 4.15 us  [the longest x4 2.74 us: send(): return lax.ppermute(value, 'tp', list(enumerate(route)))]
  transfers between devices with their start and end apart: 10 -> 10, of which waited for: 6 -> 6; matrix products, arithmetic and copies ran while one was open for 0% -> 0% of each run, Pallas kernels for 13% -> 14%
where the time goes in v5:
time: 27.9 us; the launch traced here: 27.7 us
  starting transfers between devices  13 us (47%)
  Pallas kernels  6.92 us (25%)
  waiting for transfers between devices  6.25 us (22%)
  between operations  1.45 us (5%)
    pallas_call x8, Pallas kernels, placed(): run(*(pltpu.with_memory_space_constraint(x, pltpu.HBM) if i == 'h' else x...  6.92 us
    ppermute x4, starting transfers between devices, send(): return lax.ppermute(value, 'tp', list(enumerate(route)))  6.54 us
    ppermute x4, starting transfers between devices, exchange(): lax.ppermute(value, axis, [(i, i ^ distance) for i in range(lax.axis_size...  4.68 us
    ppermute x4, waiting for transfers between devices, send(): return lax.ppermute(value, 'tp', list(enumerate(route)))  2.74 us
    ppermute x4, waiting for transfers between devices, exchange(): lax.ppermute(value, axis, [(i, i ^ distance) for i in range(lax.axis_size...  2.1 us
    ppermute x2, starting transfers between devices, send(): return lax.ppermute(value, ('cfg', 'tp'), pairs)  1.8 us
    ppermute x2, waiting for transfers between devices, send(): return lax.ppermute(value, ('cfg', 'tp'), pairs)  1.42 us
  transfers between devices with their start and end apart: 10, of which 6 were waited for; matrix products, arithmetic and copies ran while one was open for 0% of the time, Pallas kernels for 14%

profile of v5, /device:TPU:0, one launch (start us, length us, event | category | flops | bytes accessed | tf_op | source)
XLA Modules:
  0.0 27.7 jit_solution(12974957205652089295)
XLA Ops:
  0.6 1.2 %shard_map.177.rest_0_ = bf16[40,768]{1,0:T(8,128)(2,1)S(1)} custom-call(s32[4]{0:T(128)} %lengths.1, bf16[1,40,384]{2,1,0:T(8,128)(2,1)} %keys_at.1, bf16[1,40,384]{2,1,0:T(8,128)(2,1)} %values_at.1, f32[1,64]{1,0:T(1,128)} %bitcast.8), custom_call_target="tpu_custom_call" | custom-call | flops 2000000 | bytes 31250 | tf_op jit(solution)/shard_map/pallas_call | solution.py:41
  1.8 4.0 %collective-permute-start = (bf16[40,768]{1,0:T(8,128)(2,1)S(1)}, bf16[40,768]{1,0:T(8,128)(2,1)S(1)}, u32[]{:S(2)}, u32[]{:S(2)}) collective-permute-start(bf16[40,768]{1,0:T(8,128)(2,1)S(1)} %shard_map.177.rest_0_), channel_id=1, source_target_pairs={{0,12},{4,8},{8,4},{12,0},{1,13},{5,9},{9,5},{13,1},{2,14},{6,10},... | collective-permute-start | bytes 184328 | tf_op jit(solution)/shard_map/ppermute | solution.py:334
  5.8 0.5 %collective-permute-start.1 = (bf16[40,768]{1,0:T(8,128)(2,1)S(1)}, bf16[40,768]{1,0:T(8,128)(2,1)S(1)}, u32[]{:S(2)}, u32[]{:S(2)}) collective-permute-start(bf16[40,768]{1,0:T(8,128)(2,1)S(1)} %shard_map.177.rest_0_), channel_id=1, source_target_pairs={{0,8},{4,12},{8,0},{12,4},{1,9},{5,13},{9,1},{13,5},{2,10},{6,14},... | collective-permute-start | bytes 184328 | tf_op jit(solution)/shard_map/ppermute | solution.py:334
  6.3 0.1 collective-permute-start.2
  6.4 0.0 copy-start.5
  6.4 0.0 copy-start.6
  6.4 0.0 copy-start.7
  6.4 0.0 copy-start
  6.4 0.0 copy-start.1
  6.5 0.0 copy-start.2
  6.5 0.0 copy-start.3
  6.5 0.0 copy-start.4
  6.5 2.4 %shard_map.176 = (bf16[3,80,128]{2,1,0:T(8,128)(2,1)S(1)}, f32[3,80,226]{2,1,0:T(8,128)S(1)}, f32[1,160]{1,0:T(1,128)S(1)}, bf16[1,226,384]{2,1,0:T(8,128)(2,1)S(1)}, bf16[384,3072]{1,0:T(8,128)(2,1)S(1)}) custom-call(s32[4]{0:T(128)} %lengths.1, bf16[1,40,384]{2,1,0:T(8,128)(2,1)} %queries_at.1, bf16[1,226,384]{2,1,0:T(8,128)(2,1)} %text_keys_at.1, ...), custom_call_target="tpu_custom_call" | custom-call | flops 20000000 | bytes 312500 | tf_op jit(solution)/shard_map/pallas_call | solution.py:41
  8.9 0.0 collective-permute-done.rest_1_
  8.9 1.1 %collective-permute-done.1.rest_2_ = bf16[40,768]{1,0:T(8,128)(2,1)S(1)} collective-permute-done((bf16[40,768]{1,0:T(8,128)(2,1)S(1)}, bf16[40,768]{1,0:T(8,128)(2,1)S(1)}, u32[]{:S(2)}, u32[]{:S(2)}) %collective-permute-start.1) | collective-permute-done | bytes 61472 | tf_op jit(solution)/shard_map/ppermute | solution.py:334
  10.0 0.5 %collective-permute-done.2.rest_3_ = bf16[40,768]{1,0:T(8,128)(2,1)S(1)} collective-permute-done((bf16[40,768]{1,0:T(8,128)(2,1)S(1)}, bf16[40,768]{1,0:T(8,128)(2,1)S(1)}, u32[]{:S(2)}, u32[]{:S(2)}) %collective-permute-start.2) | collective-permute-done | bytes 61472 | tf_op jit(solution)/shard_map/ppermute | solution.py:334
  10.5 0.9 %shard_map.178 = (bf16[40,384]{1,0:T(8,128)(2,1)S(1)}, bf16[40,768]{1,0:T(8,128)(2,1)S(1)}, bf16[40,768]{1,0:T(8,128)(2,1)S(1)}, bf16[40,768]{1,0:T(8,128)(2,1)S(1)}) custom-call(bf16[3,80,128]{2,1,0:T(8,128)(2,1)S(1)} %get-tuple-element.23.stacked, f32[3,80,226]{2,1,0:T(8,128)S(1)} %get-tuple-element.24.text_scores, f32[1,160]{1,0:T(1,128)S(1)} %get-tuple-element.25.bias, ...), custom_call_target="tpu_custom_call" | custom-call | flops 100000000 | bytes 1562500 | tf_op jit(solution)/shard_map/pallas_call | solution.py:41
  11.4 3.7 %collective-permute-start.3 = (bf16[40,768]{1,0:T(8,128)(2,1)S(1)}, bf16[40,768]{1,0:T(8,128)(2,1)S(1)}, u32[]{:S(2)}, u32[]{:S(2)}) collective-permute-start(bf16[40,768]{1,0:T(8,128)(2,1)S(1)} %get-tuple-element.33), channel_id=1, source_target_pairs={{0,3},{1,2},{2,1},{3,0},{4,7},{5,6},{6,5},{7,4},{8,11},{9,10},{10,... | collective-permute-start | bytes 184328 | tf_op jit(solution)/shard_map/ppermute | solution.py:339
  15.1 0.0 collective-permute-start.4
  15.1 0.8 %collective-permute-start.5 = (bf16[40,768]{1,0:T(8,128)(2,1)S(1)}, bf16[40,768]{1,0:T(8,128)(2,1)S(1)}, u32[]{:S(2)}, u32[]{:S(2)}) collective-permute-start(bf16[40,768]{1,0:T(8,128)(2,1)S(1)} %get-tuple-element.35), channel_id=1, source_target_pairs={{0,1},{1,0},{2,3},{3,2},{4,5},{5,4},{6,7},{7,6},{8,9},{9,8},{10,11... | collective-permute-start | bytes 184328 | tf_op jit(solution)/shard_map/ppermute | solution.py:339
  15.9 0.0 copy-done.5
  15.9 0.0 copy-done.6
  15.9 0.0 copy-done.7
  16.6 0.0 copy-done
  16.6 0.0 copy-done.1
  16.6 0.0 copy-done.2
  16.6 0.0 copy-done.3
  16.6 0.0 copy-done.4
  16.6 0.9 %shard_map.179 = (f32[40,768]{1,0:T(8,128)S(1)}, f32[40,768]{1,0:T(8,128)S(1)}, bf16[208,768]{1,0:T(8,128)(2,1)S(1)}, f32[64,128]{1,0:T(8,128)S(1)}, f32[48,128]{1,0:T(8,128)S(1)}) custom-call(s32[4]{0:T(128)S(1)} %copy-done.2, f32[1000]{0:T(1024)S(1)} %copy-done.3, s32[1]{0:T(128)S(6)} %copy.19.step, bf16[40,384]{1,0:T(8,128)(2,1)S(1)} %get-tuple-element.28.attended, ...), custom_call_target="tpu_custom_call" | custom-call | flops 100000000 | bytes 1562500 | tf_op jit(solution)/shard_map/pallas_call | solution.py:41
  17.5 0.0 collective-permute-done.3.rest_0_
  17.5 2.7 %collective-permute-done.4.rest_1_ = bf16[40,768]{1,0:T(8,128)(2,1)S(1)} collective-permute-done((bf16[40,768]{1,0:T(8,128)(2,1)S(1)}, bf16[40,768]{1,0:T(8,128)(2,1)S(1)}, u32[]{:S(2)}, u32[]{:S(2)}) %collective-permute-start.4) | collective-permute-done | bytes 61472 | tf_op jit(solution)/shard_map/ppermute | solution.py:339
  20.2 0.0 collective-permute-done.5.rest_2_
  20.2 0.3 %shard_map.180 = (bf16[40,768]{1,0:T(8,128)(2,1)S(1)}, f32[24,128]{1,0:T(8,128)S(1)}, f32[24,128]{1,0:T(8,128)S(1)}, f32[24,128]{1,0:T(8,128)S(1)}, f32[24,128]{1,0:T(8,128)S(1)}) custom-call(f32[40,768]{1,0:T(8,128)S(1)} %get-tuple-element.29.base, f32[40,768]{1,0:T(8,128)S(1)} %get-tuple-element.30.factor, bf16[208,768]{1,0:T(8,128)(2,1)S(1)} %get-tuple-element.31.split, ...), custom_call_target="tpu_custom_call" | custom-call | flops 20000000 | bytes 312500 | tf_op jit(solution)/shard_map/pallas_call | solution.py:41
  20.5 0.1 collective-permute-start.6
  20.6 2.1 %collective-permute-start.7 = (f32[24,128]{1,0:T(8,128)S(1)}, f32[24,128]{1,0:T(8,128)S(1)}, u32[]{:S(2)}, u32[]{:S(2)}) collective-permute-start(f32[24,128]{1,0:T(8,128)S(1)} %get-tuple-element.39), channel_id=1, source_target_pairs={{0,2},{1,3},{2,0},{3,1},{4,6},{5,7},{6,4},{7,5},{8,10},{9,11},{10,... | collective-permute-start | bytes 36872 | tf_op jit(solution)/shard_map/ppermute | solution.py:339
  22.7 1.7 %collective-permute-start.8 = (f32[24,128]{1,0:T(8,128)S(1)}, f32[24,128]{1,0:T(8,128)S(1)}, u32[]{:S(2)}, u32[]{:S(2)}) collective-permute-start(f32[24,128]{1,0:T(8,128)S(1)} %get-tuple-element.40), channel_id=1, source_target_pairs={{0,17},{1,16},{2,19},{3,18},{16,1},{17,0},{18,3},{19,2},{4,21},{5,... | collective-permute-start | bytes 36872 | tf_op jit(solution)/shard_map/ppermute | solution.py:342
  24.4 1.1 %collective-permute-done.6.rest_0_ = f32[24,128]{1,0:T(8,128)S(1)} collective-permute-done((f32[24,128]{1,0:T(8,128)S(1)}, f32[24,128]{1,0:T(8,128)S(1)}, u32[]{:S(2)}, u32[]{:S(2)}) %collective-permute-start.6) | collective-permute-done | bytes 12320 | tf_op jit(solution)/shard_map/ppermute | solution.py:342
  25.5 0.0 collective-permute-done.7.rest_1_
  25.5 0.3 %collective-permute-done.8.rest_2_ = f32[24,128]{1,0:T(8,128)S(1)} collective-permute-done((f32[24,128]{1,0:T(8,128)S(1)}, f32[24,128]{1,0:T(8,128)S(1)}, u32[]{:S(2)}, u32[]{:S(2)}) %collective-permute-start.8) | collective-permute-done | bytes 12320 | tf_op jit(solution)/shard_map/ppermute | solution.py:342
  25.8 0.1 collective-permute-start.9
  25.9 0.6 %shard_map.181 = bf16[1,40,768]{2,1,0:T(8,128)(2,1)} custom-call(bf16[40,768]{1,0:T(8,128)(2,1)S(1)} %get-tuple-element.36.value), custom_call_target="tpu_custom_call" | custom-call | flops 2000000 | bytes 31250 | tf_op jit(solution)/shard_map/pallas_call | solution.py:41
  26.6 0.5 %collective-permute-done.9.theirs = f32[32,128]{1,0:T(8,128)S(1)} collective-permute-done((f32[32,128]{1,0:T(8,128)S(1)}, f32[32,128]{1,0:T(8,128)S(1)}, u32[]{:S(2)}, u32[]{:S(2)}) %collective-permute-start.9) | collective-permute-done | bytes 16416 | tf_op jit(solution)/shard_map/ppermute | solution.py:334
  27.0 0.7 %shard_map.183 = f32[8,40]{1,0:T(8,128)} custom-call(f32[32,128]{1,0:T(8,128)S(1)} %get-tuple-element.41.mine, f32[32,128]{1,0:T(8,128)S(1)} %collective-permute-done.9.theirs, f32[48,128]{1,0:T(8,128)S(1)} %get-tuple-element.43.coefs), custom_call_target="tpu_custom_call" | custom-call | tf_op jit(solution)/shard_map/pallas_call | solution.py:41
  (4 shorter events, 0.0 us)
Async XLA Ops:
  1.8 7.1 %collective-permute-start = (bf16[40,768]{1,0:T(8,128)(2,1)S(1)}, bf16[40,768]{1,0:T(8,128)(2,1)S(1)}, u32[]{:S(2)}, u32[]{:S(2)}) collective-permute-start(bf16[40,768]{1,0:T(8,128)(2,1)S(1)} %shard_map.177.rest_0_), channel_id=1, source_target_pairs={{0,12},{4,8},{8,4},{12,0},{1,13},{5,9},{9,5},{13,1},{2,14},{6,10},... | collective-permute-start | bytes 184328 | tf_op jit(solution)/shard_map/ppermute | solution.py:334
  5.8 4.2 %collective-permute-start.1 = (bf16[40,768]{1,0:T(8,128)(2,1)S(1)}, bf16[40,768]{1,0:T(8,128)(2,1)S(1)}, u32[]{:S(2)}, u32[]{:S(2)}) collective-permute-start(bf16[40,768]{1,0:T(8,128)(2,1)S(1)} %shard_map.177.rest_0_), channel_id=1, source_target_pairs={{0,8},{4,12},{8,0},{12,4},{1,9},{5,13},{9,1},{13,5},{2,10},{6,14},... | collective-permute-start | bytes 184328 | tf_op jit(solution)/shard_map/ppermute | solution.py:334
  6.3 4.2 %collective-permute-start.2 = (bf16[40,768]{1,0:T(8,128)(2,1)S(1)}, bf16[40,768]{1,0:T(8,128)(2,1)S(1)}, u32[]{:S(2)}, u32[]{:S(2)}) collective-permute-start(bf16[40,768]{1,0:T(8,128)(2,1)S(1)} %shard_map.177.rest_0_), channel_id=1, source_target_pairs={{0,4},{4,0},{8,12},{12,8},{1,5},{5,1},{9,13},{13,9},{2,6},{6,2},{1... | collective-permute-start | bytes 184328 | tf_op jit(solution)/shard_map/ppermute | solution.py:334
  6.4 9.5 %copy-start.5 = (f32[768]{0:T(1024)S(1)}, f32[768]{0:T(1024)}, u32[]{:S(2)}) copy-start(f32[768]{0:T(1024)} %param.24) | copy-start | bytes 9220
  6.4 9.5 %copy-start.6 = (f32[768]{0:T(1024)S(1)}, f32[768]{0:T(1024)}, u32[]{:S(2)}) copy-start(f32[768]{0:T(1024)} %param.25) | copy-start | bytes 9220
  6.4 9.5 %copy-start.7 = (f32[768]{0:T(1024)S(1)}, f32[768]{0:T(1024)}, u32[]{:S(2)}) copy-start(f32[768]{0:T(1024)} %param.26) | copy-start | bytes 9220
  6.4 10.1 %copy-start = (f32[768,64]{0,1:T(8,128)S(1)}, f32[768,64]{0,1:T(8,128)}, u32[]{:S(2)}) copy-start(f32[768,64]{0,1:T(8,128)} %param.27) | copy-start | bytes 589828
  6.4 10.1 %copy-start.1 = (bf16[1,40,768]{2,1,0:T(8,128)(2,1)S(1)}, bf16[1,40,768]{2,1,0:T(8,128)(2,1)}, u32[]{:S(2)}) copy-start(bf16[1,40,768]{2,1,0:T(8,128)(2,1)} %stream.1) | copy-start | bytes 184324
  6.5 10.1 %copy-start.2 = (s32[4]{0:T(128)S(1)}, s32[4]{0:T(128)}, u32[]{:S(2)}) copy-start(s32[4]{0:T(128)} %lengths.1) | copy-start | bytes 52
  6.5 10.1 %copy-start.3 = (f32[1000]{0:T(1024)S(1)}, f32[1000]{0:T(1024)}, u32[]{:S(2)}) copy-start(f32[1000]{0:T(1024)} %alphas.1) | copy-start | bytes 12004
  6.5 10.1 %copy-start.4 = (f32[40,8]{0,1:T(8,128)S(1)}, f32[40,8]{0,1:T(8,128)}, u32[]{:S(2)}) copy-start(f32[40,8]{0,1:T(8,128)} %param.31) | copy-start | bytes 3844
  11.4 6.1 %collective-permute-start.3 = (bf16[40,768]{1,0:T(8,128)(2,1)S(1)}, bf16[40,768]{1,0:T(8,128)(2,1)S(1)}, u32[]{:S(2)}, u32[]{:S(2)}) collective-permute-start(bf16[40,768]{1,0:T(8,128)(2,1)S(1)} %get-tuple-element.33), channel_id=1, source_target_pairs={{0,3},{1,2},{2,1},{3,0},{4,7},{5,6},{6,5},{7,4},{8,11},{9,10},{10,... | collective-permute-start | bytes 184328 | tf_op jit(solution)/shard_map/ppermute | solution.py:339
  15.1 5.1 %collective-permute-start.4 = (bf16[40,768]{1,0:T(8,128)(2,1)S(1)}, bf16[40,768]{1,0:T(8,128)(2,1)S(1)}, u32[]{:S(2)}, u32[]{:S(2)}) collective-permute-start(bf16[40,768]{1,0:T(8,128)(2,1)S(1)} %get-tuple-element.34), channel_id=1, source_target_pairs={{0,2},{1,3},{2,0},{3,1},{4,6},{5,7},{6,4},{7,5},{8,10},{9,11},{10,... | collective-permute-start | bytes 184328 | tf_op jit(solution)/shard_map/ppermute | solution.py:339
  15.1 5.1 %collective-permute-start.5 = (bf16[40,768]{1,0:T(8,128)(2,1)S(1)}, bf16[40,768]{1,0:T(8,128)(2,1)S(1)}, u32[]{:S(2)}, u32[]{:S(2)}) collective-permute-start(bf16[40,768]{1,0:T(8,128)(2,1)S(1)} %get-tuple-element.35), channel_id=1, source_target_pairs={{0,1},{1,0},{2,3},{3,2},{4,5},{5,4},{6,7},{7,6},{8,9},{9,8},{10,11... | collective-permute-start | bytes 184328 | tf_op jit(solution)/shard_map/ppermute | solution.py:339
  20.5 5.0 %collective-permute-start.6 = (f32[24,128]{1,0:T(8,128)S(1)}, f32[24,128]{1,0:T(8,128)S(1)}, u32[]{:S(2)}, u32[]{:S(2)}) collective-permute-start(f32[24,128]{1,0:T(8,128)S(1)} %get-tuple-element.38), channel_id=1, source_target_pairs={{0,19},{1,18},{2,17},{3,16},{16,3},{17,2},{18,1},{19,0},{4,23},{5,... | collective-permute-start | bytes 36872 | tf_op jit(solution)/shard_map/ppermute | solution.py:342
  20.6 4.9 %collective-permute-start.7 = (f32[24,128]{1,0:T(8,128)S(1)}, f32[24,128]{1,0:T(8,128)S(1)}, u32[]{:S(2)}, u32[]{:S(2)}) collective-permute-start(f32[24,128]{1,0:T(8,128)S(1)} %get-tuple-element.39), channel_id=1, source_target_pairs={{0,2},{1,3},{2,0},{3,1},{4,6},{5,7},{6,4},{7,5},{8,10},{9,11},{10,... | collective-permute-start | bytes 36872 | tf_op jit(solution)/shard_map/ppermute | solution.py:339
  22.7 3.1 %collective-permute-start.8 = (f32[24,128]{1,0:T(8,128)S(1)}, f32[24,128]{1,0:T(8,128)S(1)}, u32[]{:S(2)}, u32[]{:S(2)}) collective-permute-start(f32[24,128]{1,0:T(8,128)S(1)} %get-tuple-element.40), channel_id=1, source_target_pairs={{0,17},{1,16},{2,19},{3,18},{16,1},{17,0},{18,3},{19,2},{4,21},{5,... | collective-permute-start | bytes 36872 | tf_op jit(solution)/shard_map/ppermute | solution.py:342
  25.8 1.2 %collective-permute-start.9 = (f32[32,128]{1,0:T(8,128)S(1)}, f32[32,128]{1,0:T(8,128)S(1)}, u32[]{:S(2)}, u32[]{:S(2)}) collective-permute-start(f32[32,128]{1,0:T(8,128)S(1)} %get-tuple-element.42), channel_id=1, source_target_pairs={{0,16},{16,0},{1,17},{17,1},{2,18},{18,2},{3,19},{19,3},{4,20},{20... | collective-permute-start | bytes 49160 | tf_op jit(solution)/shard_map/ppermute | solution.py:334

commit v6 on v5

--- a/solution.py
+++ b/solution.py
@@ -94,6 +94,22 @@
     low = (square - high.astype(F32)).astype(BF16)
     spread = nn(high, average) + nn(low, average)
     normed = centre * lax.rsqrt(spread + head_eps) * gain
+    return [normed[rows * p : rows * p + rows] for p in range(len(pairs))]
+
+
+def lane_norm(field, gain):
+    rows, width = field.shape
+    pairs = [field[:, at : at + PAIR].astype(F32) for at in range(0, width, PAIR)]
+    tall = jnp.concatenate(pairs, axis=0)
+    left = lax.broadcasted_iota(jnp.int32, tall.shape, 1) < HEAD
+
+    def average(values):
+        low = jnp.sum(jnp.where(left, values, 0.0), axis=1, keepdims=True)
+        high = jnp.sum(jnp.where(left, 0.0, values), axis=1, keepdims=True)
+        return jnp.where(left, low, high) * (1.0 / HEAD)
+
+    centre = tall - average(tall)
+    normed = centre * lax.rsqrt(average(centre * centre) + head_eps) * gain
     return [normed[rows * p : rows * p + rows] for p in range(len(pairs))]
 
 
@@ -129,13 +145,12 @@
 def pack_keys_kernel(blocks, lengths_at, keys_at, values_at, gain_at, packed, lengths, keys, values, gain, sems):
     arriving = copies(sems, (lengths_at, lengths), (keys_at, keys), (gain_at, gain), (values_at, values))
     rows, width = keys.shape[1:]
-    average = averager()
     arriving[0].wait()
     tables = rope_tables(prior(lengths, lax.axis_index("seq"), blocks), rows)
     arriving[1].wait()
     arriving[2].wait()
     wide = twice(gain)
-    for p, normed in enumerate(head_norm(keys[0], average, wide)):
+    for p, normed in enumerate(lane_norm(keys[0], wide)):
         packed[:, PAIR * p : PAIR * p + PAIR] = rotate(normed, *tables).astype(BF16)
     arriving[3].wait()
     packed[:, width:] = values[0]

time: 27.9 us -> 27.8 us (level)
  no operation moved by 1% of the time
where the time goes in v6:
time: 27.8 us; the launch traced here: 27.6 us
  starting transfers between devices  13 us (47%)
  Pallas kernels  6.86 us (25%)
  waiting for transfers between devices  6.25 us (22%)
  between operations  1.45 us (5%)
    pallas_call x8, Pallas kernels, placed(): run(*(pltpu.with_memory_space_constraint(x, pltpu.HBM) if i == 'h' else x...  6.86 us
    ppermute x4, starting transfers between devices, send(): return lax.ppermute(value, 'tp', list(enumerate(route)))  6.54 us
    ppermute x4, starting transfers between devices, exchange(): lax.ppermute(value, axis, [(i, i ^ distance) for i in range(lax.axis_size...  4.68 us
    ppermute x4, waiting for transfers between devices, send(): return lax.ppermute(value, 'tp', list(enumerate(route)))  2.73 us
    ppermute x4, waiting for transfers between devices, exchange(): lax.ppermute(value, axis, [(i, i ^ distance) for i in range(lax.axis_size...  2.09 us
    ppermute x2, starting transfers between devices, send(): return lax.ppermute(value, ('cfg', 'tp'), pairs)  1.8 us
    ppermute x2, waiting for transfers between devices, send(): return lax.ppermute(value, ('cfg', 'tp'), pairs)  1.42 us
  transfers between devices with their start and end apart: 10, of which 6 were waited for; matrix products, arithmetic and copies ran while one was open for 0% of the time, Pallas kernels for 14%

profile of v6, /device:TPU:0, one launch (start us, length us, event | category | flops | bytes accessed | tf_op | source)
XLA Modules:
  0.0 27.6 jit_solution(7628254725591061699)
XLA Ops:
  0.6 1.1 %shard_map.177.rest_0_ = bf16[40,768]{1,0:T(8,128)(2,1)S(1)} custom-call(s32[4]{0:T(128)} %lengths.1, bf16[1,40,384]{2,1,0:T(8,128)(2,1)} %keys_at.1, bf16[1,40,384]{2,1,0:T(8,128)(2,1)} %values_at.1, f32[1,64]{1,0:T(1,128)} %bitcast.8), custom_call_target="tpu_custom_call" | custom-call | flops 2000000 | bytes 31250 | tf_op jit(solution)/shard_map/pallas_call | solution.py:41
  1.8 4.0 %collective-permute-start = (bf16[40,768]{1,0:T(8,128)(2,1)S(1)}, bf16[40,768]{1,0:T(8,128)(2,1)S(1)}, u32[]{:S(2)}, u32[]{:S(2)}) collective-permute-start(bf16[40,768]{1,0:T(8,128)(2,1)S(1)} %shard_map.177.rest_0_), channel_id=1, source_target_pairs={{0,12},{4,8},{8,4},{12,0},{1,13},{5,9},{9,5},{13,1},{2,14},{6,10},... | collective-permute-start | bytes 184328 | tf_op jit(solution)/shard_map/ppermute | solution.py:349
  5.7 0.5 %collective-permute-start.1 = (bf16[40,768]{1,0:T(8,128)(2,1)S(1)}, bf16[40,768]{1,0:T(8,128)(2,1)S(1)}, u32[]{:S(2)}, u32[]{:S(2)}) collective-permute-start(bf16[40,768]{1,0:T(8,128)(2,1)S(1)} %shard_map.177.rest_0_), channel_id=1, source_target_pairs={{0,8},{4,12},{8,0},{12,4},{1,9},{5,13},{9,1},{13,5},{2,10},{6,14},... | collective-permute-start | bytes 184328 | tf_op jit(solution)/shard_map/ppermute | solution.py:349
  6.2 0.1 collective-permute-start.2
  6.4 0.0 copy-start.5
  6.4 0.0 copy-start.6
  6.4 0.0 copy-start.7
  6.4 0.0 copy-start
  6.4 0.0 copy-start.1
  6.4 0.0 copy-start.2
  6.4 0.0 copy-start.3
  6.4 0.0 copy-start.4
  6.4 2.4 %shard_map.176 = (bf16[3,80,128]{2,1,0:T(8,128)(2,1)S(1)}, f32[3,80,226]{2,1,0:T(8,128)S(1)}, f32[1,160]{1,0:T(1,128)S(1)}, bf16[1,226,384]{2,1,0:T(8,128)(2,1)S(1)}, bf16[384,3072]{1,0:T(8,128)(2,1)S(1)}) custom-call(s32[4]{0:T(128)} %lengths.1, bf16[1,40,384]{2,1,0:T(8,128)(2,1)} %queries_at.1, bf16[1,226,384]{2,1,0:T(8,128)(2,1)} %text_keys_at.1, ...), custom_call_target="tpu_custom_call" | custom-call | flops 20000000 | bytes 312500 | tf_op jit(solution)/shard_map/pallas_call | solution.py:41
  8.8 0.0 collective-permute-done.rest_1_
  8.8 1.1 %collective-permute-done.1.rest_2_ = bf16[40,768]{1,0:T(8,128)(2,1)S(1)} collective-permute-done((bf16[40,768]{1,0:T(8,128)(2,1)S(1)}, bf16[40,768]{1,0:T(8,128)(2,1)S(1)}, u32[]{:S(2)}, u32[]{:S(2)}) %collective-permute-start.1) | collective-permute-done | bytes 61472 | tf_op jit(solution)/shard_map/ppermute | solution.py:349
  9.9 0.5 %collective-permute-done.2.rest_3_ = bf16[40,768]{1,0:T(8,128)(2,1)S(1)} collective-permute-done((bf16[40,768]{1,0:T(8,128)(2,1)S(1)}, bf16[40,768]{1,0:T(8,128)(2,1)S(1)}, u32[]{:S(2)}, u32[]{:S(2)}) %collective-permute-start.2) | collective-permute-done | bytes 61472 | tf_op jit(solution)/shard_map/ppermute | solution.py:349
  10.5 0.9 %shard_map.178 = (bf16[40,384]{1,0:T(8,128)(2,1)S(1)}, bf16[40,768]{1,0:T(8,128)(2,1)S(1)}, bf16[40,768]{1,0:T(8,128)(2,1)S(1)}, bf16[40,768]{1,0:T(8,128)(2,1)S(1)}) custom-call(bf16[3,80,128]{2,1,0:T(8,128)(2,1)S(1)} %get-tuple-element.23.stacked, f32[3,80,226]{2,1,0:T(8,128)S(1)} %get-tuple-element.24.text_scores, f32[1,160]{1,0:T(1,128)S(1)} %get-tuple-element.25.bias, ...), custom_call_target="tpu_custom_call" | custom-call | flops 100000000 | bytes 1562500 | tf_op jit(solution)/shard_map/pallas_call | solution.py:41
  11.4 3.7 %collective-permute-start.3 = (bf16[40,768]{1,0:T(8,128)(2,1)S(1)}, bf16[40,768]{1,0:T(8,128)(2,1)S(1)}, u32[]{:S(2)}, u32[]{:S(2)}) collective-permute-start(bf16[40,768]{1,0:T(8,128)(2,1)S(1)} %get-tuple-element.33), channel_id=1, source_target_pairs={{0,3},{1,2},{2,1},{3,0},{4,7},{5,6},{6,5},{7,4},{8,11},{9,10},{10,... | collective-permute-start | bytes 184328 | tf_op jit(solution)/shard_map/ppermute | solution.py:354
  15.0 0.0 collective-permute-start.4
  15.0 0.8 %collective-permute-start.5 = (bf16[40,768]{1,0:T(8,128)(2,1)S(1)}, bf16[40,768]{1,0:T(8,128)(2,1)S(1)}, u32[]{:S(2)}, u32[]{:S(2)}) collective-permute-start(bf16[40,768]{1,0:T(8,128)(2,1)S(1)} %get-tuple-element.35), channel_id=1, source_target_pairs={{0,1},{1,0},{2,3},{3,2},{4,5},{5,4},{6,7},{7,6},{8,9},{9,8},{10,11... | collective-permute-start | bytes 184328 | tf_op jit(solution)/shard_map/ppermute | solution.py:354
  15.8 0.0 copy-done.5
  15.8 0.0 copy-done.6
  15.8 0.0 copy-done.7
  16.5 0.0 copy-done
  16.5 0.0 copy-done.1
  16.5 0.0 copy-done.2
  16.5 0.0 copy-done.3
  16.6 0.0 copy-done.4
  16.6 0.9 %shard_map.179 = (f32[40,768]{1,0:T(8,128)S(1)}, f32[40,768]{1,0:T(8,128)S(1)}, bf16[208,768]{1,0:T(8,128)(2,1)S(1)}, f32[64,128]{1,0:T(8,128)S(1)}, f32[48,128]{1,0:T(8,128)S(1)}) custom-call(s32[4]{0:T(128)S(1)} %copy-done.2, f32[1000]{0:T(1024)S(1)} %copy-done.3, s32[1]{0:T(128)S(6)} %copy.19.step, bf16[40,384]{1,0:T(8,128)(2,1)S(1)} %get-tuple-element.28.attended, ...), custom_call_target="tpu_custom_call" | custom-call | flops 100000000 | bytes 1562500 | tf_op jit(solution)/shard_map/pallas_call | solution.py:41
  17.4 0.0 collective-permute-done.3.rest_0_
  17.5 2.7 %collective-permute-done.4.rest_1_ = bf16[40,768]{1,0:T(8,128)(2,1)S(1)} collective-permute-done((bf16[40,768]{1,0:T(8,128)(2,1)S(1)}, bf16[40,768]{1,0:T(8,128)(2,1)S(1)}, u32[]{:S(2)}, u32[]{:S(2)}) %collective-permute-start.4) | collective-permute-done | bytes 61472 | tf_op jit(solution)/shard_map/ppermute | solution.py:354
  20.2 0.0 collective-permute-done.5.rest_2_
  20.2 0.3 %shard_map.180 = (bf16[40,768]{1,0:T(8,128)(2,1)S(1)}, f32[24,128]{1,0:T(8,128)S(1)}, f32[24,128]{1,0:T(8,128)S(1)}, f32[24,128]{1,0:T(8,128)S(1)}, f32[24,128]{1,0:T(8,128)S(1)}) custom-call(f32[40,768]{1,0:T(8,128)S(1)} %get-tuple-element.29.base, f32[40,768]{1,0:T(8,128)S(1)} %get-tuple-element.30.factor, bf16[208,768]{1,0:T(8,128)(2,1)S(1)} %get-tuple-element.31.split, ...), custom_call_target="tpu_custom_call" | custom-call | flops 20000000 | bytes 312500 | tf_op jit(solution)/shard_map/pallas_call | solution.py:41
  20.4 0.1 collective-permute-start.6
  20.5 2.1 %collective-permute-start.7 = (f32[24,128]{1,0:T(8,128)S(1)}, f32[24,128]{1,0:T(8,128)S(1)}, u32[]{:S(2)}, u32[]{:S(2)}) collective-permute-start(f32[24,128]{1,0:T(8,128)S(1)} %get-tuple-element.39), channel_id=1, source_target_pairs={{0,2},{1,3},{2,0},{3,1},{4,6},{5,7},{6,4},{7,5},{8,10},{9,11},{10,... | collective-permute-start | bytes 36872 | tf_op jit(solution)/shard_map/ppermute | solution.py:354
  22.6 1.7 %collective-permute-start.8 = (f32[24,128]{1,0:T(8,128)S(1)}, f32[24,128]{1,0:T(8,128)S(1)}, u32[]{:S(2)}, u32[]{:S(2)}) collective-permute-start(f32[24,128]{1,0:T(8,128)S(1)} %get-tuple-element.40), channel_id=1, source_target_pairs={{0,17},{1,16},{2,19},{3,18},{16,1},{17,0},{18,3},{19,2},{4,21},{5,... | collective-permute-start | bytes 36872 | tf_op jit(solution)/shard_map/ppermute | solution.py:357
  24.3 1.1 %collective-permute-done.6.rest_0_ = f32[24,128]{1,0:T(8,128)S(1)} collective-permute-done((f32[24,128]{1,0:T(8,128)S(1)}, f32[24,128]{1,0:T(8,128)S(1)}, u32[]{:S(2)}, u32[]{:S(2)}) %collective-permute-start.6) | collective-permute-done | bytes 12320 | tf_op jit(solution)/shard_map/ppermute | solution.py:357
  25.4 0.0 collective-permute-done.7.rest_1_
  25.4 0.3 %collective-permute-done.8.rest_2_ = f32[24,128]{1,0:T(8,128)S(1)} collective-permute-done((f32[24,128]{1,0:T(8,128)S(1)}, f32[24,128]{1,0:T(8,128)S(1)}, u32[]{:S(2)}, u32[]{:S(2)}) %collective-permute-start.8) | collective-permute-done | bytes 12320 | tf_op jit(solution)/shard_map/ppermute | solution.py:357
  25.8 0.1 collective-permute-start.9
  25.9 0.6 %shard_map.181 = bf16[1,40,768]{2,1,0:T(8,128)(2,1)} custom-call(bf16[40,768]{1,0:T(8,128)(2,1)S(1)} %get-tuple-element.36.value), custom_call_target="tpu_custom_call" | custom-call | flops 2000000 | bytes 31250 | tf_op jit(solution)/shard_map/pallas_call | solution.py:41
  26.5 0.5 %collective-permute-done.9.theirs = f32[32,128]{1,0:T(8,128)S(1)} collective-permute-done((f32[32,128]{1,0:T(8,128)S(1)}, f32[32,128]{1,0:T(8,128)S(1)}, u32[]{:S(2)}, u32[]{:S(2)}) %collective-permute-start.9) | collective-permute-done | bytes 16416 | tf_op jit(solution)/shard_map/ppermute | solution.py:349
  27.0 0.7 %shard_map.183 = f32[8,40]{1,0:T(8,128)} custom-call(f32[32,128]{1,0:T(8,128)S(1)} %get-tuple-element.41.mine, f32[32,128]{1,0:T(8,128)S(1)} %collective-permute-done.9.theirs, f32[48,128]{1,0:T(8,128)S(1)} %get-tuple-element.43.coefs), custom_call_target="tpu_custom_call" | custom-call | tf_op jit(solution)/shard_map/pallas_call | solution.py:41
  (4 shorter events, 0.0 us)
Async XLA Ops:
  1.8 7.1 %collective-permute-start = (bf16[40,768]{1,0:T(8,128)(2,1)S(1)}, bf16[40,768]{1,0:T(8,128)(2,1)S(1)}, u32[]{:S(2)}, u32[]{:S(2)}) collective-permute-start(bf16[40,768]{1,0:T(8,128)(2,1)S(1)} %shard_map.177.rest_0_), channel_id=1, source_target_pairs={{0,12},{4,8},{8,4},{12,0},{1,13},{5,9},{9,5},{13,1},{2,14},{6,10},... | collective-permute-start | bytes 184328 | tf_op jit(solution)/shard_map/ppermute | solution.py:349
  5.7 4.2 %collective-permute-start.1 = (bf16[40,768]{1,0:T(8,128)(2,1)S(1)}, bf16[40,768]{1,0:T(8,128)(2,1)S(1)}, u32[]{:S(2)}, u32[]{:S(2)}) collective-permute-start(bf16[40,768]{1,0:T(8,128)(2,1)S(1)} %shard_map.177.rest_0_), channel_id=1, source_target_pairs={{0,8},{4,12},{8,0},{12,4},{1,9},{5,13},{9,1},{13,5},{2,10},{6,14},... | collective-permute-start | bytes 184328 | tf_op jit(solution)/shard_map/ppermute | solution.py:349
  6.2 4.2 %collective-permute-start.2 = (bf16[40,768]{1,0:T(8,128)(2,1)S(1)}, bf16[40,768]{1,0:T(8,128)(2,1)S(1)}, u32[]{:S(2)}, u32[]{:S(2)}) collective-permute-start(bf16[40,768]{1,0:T(8,128)(2,1)S(1)} %shard_map.177.rest_0_), channel_id=1, source_target_pairs={{0,4},{4,0},{8,12},{12,8},{1,5},{5,1},{9,13},{13,9},{2,6},{6,2},{1... | collective-permute-start | bytes 184328 | tf_op jit(solution)/shard_map/ppermute | solution.py:349
  6.4 9.5 %copy-start.5 = (f32[768]{0:T(1024)S(1)}, f32[768]{0:T(1024)}, u32[]{:S(2)}) copy-start(f32[768]{0:T(1024)} %param.24) | copy-start | bytes 9220
  6.4 9.5 %copy-start.6 = (f32[768]{0:T(1024)S(1)}, f32[768]{0:T(1024)}, u32[]{:S(2)}) copy-start(f32[768]{0:T(1024)} %param.25) | copy-start | bytes 9220
  6.4 9.5 %copy-start.7 = (f32[768]{0:T(1024)S(1)}, f32[768]{0:T(1024)}, u32[]{:S(2)}) copy-start(f32[768]{0:T(1024)} %param.26) | copy-start | bytes 9220
  6.4 10.1 %copy-start = (f32[768,64]{0,1:T(8,128)S(1)}, f32[768,64]{0,1:T(8,128)}, u32[]{:S(2)}) copy-start(f32[768,64]{0,1:T(8,128)} %param.27) | copy-start | bytes 589828
  6.4 10.1 %copy-start.1 = (bf16[1,40,768]{2,1,0:T(8,128)(2,1)S(1)}, bf16[1,40,768]{2,1,0:T(8,128)(2,1)}, u32[]{:S(2)}) copy-start(bf16[1,40,768]{2,1,0:T(8,128)(2,1)} %stream.1) | copy-start | bytes 184324
  6.4 10.1 %copy-start.2 = (s32[4]{0:T(128)S(1)}, s32[4]{0:T(128)}, u32[]{:S(2)}) copy-start(s32[4]{0:T(128)} %lengths.1) | copy-start | bytes 52
  6.4 10.1 %copy-start.3 = (f32[1000]{0:T(1024)S(1)}, f32[1000]{0:T(1024)}, u32[]{:S(2)}) copy-start(f32[1000]{0:T(1024)} %alphas.1) | copy-start | bytes 12004
  6.4 10.1 %copy-start.4 = (f32[40,8]{0,1:T(8,128)S(1)}, f32[40,8]{0,1:T(8,128)}, u32[]{:S(2)}) copy-start(f32[40,8]{0,1:T(8,128)} %param.31) | copy-start | bytes 3844
  11.4 6.1 %collective-permute-start.3 = (bf16[40,768]{1,0:T(8,128)(2,1)S(1)}, bf16[40,768]{1,0:T(8,128)(2,1)S(1)}, u32[]{:S(2)}, u32[]{:S(2)}) collective-permute-start(bf16[40,768]{1,0:T(8,128)(2,1)S(1)} %get-tuple-element.33), channel_id=1, source_target_pairs={{0,3},{1,2},{2,1},{3,0},{4,7},{5,6},{6,5},{7,4},{8,11},{9,10},{10,... | collective-permute-start | bytes 184328 | tf_op jit(solution)/shard_map/ppermute | solution.py:354
  15.0 5.1 %collective-permute-start.4 = (bf16[40,768]{1,0:T(8,128)(2,1)S(1)}, bf16[40,768]{1,0:T(8,128)(2,1)S(1)}, u32[]{:S(2)}, u32[]{:S(2)}) collective-permute-start(bf16[40,768]{1,0:T(8,128)(2,1)S(1)} %get-tuple-element.34), channel_id=1, source_target_pairs={{0,2},{1,3},{2,0},{3,1},{4,6},{5,7},{6,4},{7,5},{8,10},{9,11},{10,... | collective-permute-start | bytes 184328 | tf_op jit(solution)/shard_map/ppermute | solution.py:354
  15.0 5.1 %collective-permute-start.5 = (bf16[40,768]{1,0:T(8,128)(2,1)S(1)}, bf16[40,768]{1,0:T(8,128)(2,1)S(1)}, u32[]{:S(2)}, u32[]{:S(2)}) collective-permute-start(bf16[40,768]{1,0:T(8,128)(2,1)S(1)} %get-tuple-element.35), channel_id=1, source_target_pairs={{0,1},{1,0},{2,3},{3,2},{4,5},{5,4},{6,7},{7,6},{8,9},{9,8},{10,11... | collective-permute-start | bytes 184328 | tf_op jit(solution)/shard_map/ppermute | solution.py:354
  20.4 5.0 %collective-permute-start.6 = (f32[24,128]{1,0:T(8,128)S(1)}, f32[24,128]{1,0:T(8,128)S(1)}, u32[]{:S(2)}, u32[]{:S(2)}) collective-permute-start(f32[24,128]{1,0:T(8,128)S(1)} %get-tuple-element.38), channel_id=1, source_target_pairs={{0,19},{1,18},{2,17},{3,16},{16,3},{17,2},{18,1},{19,0},{4,23},{5,... | collective-permute-start | bytes 36872 | tf_op jit(solution)/shard_map/ppermute | solution.py:357
  20.5 4.9 %collective-permute-start.7 = (f32[24,128]{1,0:T(8,128)S(1)}, f32[24,128]{1,0:T(8,128)S(1)}, u32[]{:S(2)}, u32[]{:S(2)}) collective-permute-start(f32[24,128]{1,0:T(8,128)S(1)} %get-tuple-element.39), channel_id=1, source_target_pairs={{0,2},{1,3},{2,0},{3,1},{4,6},{5,7},{6,4},{7,5},{8,10},{9,11},{10,... | collective-permute-start | bytes 36872 | tf_op jit(solution)/shard_map/ppermute | solution.py:354
  22.6 3.2 %collective-permute-start.8 = (f32[24,128]{1,0:T(8,128)S(1)}, f32[24,128]{1,0:T(8,128)S(1)}, u32[]{:S(2)}, u32[]{:S(2)}) collective-permute-start(f32[24,128]{1,0:T(8,128)S(1)} %get-tuple-element.40), channel_id=1, source_target_pairs={{0,17},{1,16},{2,19},{3,18},{16,1},{17,0},{18,3},{19,2},{4,21},{5,... | collective-permute-start | bytes 36872 | tf_op jit(solution)/shard_map/ppermute | solution.py:357
  25.8 1.2 %collective-permute-start.9 = (f32[32,128]{1,0:T(8,128)S(1)}, f32[32,128]{1,0:T(8,128)S(1)}, u32[]{:S(2)}, u32[]{:S(2)}) collective-permute-start(f32[32,128]{1,0:T(8,128)S(1)} %get-tuple-element.42), channel_id=1, source_target_pairs={{0,16},{16,0},{1,17},{17,1},{2,18},{18,2},{3,19},{19,3},{4,20},{20... | collective-permute-start | bytes 49160 | tf_op jit(solution)/shard_map/ppermute | solution.py:349

commit v7 on v6

--- a/solution.py
+++ b/solution.py
@@ -265,13 +265,12 @@
     at = step[0]
     now = jnp.full((8, LANES), alphas[at], F32)
     earlier = jnp.full((8, LANES), alphas[at - STRIDE], F32)
-    coefs[0:8] = jnp.sqrt(now)
-    coefs[8:16] = jnp.sqrt(1.0 - now)
-    coefs[16:24] = jnp.sqrt(earlier)
-    coefs[24:32] = jnp.sqrt(1.0 - earlier)
+    root_now, rest_now = jnp.sqrt(now), jnp.sqrt(1.0 - now)
+    root_next, rest_next = jnp.sqrt(earlier), jnp.sqrt(1.0 - earlier)
     lane8 = lax.broadcasted_iota(jnp.int32, (8, LANES), 1)
-    coefs[32:40] = jnp.where(lane8 < count, 1.0, 0.0)
-    coefs[40:48] = jnp.concatenate([latents[...], jnp.zeros((8, LANES - rows), F32)], axis=1)
+    noisy = jnp.concatenate([latents[...], jnp.zeros((8, LANES - rows), F32)], axis=1)
+    coefs[0:8] = jnp.where(lane8 < count, (root_next * root_now + rest_next * rest_now) * noisy, 0.0)
+    coefs[8:16] = jnp.where(lane8 < count, rest_next * root_now - root_next * rest_now, 0.0)
     own = nn(attended[...], weight[:, pl.ds(pl.multiple_of(rank * columns, columns), columns)])
     base[...] = jnp.where(alive, stream[0].astype(F32) + gate[...] * own, 0.0)
 
@@ -337,12 +336,7 @@
     conditioned = jnp.where(is_conditioned, own, partner)
     unconditioned = jnp.where(is_conditioned, partner, own)
     guided = unconditioned + guide_scale * (conditioned - unconditioned)
-    root_now, rest_now, root_next, rest_next, live, latents = (
-        coefs[8 * i : 8 * i + 8, :rows] for i in range(6)
-    )
-    clean = root_now * latents - rest_now * guided
-    noise = root_now * guided + rest_now * latents
-    out[...] = jnp.where(live > 0.0, root_next * clean + rest_next * noise, 0.0)
+    out[...] = coefs[0:8, :rows] + coefs[8:16, :rows] * guided
 
 
 def exchange(value, axis, distance):
@@ -426,7 +420,7 @@
             vmem((rows, columns)),
             vmem((3 * channels + 16, columns), BF16),
             vmem((channels, LANES)),
-            vmem((48, LANES)),
+            vmem((16, LANES)),
         ],
         "sss" + "v" * 8,
         cost=100000000,

time: 27.8 us -> 27.8 us (level)
  no operation moved by 1% of the time
where the time goes in v7:
time: 27.8 us; the launch traced here: 27.6 us
  starting transfers between devices  13 us (47%)
  Pallas kernels  6.86 us (25%)
  waiting for transfers between devices  6.25 us (22%)
  between operations  1.45 us (5%)
    pallas_call x8, Pallas kernels, placed(): run(*(pltpu.with_memory_space_constraint(x, pltpu.HBM) if i == 'h' else x...  6.86 us
    ppermute x4, starting transfers between devices, send(): return lax.ppermute(value, 'tp', list(enumerate(route)))  6.54 us
    ppermute x4, starting transfers between devices, exchange(): lax.ppermute(value, axis, [(i, i ^ distance) for i in range(lax.axis_size...  4.68 us
    ppermute x4, waiting for transfers between devices, send(): return lax.ppermute(value, 'tp', list(enumerate(route)))  2.73 us
    ppermute x4, waiting for transfers between devices, exchange(): lax.ppermute(value, axis, [(i, i ^ distance) for i in range(lax.axis_size...  2.09 us
    ppermute x2, starting transfers between devices, send(): return lax.ppermute(value, ('cfg', 'tp'), pairs)  1.8 us
    ppermute x2, waiting for transfers between devices, send(): return lax.ppermute(value, ('cfg', 'tp'), pairs)  1.42 us
  transfers between devices with their start and end apart: 10, of which 6 were waited for; matrix products, arithmetic and copies ran while one was open for 0% of the time, Pallas kernels for 14%

profile of v7, /device:TPU:0, one launch (start us, length us, event | category | flops | bytes accessed | tf_op | source)
XLA Modules:
  0.0 27.6 jit_solution(5908807115683494510)
XLA Ops:
  0.6 1.1 %shard_map.177.rest_0_ = bf16[40,768]{1,0:T(8,128)(2,1)S(1)} custom-call(s32[4]{0:T(128)} %lengths.1, bf16[1,40,384]{2,1,0:T(8,128)(2,1)} %keys_at.1, bf16[1,40,384]{2,1,0:T(8,128)(2,1)} %values_at.1, f32[1,64]{1,0:T(1,128)} %bitcast.8), custom_call_target="tpu_custom_call" | custom-call | flops 2000000 | bytes 31250 | tf_op jit(solution)/shard_map/pallas_call | solution.py:41
  1.8 4.0 %collective-permute-start = (bf16[40,768]{1,0:T(8,128)(2,1)S(1)}, bf16[40,768]{1,0:T(8,128)(2,1)S(1)}, u32[]{:S(2)}, u32[]{:S(2)}) collective-permute-start(bf16[40,768]{1,0:T(8,128)(2,1)S(1)} %shard_map.177.rest_0_), channel_id=1, source_target_pairs={{0,12},{4,8},{8,4},{12,0},{1,13},{5,9},{9,5},{13,1},{2,14},{6,10},... | collective-permute-start | bytes 184328 | tf_op jit(solution)/shard_map/ppermute | solution.py:343
  5.7 0.5 %collective-permute-start.1 = (bf16[40,768]{1,0:T(8,128)(2,1)S(1)}, bf16[40,768]{1,0:T(8,128)(2,1)S(1)}, u32[]{:S(2)}, u32[]{:S(2)}) collective-permute-start(bf16[40,768]{1,0:T(8,128)(2,1)S(1)} %shard_map.177.rest_0_), channel_id=1, source_target_pairs={{0,8},{4,12},{8,0},{12,4},{1,9},{5,13},{9,1},{13,5},{2,10},{6,14},... | collective-permute-start | bytes 184328 | tf_op jit(solution)/shard_map/ppermute | solution.py:343
  6.2 0.1 collective-permute-start.2
  6.4 0.0 copy-start.5
  6.4 0.0 copy-start.6
  6.4 0.0 copy-start.7
  6.4 0.0 copy-start
  6.4 0.0 copy-start.1
  6.4 0.0 copy-start.2
  6.4 0.0 copy-start.3
  6.4 0.0 copy-start.4
  6.4 2.4 %shard_map.176 = (bf16[3,80,128]{2,1,0:T(8,128)(2,1)S(1)}, f32[3,80,226]{2,1,0:T(8,128)S(1)}, f32[1,160]{1,0:T(1,128)S(1)}, bf16[1,226,384]{2,1,0:T(8,128)(2,1)S(1)}, bf16[384,3072]{1,0:T(8,128)(2,1)S(1)}) custom-call(s32[4]{0:T(128)} %lengths.1, bf16[1,40,384]{2,1,0:T(8,128)(2,1)} %queries_at.1, bf16[1,226,384]{2,1,0:T(8,128)(2,1)} %text_keys_at.1, ...), custom_call_target="tpu_custom_call" | custom-call | flops 20000000 | bytes 312500 | tf_op jit(solution)/shard_map/pallas_call | solution.py:41
  8.8 0.0 collective-permute-done.rest_1_
  8.8 1.1 %collective-permute-done.1.rest_2_ = bf16[40,768]{1,0:T(8,128)(2,1)S(1)} collective-permute-done((bf16[40,768]{1,0:T(8,128)(2,1)S(1)}, bf16[40,768]{1,0:T(8,128)(2,1)S(1)}, u32[]{:S(2)}, u32[]{:S(2)}) %collective-permute-start.1) | collective-permute-done | bytes 61472 | tf_op jit(solution)/shard_map/ppermute | solution.py:343
  9.9 0.5 %collective-permute-done.2.rest_3_ = bf16[40,768]{1,0:T(8,128)(2,1)S(1)} collective-permute-done((bf16[40,768]{1,0:T(8,128)(2,1)S(1)}, bf16[40,768]{1,0:T(8,128)(2,1)S(1)}, u32[]{:S(2)}, u32[]{:S(2)}) %collective-permute-start.2) | collective-permute-done | bytes 61472 | tf_op jit(solution)/shard_map/ppermute | solution.py:343
  10.5 0.9 %shard_map.178 = (bf16[40,384]{1,0:T(8,128)(2,1)S(1)}, bf16[40,768]{1,0:T(8,128)(2,1)S(1)}, bf16[40,768]{1,0:T(8,128)(2,1)S(1)}, bf16[40,768]{1,0:T(8,128)(2,1)S(1)}) custom-call(bf16[3,80,128]{2,1,0:T(8,128)(2,1)S(1)} %get-tuple-element.23.stacked, f32[3,80,226]{2,1,0:T(8,128)S(1)} %get-tuple-element.24.text_scores, f32[1,160]{1,0:T(1,128)S(1)} %get-tuple-element.25.bias, ...), custom_call_target="tpu_custom_call" | custom-call | flops 100000000 | bytes 1562500 | tf_op jit(solution)/shard_map/pallas_call | solution.py:41
  11.4 3.7 %collective-permute-start.3 = (bf16[40,768]{1,0:T(8,128)(2,1)S(1)}, bf16[40,768]{1,0:T(8,128)(2,1)S(1)}, u32[]{:S(2)}, u32[]{:S(2)}) collective-permute-start(bf16[40,768]{1,0:T(8,128)(2,1)S(1)} %get-tuple-element.33), channel_id=1, source_target_pairs={{0,3},{1,2},{2,1},{3,0},{4,7},{5,6},{6,5},{7,4},{8,11},{9,10},{10,... | collective-permute-start | bytes 184328 | tf_op jit(solution)/shard_map/ppermute | solution.py:348
  15.0 0.0 collective-permute-start.4
  15.0 0.8 %collective-permute-start.5 = (bf16[40,768]{1,0:T(8,128)(2,1)S(1)}, bf16[40,768]{1,0:T(8,128)(2,1)S(1)}, u32[]{:S(2)}, u32[]{:S(2)}) collective-permute-start(bf16[40,768]{1,0:T(8,128)(2,1)S(1)} %get-tuple-element.35), channel_id=1, source_target_pairs={{0,1},{1,0},{2,3},{3,2},{4,5},{5,4},{6,7},{7,6},{8,9},{9,8},{10,11... | collective-permute-start | bytes 184328 | tf_op jit(solution)/shard_map/ppermute | solution.py:348
  15.8 0.0 copy-done.5
  15.8 0.0 copy-done.6
  15.8 0.0 copy-done.7
  16.5 0.0 copy-done
  16.5 0.0 copy-done.1
  16.5 0.0 copy-done.2
  16.5 0.0 copy-done.3
  16.6 0.0 copy-done.4
  16.6 0.9 %shard_map.179 = (f32[40,768]{1,0:T(8,128)S(1)}, f32[40,768]{1,0:T(8,128)S(1)}, bf16[208,768]{1,0:T(8,128)(2,1)S(1)}, f32[64,128]{1,0:T(8,128)S(1)}, f32[16,128]{1,0:T(8,128)S(1)}) custom-call(s32[4]{0:T(128)S(1)} %copy-done.2, f32[1000]{0:T(1024)S(1)} %copy-done.3, s32[1]{0:T(128)S(6)} %copy.19.step, bf16[40,384]{1,0:T(8,128)(2,1)S(1)} %get-tuple-element.28.attended, ...), custom_call_target="tpu_custom_call" | custom-call | flops 100000000 | bytes 1562500 | tf_op jit(solution)/shard_map/pallas_call | solution.py:41
  17.4 0.0 collective-permute-done.3.rest_0_
  17.5 2.7 %collective-permute-done.4.rest_1_ = bf16[40,768]{1,0:T(8,128)(2,1)S(1)} collective-permute-done((bf16[40,768]{1,0:T(8,128)(2,1)S(1)}, bf16[40,768]{1,0:T(8,128)(2,1)S(1)}, u32[]{:S(2)}, u32[]{:S(2)}) %collective-permute-start.4) | collective-permute-done | bytes 61472 | tf_op jit(solution)/shard_map/ppermute | solution.py:348
  20.2 0.0 collective-permute-done.5.rest_2_
  20.2 0.3 %shard_map.180 = (bf16[40,768]{1,0:T(8,128)(2,1)S(1)}, f32[24,128]{1,0:T(8,128)S(1)}, f32[24,128]{1,0:T(8,128)S(1)}, f32[24,128]{1,0:T(8,128)S(1)}, f32[24,128]{1,0:T(8,128)S(1)}) custom-call(f32[40,768]{1,0:T(8,128)S(1)} %get-tuple-element.29.base, f32[40,768]{1,0:T(8,128)S(1)} %get-tuple-element.30.factor, bf16[208,768]{1,0:T(8,128)(2,1)S(1)} %get-tuple-element.31.split, ...), custom_call_target="tpu_custom_call" | custom-call | flops 20000000 | bytes 312500 | tf_op jit(solution)/shard_map/pallas_call | solution.py:41
  20.4 0.1 collective-permute-start.6
  20.5 2.1 %collective-permute-start.7 = (f32[24,128]{1,0:T(8,128)S(1)}, f32[24,128]{1,0:T(8,128)S(1)}, u32[]{:S(2)}, u32[]{:S(2)}) collective-permute-start(f32[24,128]{1,0:T(8,128)S(1)} %get-tuple-element.39), channel_id=1, source_target_pairs={{0,2},{1,3},{2,0},{3,1},{4,6},{5,7},{6,4},{7,5},{8,10},{9,11},{10,... | collective-permute-start | bytes 36872 | tf_op jit(solution)/shard_map/ppermute | solution.py:348
  22.6 1.7 %collective-permute-start.8 = (f32[24,128]{1,0:T(8,128)S(1)}, f32[24,128]{1,0:T(8,128)S(1)}, u32[]{:S(2)}, u32[]{:S(2)}) collective-permute-start(f32[24,128]{1,0:T(8,128)S(1)} %get-tuple-element.40), channel_id=1, source_target_pairs={{0,17},{1,16},{2,19},{3,18},{16,1},{17,0},{18,3},{19,2},{4,21},{5,... | collective-permute-start | bytes 36872 | tf_op jit(solution)/shard_map/ppermute | solution.py:351
  24.3 1.1 %collective-permute-done.6.rest_0_ = f32[24,128]{1,0:T(8,128)S(1)} collective-permute-done((f32[24,128]{1,0:T(8,128)S(1)}, f32[24,128]{1,0:T(8,128)S(1)}, u32[]{:S(2)}, u32[]{:S(2)}) %collective-permute-start.6) | collective-permute-done | bytes 12320 | tf_op jit(solution)/shard_map/ppermute | solution.py:351
  25.4 0.0 collective-permute-done.7.rest_1_
  25.4 0.3 %collective-permute-done.8.rest_2_ = f32[24,128]{1,0:T(8,128)S(1)} collective-permute-done((f32[24,128]{1,0:T(8,128)S(1)}, f32[24,128]{1,0:T(8,128)S(1)}, u32[]{:S(2)}, u32[]{:S(2)}) %collective-permute-start.8) | collective-permute-done | bytes 12320 | tf_op jit(solution)/shard_map/ppermute | solution.py:351
  25.8 0.1 collective-permute-start.9
  25.9 0.6 %shard_map.181 = bf16[1,40,768]{2,1,0:T(8,128)(2,1)} custom-call(bf16[40,768]{1,0:T(8,128)(2,1)S(1)} %get-tuple-element.36.value), custom_call_target="tpu_custom_call" | custom-call | flops 2000000 | bytes 31250 | tf_op jit(solution)/shard_map/pallas_call | solution.py:41
  26.5 0.5 %collective-permute-done.9.theirs = f32[32,128]{1,0:T(8,128)S(1)} collective-permute-done((f32[32,128]{1,0:T(8,128)S(1)}, f32[32,128]{1,0:T(8,128)S(1)}, u32[]{:S(2)}, u32[]{:S(2)}) %collective-permute-start.9) | collective-permute-done | bytes 16416 | tf_op jit(solution)/shard_map/ppermute | solution.py:343
  27.0 0.7 %shard_map.183 = f32[8,40]{1,0:T(8,128)} custom-call(f32[32,128]{1,0:T(8,128)S(1)} %get-tuple-element.41.mine, f32[32,128]{1,0:T(8,128)S(1)} %collective-permute-done.9.theirs, f32[16,128]{1,0:T(8,128)S(1)} %get-tuple-element.43.coefs), custom_call_target="tpu_custom_call" | custom-call | tf_op jit(solution)/shard_map/pallas_call | solution.py:41
  (4 shorter events, 0.0 us)
Async XLA Ops:
  1.8 7.1 %collective-permute-start = (bf16[40,768]{1,0:T(8,128)(2,1)S(1)}, bf16[40,768]{1,0:T(8,128)(2,1)S(1)}, u32[]{:S(2)}, u32[]{:S(2)}) collective-permute-start(bf16[40,768]{1,0:T(8,128)(2,1)S(1)} %shard_map.177.rest_0_), channel_id=1, source_target_pairs={{0,12},{4,8},{8,4},{12,0},{1,13},{5,9},{9,5},{13,1},{2,14},{6,10},... | collective-permute-start | bytes 184328 | tf_op jit(solution)/shard_map/ppermute | solution.py:343
  5.7 4.2 %collective-permute-start.1 = (bf16[40,768]{1,0:T(8,128)(2,1)S(1)}, bf16[40,768]{1,0:T(8,128)(2,1)S(1)}, u32[]{:S(2)}, u32[]{:S(2)}) collective-permute-start(bf16[40,768]{1,0:T(8,128)(2,1)S(1)} %shard_map.177.rest_0_), channel_id=1, source_target_pairs={{0,8},{4,12},{8,0},{12,4},{1,9},{5,13},{9,1},{13,5},{2,10},{6,14},... | collective-permute-start | bytes 184328 | tf_op jit(solution)/shard_map/ppermute | solution.py:343
  6.2 4.2 %collective-permute-start.2 = (bf16[40,768]{1,0:T(8,128)(2,1)S(1)}, bf16[40,768]{1,0:T(8,128)(2,1)S(1)}, u32[]{:S(2)}, u32[]{:S(2)}) collective-permute-start(bf16[40,768]{1,0:T(8,128)(2,1)S(1)} %shard_map.177.rest_0_), channel_id=1, source_target_pairs={{0,4},{4,0},{8,12},{12,8},{1,5},{5,1},{9,13},{13,9},{2,6},{6,2},{1... | collective-permute-start | bytes 184328 | tf_op jit(solution)/shard_map/ppermute | solution.py:343
  6.4 9.5 %copy-start.5 = (f32[768]{0:T(1024)S(1)}, f32[768]{0:T(1024)}, u32[]{:S(2)}) copy-start(f32[768]{0:T(1024)} %param.24) | copy-start | bytes 9220
  6.4 9.5 %copy-start.6 = (f32[768]{0:T(1024)S(1)}, f32[768]{0:T(1024)}, u32[]{:S(2)}) copy-start(f32[768]{0:T(1024)} %param.25) | copy-start | bytes 9220
  6.4 9.5 %copy-start.7 = (f32[768]{0:T(1024)S(1)}, f32[768]{0:T(1024)}, u32[]{:S(2)}) copy-start(f32[768]{0:T(1024)} %param.26) | copy-start | bytes 9220
  6.4 10.1 %copy-start = (f32[768,64]{0,1:T(8,128)S(1)}, f32[768,64]{0,1:T(8,128)}, u32[]{:S(2)}) copy-start(f32[768,64]{0,1:T(8,128)} %param.27) | copy-start | bytes 589828
  6.4 10.1 %copy-start.1 = (bf16[1,40,768]{2,1,0:T(8,128)(2,1)S(1)}, bf16[1,40,768]{2,1,0:T(8,128)(2,1)}, u32[]{:S(2)}) copy-start(bf16[1,40,768]{2,1,0:T(8,128)(2,1)} %stream.1) | copy-start | bytes 184324
  6.4 10.1 %copy-start.2 = (s32[4]{0:T(128)S(1)}, s32[4]{0:T(128)}, u32[]{:S(2)}) copy-start(s32[4]{0:T(128)} %lengths.1) | copy-start | bytes 52
  6.4 10.1 %copy-start.3 = (f32[1000]{0:T(1024)S(1)}, f32[1000]{0:T(1024)}, u32[]{:S(2)}) copy-start(f32[1000]{0:T(1024)} %alphas.1) | copy-start | bytes 12004
  6.4 10.1 %copy-start.4 = (f32[40,8]{0,1:T(8,128)S(1)}, f32[40,8]{0,1:T(8,128)}, u32[]{:S(2)}) copy-start(f32[40,8]{0,1:T(8,128)} %param.31) | copy-start | bytes 3844
  11.4 6.1 %collective-permute-start.3 = (bf16[40,768]{1,0:T(8,128)(2,1)S(1)}, bf16[40,768]{1,0:T(8,128)(2,1)S(1)}, u32[]{:S(2)}, u32[]{:S(2)}) collective-permute-start(bf16[40,768]{1,0:T(8,128)(2,1)S(1)} %get-tuple-element.33), channel_id=1, source_target_pairs={{0,3},{1,2},{2,1},{3,0},{4,7},{5,6},{6,5},{7,4},{8,11},{9,10},{10,... | collective-permute-start | bytes 184328 | tf_op jit(solution)/shard_map/ppermute | solution.py:348
  15.0 5.1 %collective-permute-start.4 = (bf16[40,768]{1,0:T(8,128)(2,1)S(1)}, bf16[40,768]{1,0:T(8,128)(2,1)S(1)}, u32[]{:S(2)}, u32[]{:S(2)}) collective-permute-start(bf16[40,768]{1,0:T(8,128)(2,1)S(1)} %get-tuple-element.34), channel_id=1, source_target_pairs={{0,2},{1,3},{2,0},{3,1},{4,6},{5,7},{6,4},{7,5},{8,10},{9,11},{10,... | collective-permute-start | bytes 184328 | tf_op jit(solution)/shard_map/ppermute | solution.py:348
  15.0 5.1 %collective-permute-start.5 = (bf16[40,768]{1,0:T(8,128)(2,1)S(1)}, bf16[40,768]{1,0:T(8,128)(2,1)S(1)}, u32[]{:S(2)}, u32[]{:S(2)}) collective-permute-start(bf16[40,768]{1,0:T(8,128)(2,1)S(1)} %get-tuple-element.35), channel_id=1, source_target_pairs={{0,1},{1,0},{2,3},{3,2},{4,5},{5,4},{6,7},{7,6},{8,9},{9,8},{10,11... | collective-permute-start | bytes 184328 | tf_op jit(solution)/shard_map/ppermute | solution.py:348
  20.4 5.0 %collective-permute-start.6 = (f32[24,128]{1,0:T(8,128)S(1)}, f32[24,128]{1,0:T(8,128)S(1)}, u32[]{:S(2)}, u32[]{:S(2)}) collective-permute-start(f32[24,128]{1,0:T(8,128)S(1)} %get-tuple-element.38), channel_id=1, source_target_pairs={{0,19},{1,18},{2,17},{3,16},{16,3},{17,2},{18,1},{19,0},{4,23},{5,... | collective-permute-start | bytes 36872 | tf_op jit(solution)/shard_map/ppermute | solution.py:351
  20.5 4.9 %collective-permute-start.7 = (f32[24,128]{1,0:T(8,128)S(1)}, f32[24,128]{1,0:T(8,128)S(1)}, u32[]{:S(2)}, u32[]{:S(2)}) collective-permute-start(f32[24,128]{1,0:T(8,128)S(1)} %get-tuple-element.39), channel_id=1, source_target_pairs={{0,2},{1,3},{2,0},{3,1},{4,6},{5,7},{6,4},{7,5},{8,10},{9,11},{10,... | collective-permute-start | bytes 36872 | tf_op jit(solution)/shard_map/ppermute | solution.py:348
  22.6 3.2 %collective-permute-start.8 = (f32[24,128]{1,0:T(8,128)S(1)}, f32[24,128]{1,0:T(8,128)S(1)}, u32[]{:S(2)}, u32[]{:S(2)}) collective-permute-start(f32[24,128]{1,0:T(8,128)S(1)} %get-tuple-element.40), channel_id=1, source_target_pairs={{0,17},{1,16},{2,19},{3,18},{16,1},{17,0},{18,3},{19,2},{4,21},{5,... | collective-permute-start | bytes 36872 | tf_op jit(solution)/shard_map/ppermute | solution.py:351
  25.8 1.2 %collective-permute-start.9 = (f32[32,128]{1,0:T(8,128)S(1)}, f32[32,128]{1,0:T(8,128)S(1)}, u32[]{:S(2)}, u32[]{:S(2)}) collective-permute-start(f32[32,128]{1,0:T(8,128)S(1)} %get-tuple-element.42), channel_id=1, source_target_pairs={{0,16},{16,0},{1,17},{17,1},{2,18},{18,2},{3,19},{19,3},{4,20},{20... | collective-permute-start | bytes 49160 | tf_op jit(solution)/shard_map/ppermute | solution.py:343

commit v8 on v6

--- a/solution.py
+++ b/solution.py
@@ -143,12 +143,11 @@
 
 
 def pack_keys_kernel(blocks, lengths_at, keys_at, values_at, gain_at, packed, lengths, keys, values, gain, sems):
-    arriving = copies(sems, (lengths_at, lengths), (keys_at, keys), (gain_at, gain), (values_at, values))
+    arriving = copies(sems, (keys_at, keys), (lengths_at, lengths), (gain_at, gain), (values_at, values))
     rows, width = keys.shape[1:]
-    arriving[0].wait()
+    for one in arriving[:3]:
+        one.wait()
     tables = rope_tables(prior(lengths, lax.axis_index("seq"), blocks), rows)
-    arriving[1].wait()
-    arriving[2].wait()
     wide = twice(gain)
     for p, normed in enumerate(lane_norm(keys[0], wide)):
         packed[:, PAIR * p : PAIR * p + PAIR] = rotate(normed, *tables).astype(BF16)

time: 27.8 us -> 27.9 us (level)
  no operation moved by 1% of the time
where the time goes in v8:
time: 27.9 us; the launch traced here: 27.7 us
  starting transfers between devices  13 us (47%)
  Pallas kernels  6.88 us (25%)
  waiting for transfers between devices  6.25 us (22%)
  between operations  1.45 us (5%)
    pallas_call x8, Pallas kernels, placed(): run(*(pltpu.with_memory_space_constraint(x, pltpu.HBM) if i == 'h' else x...  6.88 us
    ppermute x4, starting transfers between devices, send(): return lax.ppermute(value, 'tp', list(enumerate(route)))  6.54 us
    ppermute x4, starting transfers between devices, exchange(): lax.ppermute(value, axis, [(i, i ^ distance) for i in range(lax.axis_size...  4.68 us
    ppermute x4, waiting for transfers between devices, send(): return lax.ppermute(value, 'tp', list(enumerate(route)))  2.74 us
    ppermute x4, waiting for transfers between devices, exchange(): lax.ppermute(value, axis, [(i, i ^ distance) for i in range(lax.axis_size...  2.1 us
    ppermute x2, starting transfers between devices, send(): return lax.ppermute(value, ('cfg', 'tp'), pairs)  1.8 us
    ppermute x2, waiting for transfers between devices, send(): return lax.ppermute(value, ('cfg', 'tp'), pairs)  1.42 us
  transfers between devices with their start and end apart: 10, of which 6 were waited for; matrix products, arithmetic and copies ran while one was open for 0% of the time, Pallas kernels for 14%

profile of v8, /device:TPU:0, one launch (start us, length us, event | category | flops | bytes accessed | tf_op | source)
XLA Modules:
  0.0 27.7 jit_solution(16762727672561565296)
XLA Ops:
  0.6 1.1 %shard_map.177.rest_0_ = bf16[40,768]{1,0:T(8,128)(2,1)S(1)} custom-call(s32[4]{0:T(128)} %lengths.1, bf16[1,40,384]{2,1,0:T(8,128)(2,1)} %keys_at.1, bf16[1,40,384]{2,1,0:T(8,128)(2,1)} %values_at.1, f32[1,64]{1,0:T(1,128)} %bitcast.8), custom_call_target="tpu_custom_call" | custom-call | flops 2000000 | bytes 31250 | tf_op jit(solution)/shard_map/pallas_call | solution.py:41
  1.8 4.0 %collective-permute-start = (bf16[40,768]{1,0:T(8,128)(2,1)S(1)}, bf16[40,768]{1,0:T(8,128)(2,1)S(1)}, u32[]{:S(2)}, u32[]{:S(2)}) collective-permute-start(bf16[40,768]{1,0:T(8,128)(2,1)S(1)} %shard_map.177.rest_0_), channel_id=1, source_target_pairs={{0,12},{4,8},{8,4},{12,0},{1,13},{5,9},{9,5},{13,1},{2,14},{6,10},... | collective-permute-start | bytes 184328 | tf_op jit(solution)/shard_map/ppermute | solution.py:348
  5.7 0.5 %collective-permute-start.1 = (bf16[40,768]{1,0:T(8,128)(2,1)S(1)}, bf16[40,768]{1,0:T(8,128)(2,1)S(1)}, u32[]{:S(2)}, u32[]{:S(2)}) collective-permute-start(bf16[40,768]{1,0:T(8,128)(2,1)S(1)} %shard_map.177.rest_0_), channel_id=1, source_target_pairs={{0,8},{4,12},{8,0},{12,4},{1,9},{5,13},{9,1},{13,5},{2,10},{6,14},... | collective-permute-start | bytes 184328 | tf_op jit(solution)/shard_map/ppermute | solution.py:348
  6.3 0.1 collective-permute-start.2
  6.4 0.0 copy-start.5
  6.4 0.0 copy-start.6
  6.4 0.0 copy-start.7
  6.4 0.0 copy-start
  6.4 0.0 copy-start.1
  6.4 0.0 copy-start.2
  6.4 0.0 copy-start.3
  6.4 0.0 copy-start.4
  6.4 2.4 %shard_map.176 = (bf16[3,80,128]{2,1,0:T(8,128)(2,1)S(1)}, f32[3,80,226]{2,1,0:T(8,128)S(1)}, f32[1,160]{1,0:T(1,128)S(1)}, bf16[1,226,384]{2,1,0:T(8,128)(2,1)S(1)}, bf16[384,3072]{1,0:T(8,128)(2,1)S(1)}) custom-call(s32[4]{0:T(128)} %lengths.1, bf16[1,40,384]{2,1,0:T(8,128)(2,1)} %queries_at.1, bf16[1,226,384]{2,1,0:T(8,128)(2,1)} %text_keys_at.1, ...), custom_call_target="tpu_custom_call" | custom-call | flops 20000000 | bytes 312500 | tf_op jit(solution)/shard_map/pallas_call | solution.py:41
  8.8 0.0 collective-permute-done.rest_1_
  8.8 1.1 %collective-permute-done.1.rest_2_ = bf16[40,768]{1,0:T(8,128)(2,1)S(1)} collective-permute-done((bf16[40,768]{1,0:T(8,128)(2,1)S(1)}, bf16[40,768]{1,0:T(8,128)(2,1)S(1)}, u32[]{:S(2)}, u32[]{:S(2)}) %collective-permute-start.1) | collective-permute-done | bytes 61472 | tf_op jit(solution)/shard_map/ppermute | solution.py:348
  10.0 0.5 %collective-permute-done.2.rest_3_ = bf16[40,768]{1,0:T(8,128)(2,1)S(1)} collective-permute-done((bf16[40,768]{1,0:T(8,128)(2,1)S(1)}, bf16[40,768]{1,0:T(8,128)(2,1)S(1)}, u32[]{:S(2)}, u32[]{:S(2)}) %collective-permute-start.2) | collective-permute-done | bytes 61472 | tf_op jit(solution)/shard_map/ppermute | solution.py:348
  10.5 0.9 %shard_map.178 = (bf16[40,384]{1,0:T(8,128)(2,1)S(1)}, bf16[40,768]{1,0:T(8,128)(2,1)S(1)}, bf16[40,768]{1,0:T(8,128)(2,1)S(1)}, bf16[40,768]{1,0:T(8,128)(2,1)S(1)}) custom-call(bf16[3,80,128]{2,1,0:T(8,128)(2,1)S(1)} %get-tuple-element.23.stacked, f32[3,80,226]{2,1,0:T(8,128)S(1)} %get-tuple-element.24.text_scores, f32[1,160]{1,0:T(1,128)S(1)} %get-tuple-element.25.bias, ...), custom_call_target="tpu_custom_call" | custom-call | flops 100000000 | bytes 1562500 | tf_op jit(solution)/shard_map/pallas_call | solution.py:41
  11.4 3.7 %collective-permute-start.3 = (bf16[40,768]{1,0:T(8,128)(2,1)S(1)}, bf16[40,768]{1,0:T(8,128)(2,1)S(1)}, u32[]{:S(2)}, u32[]{:S(2)}) collective-permute-start(bf16[40,768]{1,0:T(8,128)(2,1)S(1)} %get-tuple-element.33), channel_id=1, source_target_pairs={{0,3},{1,2},{2,1},{3,0},{4,7},{5,6},{6,5},{7,4},{8,11},{9,10},{10,... | collective-permute-start | bytes 184328 | tf_op jit(solution)/shard_map/ppermute | solution.py:353
  15.1 0.0 collective-permute-start.4
  15.1 0.8 %collective-permute-start.5 = (bf16[40,768]{1,0:T(8,128)(2,1)S(1)}, bf16[40,768]{1,0:T(8,128)(2,1)S(1)}, u32[]{:S(2)}, u32[]{:S(2)}) collective-permute-start(bf16[40,768]{1,0:T(8,128)(2,1)S(1)} %get-tuple-element.35), channel_id=1, source_target_pairs={{0,1},{1,0},{2,3},{3,2},{4,5},{5,4},{6,7},{7,6},{8,9},{9,8},{10,11... | collective-permute-start | bytes 184328 | tf_op jit(solution)/shard_map/ppermute | solution.py:353
  15.8 0.0 copy-done.5
  15.8 0.0 copy-done.6
  15.9 0.0 copy-done.7
  16.5 0.0 copy-done
  16.5 0.0 copy-done.1
  16.6 0.0 copy-done.2
  16.6 0.0 copy-done.3
  16.6 0.0 copy-done.4
  16.6 0.9 %shard_map.179 = (f32[40,768]{1,0:T(8,128)S(1)}, f32[40,768]{1,0:T(8,128)S(1)}, bf16[208,768]{1,0:T(8,128)(2,1)S(1)}, f32[64,128]{1,0:T(8,128)S(1)}, f32[48,128]{1,0:T(8,128)S(1)}) custom-call(s32[4]{0:T(128)S(1)} %copy-done.2, f32[1000]{0:T(1024)S(1)} %copy-done.3, s32[1]{0:T(128)S(6)} %copy.19.step, bf16[40,384]{1,0:T(8,128)(2,1)S(1)} %get-tuple-element.28.attended, ...), custom_call_target="tpu_custom_call" | custom-call | flops 100000000 | bytes 1562500 | tf_op jit(solution)/shard_map/pallas_call | solution.py:41
  17.4 0.0 collective-permute-done.3.rest_0_
  17.5 2.7 %collective-permute-done.4.rest_1_ = bf16[40,768]{1,0:T(8,128)(2,1)S(1)} collective-permute-done((bf16[40,768]{1,0:T(8,128)(2,1)S(1)}, bf16[40,768]{1,0:T(8,128)(2,1)S(1)}, u32[]{:S(2)}, u32[]{:S(2)}) %collective-permute-start.4) | collective-permute-done | bytes 61472 | tf_op jit(solution)/shard_map/ppermute | solution.py:353
  20.2 0.0 collective-permute-done.5.rest_2_
  20.2 0.3 %shard_map.180 = (bf16[40,768]{1,0:T(8,128)(2,1)S(1)}, f32[24,128]{1,0:T(8,128)S(1)}, f32[24,128]{1,0:T(8,128)S(1)}, f32[24,128]{1,0:T(8,128)S(1)}, f32[24,128]{1,0:T(8,128)S(1)}) custom-call(f32[40,768]{1,0:T(8,128)S(1)} %get-tuple-element.29.base, f32[40,768]{1,0:T(8,128)S(1)} %get-tuple-element.30.factor, bf16[208,768]{1,0:T(8,128)(2,1)S(1)} %get-tuple-element.31.split, ...), custom_call_target="tpu_custom_call" | custom-call | flops 20000000 | bytes 312500 | tf_op jit(solution)/shard_map/pallas_call | solution.py:41
  20.5 0.1 collective-permute-start.6
  20.5 2.1 %collective-permute-start.7 = (f32[24,128]{1,0:T(8,128)S(1)}, f32[24,128]{1,0:T(8,128)S(1)}, u32[]{:S(2)}, u32[]{:S(2)}) collective-permute-start(f32[24,128]{1,0:T(8,128)S(1)} %get-tuple-element.39), channel_id=1, source_target_pairs={{0,2},{1,3},{2,0},{3,1},{4,6},{5,7},{6,4},{7,5},{8,10},{9,11},{10,... | collective-permute-start | bytes 36872 | tf_op jit(solution)/shard_map/ppermute | solution.py:353
  22.6 1.7 %collective-permute-start.8 = (f32[24,128]{1,0:T(8,128)S(1)}, f32[24,128]{1,0:T(8,128)S(1)}, u32[]{:S(2)}, u32[]{:S(2)}) collective-permute-start(f32[24,128]{1,0:T(8,128)S(1)} %get-tuple-element.40), channel_id=1, source_target_pairs={{0,17},{1,16},{2,19},{3,18},{16,1},{17,0},{18,3},{19,2},{4,21},{5,... | collective-permute-start | bytes 36872 | tf_op jit(solution)/shard_map/ppermute | solution.py:356
  24.4 1.1 %collective-permute-done.6.rest_0_ = f32[24,128]{1,0:T(8,128)S(1)} collective-permute-done((f32[24,128]{1,0:T(8,128)S(1)}, f32[24,128]{1,0:T(8,128)S(1)}, u32[]{:S(2)}, u32[]{:S(2)}) %collective-permute-start.6) | collective-permute-done | bytes 12320 | tf_op jit(solution)/shard_map/ppermute | solution.py:356
  25.5 0.0 collective-permute-done.7.rest_1_
  25.5 0.3 %collective-permute-done.8.rest_2_ = f32[24,128]{1,0:T(8,128)S(1)} collective-permute-done((f32[24,128]{1,0:T(8,128)S(1)}, f32[24,128]{1,0:T(8,128)S(1)}, u32[]{:S(2)}, u32[]{:S(2)}) %collective-permute-start.8) | collective-permute-done | bytes 12320 | tf_op jit(solution)/shard_map/ppermute | solution.py:356
  25.8 0.1 collective-permute-start.9
  25.9 0.6 %shard_map.181 = bf16[1,40,768]{2,1,0:T(8,128)(2,1)} custom-call(bf16[40,768]{1,0:T(8,128)(2,1)S(1)} %get-tuple-element.36.value), custom_call_target="tpu_custom_call" | custom-call | flops 2000000 | bytes 31250 | tf_op jit(solution)/shard_map/pallas_call | solution.py:41
  26.5 0.5 %collective-permute-done.9.theirs = f32[32,128]{1,0:T(8,128)S(1)} collective-permute-done((f32[32,128]{1,0:T(8,128)S(1)}, f32[32,128]{1,0:T(8,128)S(1)}, u32[]{:S(2)}, u32[]{:S(2)}) %collective-permute-start.9) | collective-permute-done | bytes 16416 | tf_op jit(solution)/shard_map/ppermute | solution.py:348
  27.0 0.7 %shard_map.183 = f32[8,40]{1,0:T(8,128)} custom-call(f32[32,128]{1,0:T(8,128)S(1)} %get-tuple-element.41.mine, f32[32,128]{1,0:T(8,128)S(1)} %collective-permute-done.9.theirs, f32[48,128]{1,0:T(8,128)S(1)} %get-tuple-element.43.coefs), custom_call_target="tpu_custom_call" | custom-call | tf_op jit(solution)/shard_map/pallas_call | solution.py:41
  (4 shorter events, 0.0 us)
Async XLA Ops:
  1.8 7.1 %collective-permute-start = (bf16[40,768]{1,0:T(8,128)(2,1)S(1)}, bf16[40,768]{1,0:T(8,128)(2,1)S(1)}, u32[]{:S(2)}, u32[]{:S(2)}) collective-permute-start(bf16[40,768]{1,0:T(8,128)(2,1)S(1)} %shard_map.177.rest_0_), channel_id=1, source_target_pairs={{0,12},{4,8},{8,4},{12,0},{1,13},{5,9},{9,5},{13,1},{2,14},{6,10},... | collective-permute-start | bytes 184328 | tf_op jit(solution)/shard_map/ppermute | solution.py:348
  5.7 4.2 %collective-permute-start.1 = (bf16[40,768]{1,0:T(8,128)(2,1)S(1)}, bf16[40,768]{1,0:T(8,128)(2,1)S(1)}, u32[]{:S(2)}, u32[]{:S(2)}) collective-permute-start(bf16[40,768]{1,0:T(8,128)(2,1)S(1)} %shard_map.177.rest_0_), channel_id=1, source_target_pairs={{0,8},{4,12},{8,0},{12,4},{1,9},{5,13},{9,1},{13,5},{2,10},{6,14},... | collective-permute-start | bytes 184328 | tf_op jit(solution)/shard_map/ppermute | solution.py:348
  6.3 4.2 %collective-permute-start.2 = (bf16[40,768]{1,0:T(8,128)(2,1)S(1)}, bf16[40,768]{1,0:T(8,128)(2,1)S(1)}, u32[]{:S(2)}, u32[]{:S(2)}) collective-permute-start(bf16[40,768]{1,0:T(8,128)(2,1)S(1)} %shard_map.177.rest_0_), channel_id=1, source_target_pairs={{0,4},{4,0},{8,12},{12,8},{1,5},{5,1},{9,13},{13,9},{2,6},{6,2},{1... | collective-permute-start | bytes 184328 | tf_op jit(solution)/shard_map/ppermute | solution.py:348
  6.4 9.5 %copy-start.5 = (f32[768]{0:T(1024)S(1)}, f32[768]{0:T(1024)}, u32[]{:S(2)}) copy-start(f32[768]{0:T(1024)} %param.24) | copy-start | bytes 9220
  6.4 9.5 %copy-start.6 = (f32[768]{0:T(1024)S(1)}, f32[768]{0:T(1024)}, u32[]{:S(2)}) copy-start(f32[768]{0:T(1024)} %param.25) | copy-start | bytes 9220
  6.4 9.5 %copy-start.7 = (f32[768]{0:T(1024)S(1)}, f32[768]{0:T(1024)}, u32[]{:S(2)}) copy-start(f32[768]{0:T(1024)} %param.26) | copy-start | bytes 9220
  6.4 10.1 %copy-start = (f32[768,64]{0,1:T(8,128)S(1)}, f32[768,64]{0,1:T(8,128)}, u32[]{:S(2)}) copy-start(f32[768,64]{0,1:T(8,128)} %param.27) | copy-start | bytes 589828
  6.4 10.1 %copy-start.1 = (bf16[1,40,768]{2,1,0:T(8,128)(2,1)S(1)}, bf16[1,40,768]{2,1,0:T(8,128)(2,1)}, u32[]{:S(2)}) copy-start(bf16[1,40,768]{2,1,0:T(8,128)(2,1)} %stream.1) | copy-start | bytes 184324
  6.4 10.1 %copy-start.2 = (s32[4]{0:T(128)S(1)}, s32[4]{0:T(128)}, u32[]{:S(2)}) copy-start(s32[4]{0:T(128)} %lengths.1) | copy-start | bytes 52
  6.4 10.1 %copy-start.3 = (f32[1000]{0:T(1024)S(1)}, f32[1000]{0:T(1024)}, u32[]{:S(2)}) copy-start(f32[1000]{0:T(1024)} %alphas.1) | copy-start | bytes 12004
  6.4 10.1 %copy-start.4 = (f32[40,8]{0,1:T(8,128)S(1)}, f32[40,8]{0,1:T(8,128)}, u32[]{:S(2)}) copy-start(f32[40,8]{0,1:T(8,128)} %param.31) | copy-start | bytes 3844
  11.4 6.1 %collective-permute-start.3 = (bf16[40,768]{1,0:T(8,128)(2,1)S(1)}, bf16[40,768]{1,0:T(8,128)(2,1)S(1)}, u32[]{:S(2)}, u32[]{:S(2)}) collective-permute-start(bf16[40,768]{1,0:T(8,128)(2,1)S(1)} %get-tuple-element.33), channel_id=1, source_target_pairs={{0,3},{1,2},{2,1},{3,0},{4,7},{5,6},{6,5},{7,4},{8,11},{9,10},{10,... | collective-permute-start | bytes 184328 | tf_op jit(solution)/shard_map/ppermute | solution.py:353
  15.1 5.1 %collective-permute-start.4 = (bf16[40,768]{1,0:T(8,128)(2,1)S(1)}, bf16[40,768]{1,0:T(8,128)(2,1)S(1)}, u32[]{:S(2)}, u32[]{:S(2)}) collective-permute-start(bf16[40,768]{1,0:T(8,128)(2,1)S(1)} %get-tuple-element.34), channel_id=1, source_target_pairs={{0,2},{1,3},{2,0},{3,1},{4,6},{5,7},{6,4},{7,5},{8,10},{9,11},{10,... | collective-permute-start | bytes 184328 | tf_op jit(solution)/shard_map/ppermute | solution.py:353
  15.1 5.1 %collective-permute-start.5 = (bf16[40,768]{1,0:T(8,128)(2,1)S(1)}, bf16[40,768]{1,0:T(8,128)(2,1)S(1)}, u32[]{:S(2)}, u32[]{:S(2)}) collective-permute-start(bf16[40,768]{1,0:T(8,128)(2,1)S(1)} %get-tuple-element.35), channel_id=1, source_target_pairs={{0,1},{1,0},{2,3},{3,2},{4,5},{5,4},{6,7},{7,6},{8,9},{9,8},{10,11... | collective-permute-start | bytes 184328 | tf_op jit(solution)/shard_map/ppermute | solution.py:353
  20.5 5.0 %collective-permute-start.6 = (f32[24,128]{1,0:T(8,128)S(1)}, f32[24,128]{1,0:T(8,128)S(1)}, u32[]{:S(2)}, u32[]{:S(2)}) collective-permute-start(f32[24,128]{1,0:T(8,128)S(1)} %get-tuple-element.38), channel_id=1, source_target_pairs={{0,19},{1,18},{2,17},{3,16},{16,3},{17,2},{18,1},{19,0},{4,23},{5,... | collective-permute-start | bytes 36872 | tf_op jit(solution)/shard_map/ppermute | solution.py:356
  20.5 4.9 %collective-permute-start.7 = (f32[24,128]{1,0:T(8,128)S(1)}, f32[24,128]{1,0:T(8,128)S(1)}, u32[]{:S(2)}, u32[]{:S(2)}) collective-permute-start(f32[24,128]{1,0:T(8,128)S(1)} %get-tuple-element.39), channel_id=1, source_target_pairs={{0,2},{1,3},{2,0},{3,1},{4,6},{5,7},{6,4},{7,5},{8,10},{9,11},{10,... | collective-permute-start | bytes 36872 | tf_op jit(solution)/shard_map/ppermute | solution.py:353
  22.6 3.1 %collective-permute-start.8 = (f32[24,128]{1,0:T(8,128)S(1)}, f32[24,128]{1,0:T(8,128)S(1)}, u32[]{:S(2)}, u32[]{:S(2)}) collective-permute-start(f32[24,128]{1,0:T(8,128)S(1)} %get-tuple-element.40), channel_id=1, source_target_pairs={{0,17},{1,16},{2,19},{3,18},{16,1},{17,0},{18,3},{19,2},{4,21},{5,... | collective-permute-start | bytes 36872 | tf_op jit(solution)/shard_map/ppermute | solution.py:356
  25.8 1.2 %collective-permute-start.9 = (f32[32,128]{1,0:T(8,128)S(1)}, f32[32,128]{1,0:T(8,128)S(1)}, u32[]{:S(2)}, u32[]{:S(2)}) collective-permute-start(f32[32,128]{1,0:T(8,128)S(1)} %get-tuple-element.42), channel_id=1, source_target_pairs={{0,16},{16,0},{1,17},{17,1},{2,18},{18,2},{3,19},{19,3},{4,20},{20... | collective-permute-start | bytes 49160 | tf_op jit(solution)/shard_map/ppermute | solution.py:348
